TPU v7x, 32 devices: a whole 2x2x4 slice. The times are simulated.
32 devices in a mesh: tx: 4 (over x, core), ty: 8 (over z, y).
Axes of the slice: x: 2, y: 2, z: 4, core: 2. Of those that a mesh axis runs over, the one named last changes fastest.
Arguments:
- signal: float32 [8388608], P(('tx', 'ty')), may hold values from -6 to 6
- band_start: int32 [64], replicated, may hold values from 0 to 8372192
- band_width: int32 [64], replicated, may hold values from 2048 to 16384, as said below
- band_gain: float32 [64], replicated, may hold values from 0.5 to 2
- slot_band: int32 [128], replicated, may hold values from -1 to 63, as said below
Outputs:
- band_signals: float32 [128, 16384], P(('tx', 'ty'))
Inputs may be any that keep to these rules, and one draw needn't show every extreme that they name: `band_width`: every band's width lies between 2048 and 16384; some band has exactly 16384 bins. `slot_band`: slots d * 4 to d * 4 + 3 belong to device d; every band stands in exactly one slot, the others hold -1; in every draw some device has all its 4 slots filled.
All inputs are finite; a program needn't handle non-finite values.
Results may differ from a plain program's by a relative error of at most 0.0003.
Values sent between devices are 32-bit elements; how exact they have to be, the bound alone decides.
A program may use at most 64 MiB of HBM per device.

v0:
```python
import math

import jax
import jax.numpy as jnp
from jax import lax
from jax.sharding import PartitionSpec as P

BL = 16384


two_pi = 2.0 * math.pi


def partner(array, axis, distance):
    return lax.ppermute(array, axis, [(i, i ^ 1 << distance) for i in range(lax.axis_size(axis))])


def angle_grid(first_index, second_index, modulus):
    product = first_index[:, None] * second_index[None, :] % modulus
    return product.astype(jnp.float32) * (two_pi / modulus)


def apply_left(matrix, values):
    return jnp.einsum("ab,...bc->...ac", matrix, values, precision=lax.Precision.HIGHEST)


def apply_right(values, matrix):
    return jnp.einsum("...ab,bc->...ac", values, matrix, precision=lax.Precision.HIGHEST)


def split_length(length):
    row_count = 1
    while row_count * row_count * 4 <= length and length % (row_count * 2) == 0:
        row_count = row_count * 2
    return (row_count, length // row_count)


def four_step(real_part, imag_part, row_count, column_count):
    row_index = jnp.arange(row_count, dtype=jnp.int32)
    column_index = jnp.arange(column_count, dtype=jnp.int32)
    first_angle = angle_grid(row_index, row_index, row_count)
    first_cos = jnp.cos(first_angle)
    first_sin = jnp.sin(first_angle)
    section_real = apply_left(first_cos, real_part) + apply_left(first_sin, imag_part)
    section_imag = apply_left(first_cos, imag_part) - apply_left(first_sin, real_part)
    twist_angle = angle_grid(row_index, column_index, row_count * column_count)
    twist_cos = jnp.cos(twist_angle)
    twist_sin = jnp.sin(twist_angle)
    turned_real = section_real * twist_cos + section_imag * twist_sin
    turned_imag = section_imag * twist_cos - section_real * twist_sin
    second_angle = angle_grid(column_index, column_index, column_count)
    second_cos = jnp.cos(second_angle)
    second_sin = jnp.sin(second_angle)
    out_real = apply_right(turned_real, second_cos) + apply_right(turned_imag, second_sin)
    out_imag = apply_right(turned_imag, second_cos) - apply_right(turned_real, second_sin)
    return (jnp.swapaxes(out_real, -1, -2), jnp.swapaxes(out_imag, -1, -2))


def reverse_bits(numbers, bit_total):
    reversed_value = jnp.zeros_like(numbers)
    for bit_pos in range(bit_total):
        reversed_value = reversed_value + numbers // (1 << bit_pos) % 2 * (
            1 << bit_total - 1 - bit_pos
        )
    return reversed_value


def lookup(values_table, positions):
    one_hot = positions[:, None] == jnp.arange(values_table.shape[0], dtype=jnp.int32)[None, :]
    return jnp.sum(
        jnp.where(one_hot, values_table[None, :], jnp.zeros((), values_table.dtype)), axis=1
    )


def take_windows(hartley, first_rows, band_rows):
    length = hartley.shape[0]
    row_total = (length + band_rows - 1) // band_rows + 1
    padded = jnp.pad(hartley, (0, row_total * band_rows - length))
    table = padded.reshape(row_total, band_rows)
    upper_row = jnp.clip(first_rows // band_rows, 0, row_total - 2)
    remainder = first_rows - upper_row * band_rows
    paired = jnp.concatenate([table[upper_row], table[upper_row + 1]], axis=1)
    for bit_pos in range(band_rows.bit_length() - 1):
        step_size = 1 << bit_pos
        moved = jnp.roll(paired, -step_size, axis=1)
        paired = jnp.where((remainder // step_size % 2 == 1)[:, None], moved, paired)
    return paired[:, :band_rows]


def body(signal, band_start, band_width, band_gain, slot_band):
    length = signal.shape[0]
    size_x = lax.axis_size("tx")
    size_y = lax.axis_size("ty")
    device_count = size_x * size_y
    low_bits = size_y.bit_length() - 1
    high_bits = size_x.bit_length() - 1
    bit_total = low_bits + high_bits
    device = lax.axis_index("tx") * size_y + lax.axis_index("ty")
    total_length = length * device_count
    real_part = signal
    imag_part = jnp.zeros_like(signal)
    for bit_level in range(bit_total - 1, -1, -1):
        if bit_level >= low_bits:
            other_real, other_imag = partner((real_part, imag_part), "tx", bit_level - low_bits)
        else:
            other_real, other_imag = partner((real_part, imag_part), "ty", bit_level)
        stride = 1 << bit_level
        is_upper = device // stride % 2 == 1
        phase_angle = (device % stride).astype(jnp.float32) * (math.pi / stride)
        phase_cos = jnp.cos(phase_angle)
        phase_sin = jnp.sin(phase_angle)
        diff_real = other_real - real_part
        diff_imag = other_imag - imag_part
        real_part, imag_part = (
            jnp.where(
                is_upper, diff_real * phase_cos + diff_imag * phase_sin, real_part + other_real
            ),
            jnp.where(
                is_upper, diff_imag * phase_cos - diff_real * phase_sin, imag_part + other_imag
            ),
        )
    bin_offset = reverse_bits(device, bit_total)
    sample_index = jnp.arange(length, dtype=jnp.int32)
    product = sample_index * bin_offset % total_length
    twist_angle = product.astype(jnp.float32) * (two_pi / total_length)
    twist_cos = jnp.cos(twist_angle)
    twist_sin = jnp.sin(twist_angle)
    turned_real = real_part * twist_cos + imag_part * twist_sin
    turned_imag = imag_part * twist_cos - real_part * twist_sin
    row_count, column_count = split_length(length)
    local_real, local_imag = four_step(
        turned_real.reshape(row_count, column_count),
        turned_imag.reshape(row_count, column_count),
        row_count,
        column_count,
    )
    hartley = (local_real - local_imag).reshape(length) * (1.0 / math.sqrt(total_length))
    slot_count = slot_band.shape[0] // device_count
    band_rows = BL // device_count
    slot_valid = slot_band >= 0
    slot_index = jnp.maximum(slot_band, 0)
    starts = lookup(band_start, slot_index)
    widths = lookup(band_width, slot_index)
    offsets = (bin_offset - starts) % device_count
    first_rows = (starts + offsets - bin_offset) // device_count
    row_numbers = jnp.arange(band_rows, dtype=jnp.int32)[None, :]
    pieces = take_windows(hartley, first_rows, band_rows)
    positions = offsets[:, None] + row_numbers * device_count
    keep_mask = slot_valid[:, None] & (positions < widths[:, None])
    outgoing = jnp.where(keep_mask, pieces, 0.0).reshape(device_count, slot_count, band_rows)
    incoming = lax.all_to_all(outgoing, ("tx", "ty"), split_axis=0, concat_axis=0, tiled=True)
    my_slots = lax.dynamic_slice_in_dim(slot_band, device * slot_count, slot_count)
    my_valid = my_slots >= 0
    my_index = jnp.maximum(my_slots, 0)
    my_start = lookup(band_start, my_index)
    my_width = lookup(band_width, my_index)
    my_gain = lookup(band_gain, my_index)
    residues = (
        my_start[:, None] + jnp.arange(device_count, dtype=jnp.int32)[None, :]
    ) % device_count
    holders = reverse_bits(residues, bit_total)
    selector = (
        holders[:, :, None] == jnp.arange(device_count, dtype=jnp.int32)[None, None, :]
    ).astype(jnp.float32)
    band_grid = jnp.einsum("scd,dsr->src", selector, incoming, precision=lax.Precision.HIGHEST)
    bin_index = (
        jnp.arange(band_rows, dtype=jnp.int32)[:, None] * device_count
        + jnp.arange(device_count, dtype=jnp.int32)[None, :]
    ).astype(jnp.float32)
    width_value = my_width.astype(jnp.float32)[:, None, None]
    taper_gain = jnp.where(
        bin_index[None] < width_value,
        0.5 - 0.5 * jnp.cos(two_pi * (bin_index[None] + 0.5) / width_value),
        0.0,
    )
    tapered = band_grid * taper_gain
    band_real, band_imag = four_step(tapered, jnp.zeros_like(tapered), band_rows, device_count)
    result = (band_real - band_imag).reshape(slot_count, BL) * (
        my_gain / jnp.sqrt(my_width.astype(jnp.float32))
    )[:, None]
    return jnp.where(my_valid[:, None], result, 0.0)


def solution(mesh):
    return jax.shard_map(
        body,
        mesh=mesh,
        in_specs=(P(("tx", "ty")), P(), P(), P(), P()),
        out_specs=P(("tx", "ty"), None),
        check_vma=False,
    )
```

profile of v0, /device:TPU:0, one launch (start us, length us, event | category | flops | bytes accessed | tf_op | source)
XLA Modules:
  0.0 378.5 jit_solution(15174167763473202960)
XLA Ops:
  3.3 23.7 %collective-permute-done.1 = f32[262144]{0:T(1024)S(1)} collective-permute-done((f32[262144]{0:T(1024)S(1)}, f32[262144]{0:T(1024)S(1)}, u32[]{:S(2)}, u32[]{:S(2)}) %collective-permute-start.1) | collective-permute-done | bytes 1048608 | tf_op jit(solution)/shard_map/ppermute | solution.py:15
  28.0 20.8 %collective-permute-done = f32[262144]{0:T(1024)} collective-permute-done((f32[262144]{0:T(1024)}, f32[262144]{0:T(1024)}, u32[]{:S(2)}, u32[]{:S(2)}) %collective-permute-start) | collective-permute-done | bytes 1048608 | tf_op jit(solution)/shard_map/ppermute | solution.py:15
  60.7 68.7 %collective-permute-done.4 = f32[262144]{0:T(1024)S(1)} collective-permute-done((f32[262144]{0:T(1024)S(1)}, f32[262144]{0:T(1024)S(1)}, u32[]{:S(2)}, u32[]{:S(2)}) %collective-permute-start.4) | collective-permute-done | bytes 1048608 | tf_op jit(solution)/shard_map/ppermute | solution.py:15
  130.4 21.0 %collective-permute-done.5 = f32[262144]{0:T(1024)} collective-permute-done((f32[262144]{0:T(1024)S(1)}, f32[262144]{0:T(1024)}, u32[]{:S(2)}, u32[]{:S(2)}) %collective-permute-start.5) | collective-permute-done | bytes 1048608 | tf_op jit(solution)/shard_map/ppermute | solution.py:15
  156.9 23.0 %collective-permute-done.6 = f32[262144]{0:T(1024)S(1)} collective-permute-done((f32[262144]{0:T(1024)S(1)}, f32[262144]{0:T(1024)S(1)}, u32[]{:S(2)}, u32[]{:S(2)}) %collective-permute-start.6) | collective-permute-done | bytes 1048608 | tf_op jit(solution)/shard_map/ppermute | solution.py:15
  180.8 20.1 %collective-permute-done.7 = f32[262144]{0:T(1024)} collective-permute-done((f32[262144]{0:T(1024)S(1)}, f32[262144]{0:T(1024)}, u32[]{:S(2)}, u32[]{:S(2)}) %collective-permute-start.7) | collective-permute-done | bytes 1048608 | tf_op jit(solution)/shard_map/ppermute | solution.py:15
  205.9 6.2 %fusion.16 = f32[4,32,512]{2,1,0:T(8,128)} fusion(), kind=kOutput, calls=%fused_computation.35 | convolution fusion | flops 406323200 | bytes 262144 | tf_op jit(solution)/shard_map/ab,...bc->...ac/dot_general | solution.py:24
  212.3 17.7 %collective-permute-done.8 = f32[262144]{0:T(1024)S(1)} collective-permute-done((f32[262144]{0:T(1024)S(1)}, f32[262144]{0:T(1024)S(1)}, u32[]{:S(2)}, u32[]{:S(2)}) %collective-permute-start.8) | collective-permute-done | bytes 1048608 | tf_op jit(solution)/shard_map/ppermute | solution.py:15
  231.0 19.2 %collective-permute-done.9 = f32[262144]{0:T(1024)} collective-permute-done((f32[262144]{0:T(1024)}, f32[262144]{0:T(1024)}, u32[]{:S(2)}, u32[]{:S(2)}) %collective-permute-start.9) | collective-permute-done | bytes 1048608 | tf_op jit(solution)/shard_map/ppermute | solution.py:15
  250.2 7.3 %multiply_add_fusion.1 = (f32[262144]{0:T(1024)S(1)}, f32[262144]{0:T(1024)S(1)}, f32[262144]{0:T(1024)S(1)}) fusion(s32[]{:T(128)S(6)} %add.708, f32[262144]{0:T(1024)} %get-tuple-element.16, f32[262144]{0:T(1024)} %collective-permute-done.9, f32[262144]{0:T(1024)} %copy-done.10, f32[262144]{0:T(1024)} %copy-done.2, pred[]{:T(512)S(6)} %eq.195), kind=kLoop, calls=%fused_computation.42 | loop fusion | flops 7077888 | bytes 7340037 | tf_op jit(solution)/shard_map/add | solution.py:128
  258.7 7.9 %fusion.44 = f32[512,512]{1,0:T(8,128)} fusion(f32[512,512]{1,0:T(8,128)} %reshape.642), kind=kOutput, calls=%fused_computation.81 | convolution fusion | flops 1614282752 | bytes 2097152 | tf_op jit(solution)/shard_map/ab,...bc->...ac/dot_general | solution.py:24
  266.5 4.5 %multiply_subtract_fusion.1 = f32[262144]{0:T(1024)S(1)} fusion(f32[262144]{0:T(1024)S(1)} %get-tuple-element.14, f32[262144]{0:T(1024)S(1)} %get-tuple-element.13, s32[]{:T(128)S(6)} %add.708), kind=kLoop, calls=%fused_computation.41 | loop fusion | flops 4456448 | bytes 3145732 | tf_op jit(solution)/shard_map/sub | solution.py:129
  271.2 5.7 %fusion.42 = f32[512,512]{1,0:T(8,128)S(1)} fusion(f32[512,512]{1,0:T(8,128)S(1)} %reshape.643), kind=kOutput, calls=%fused_computation.80 | convolution fusion | flops 1614282752 | bytes 2097152 | tf_op jit(solution)/shard_map/ab,...bc->...ac/dot_general | solution.py:24
  276.9 5.7 %convolution_add_fusion.1 = f32[512,512]{1,0:T(8,128)S(1)} fusion(f32[512,512]{1,0:T(8,128)S(1)} %copy-done.15, f32[512,512]{1,0:T(8,128)S(1)} %reshape.643), kind=kOutput, calls=%fused_computation.14 | convolution fusion | flops 1614544896 | bytes 3145728 | tf_op jit(solution)/shard_map/ab,...bc->...ac/dot_general | solution.py:24
  282.6 5.9 %convolution_subtract_fusion.1 = f32[512,512]{1,0:T(8,128)S(1)} fusion(f32[512,512]{1,0:T(8,128)S(1)} %fusion.42, f32[512,512]{1,0:T(8,128)S(1)} %copy-done.4), kind=kOutput, calls=%fused_computation.13 | convolution fusion | flops 1614544896 | bytes 3145728 | tf_op jit(solution)/shard_map/ab,...bc->...ac/dot_general | solution.py:24
  288.6 11.6 %fusion.38 = f32[512,512]{1,0:T(8,128)S(1)} fusion(f32[512,512]{1,0:T(8,128)S(1)} %convolution_add_fusion.1, f32[512,512]{1,0:T(8,128)S(1)} %convolution_subtract_fusion.1), kind=kOutput, calls=%fused_computation.78 | convolution fusion | flops 1618739200 | bytes 3145728 | tf_op jit(solution)/shard_map/...ab,bc->...ac/dot_general | solution.py:28
  300.2 11.4 %fusion.40 = f32[512,512]{1,0:T(8,128)S(1)} fusion(f32[512,512]{1,0:T(8,128)S(1)} %convolution_subtract_fusion.1, f32[512,512]{1,0:T(8,128)S(1)} %convolution_add_fusion.1), kind=kOutput, calls=%fused_computation.79 | convolution fusion | flops 1618739200 | bytes 3145728 | tf_op jit(solution)/shard_map/...ab,bc->...ac/dot_general | solution.py:28
  311.5 11.6 %convolution_add_fusion = f32[512,512]{1,0:T(8,128)S(1)} fusion(f32[512,512]{1,0:T(8,128)S(1)} %fusion.40, f32[512,512]{1,0:T(8,128)S(1)} %convolution_add_fusion.1, f32[512,512]{1,0:T(8,128)S(1)} %convolution_subtract_fusion.1), kind=kOutput, calls=%fused_computation.12 | convolution fusion | flops 1619001344 | bytes 4194304 | tf_op jit(solution)/shard_map/...ab,bc->...ac/dot_general | solution.py:28
  323.2 11.4 %fusion.2 = f32[64,4,8,128]{3,2,1,0:T(8,128)S(1)} fusion(f32[512,512]{1,0:T(8,128)S(1)} %convolution_add_fusion, f32[512,512]{1,0:T(8,128)S(1)} %fusion.38, f32[512,512]{1,0:T(8,128)S(1)} %convolution_subtract_fusion.1, f32[512,512]{1,0:T(8,128)S(1)} %convolution_add_fusion.1), kind=kOutput, calls=%fused_computation.16 | convolution fusion | flops 1619525632 | bytes 5242880 | tf_op jit(solution)/shard_map/...ab,bc->...ac/dot_general | solution.py:28
  341.0 6.9 %all-to-all-start = ((f32[32,4,512]{2,1,0:T(4,128)}), f32[32,4,512]{2,1,0:T(4,128)S(1)}, u32[]{:S(2)}, u32[]{:S(2)}) async-start(f32[32,4,512]{2,1,0:T(4,128)} %reshape.645), calls=%async_computation | async-start | bytes 524288 | tf_op jit(solution)/shard_map/all_to_all | solution.py:151
  348.0 10.5 %all-to-all-done = f32[32,4,512]{2,1,0:T(4,128)S(1)} async-done(((f32[32,4,512]{2,1,0:T(4,128)}), f32[32,4,512]{2,1,0:T(4,128)S(1)}, u32[]{:S(2)}, u32[]{:S(2)}) %all-to-all-start) | async-done | bytes 262176 | tf_op jit(solution)/shard_map/all_to_all | solution.py:151
  359.7 5.2 %fusion.18 = f32[4,32,512]{2,1,0:T(8,128)S(1)} fusion(f32[4,512,32]{1,2,0:T(8,128)S(1)} %convolution_multiply_fusion), kind=kOutput, calls=%fused_computation.37 | convolution fusion | flops 406323200 | bytes 524288 | tf_op jit(solution)/shard_map/ab,...bc->...ac/dot_general | solution.py:24
  364.9 5.2 %fusion.6 = f32[4,512,32]{1,2,0:T(8,128)S(1)} fusion(f32[4,32,512]{2,1,0:T(8,128)S(1)} %fusion.18), kind=kOutput, calls=%fused_computation.25 | convolution fusion | flops 406388736 | bytes 524288 | tf_op jit(solution)/shard_map/ab,...bc->...ac/dot_general | solution.py:24
  370.1 5.2 %fusion.5 = f32[4,512,32]{1,2,0:T(8,128)S(1)} fusion(f32[4,32,512]{2,1,0:T(8,128)S(1)} %copy-done.16, f32[4,512,32]{1,2,0:T(8,128)S(1)} %convolution_multiply_fusion), kind=kOutput, calls=%fused_computation.23 | convolution fusion | flops 406388736 | bytes 786432 | tf_op jit(solution)/shard_map/ab,...bc->...ac/dot_general | solution.py:24
  (114 shorter events, 40.7 us)
Async XLA Ops:
  0.0 48.8 %copy-start.5 = (f32[262144]{0:T(1024)S(1)}, f32[262144]{0:T(1024)}, u32[]{:S(2)}) copy-start(f32[262144]{0:T(1024)} %param.5) | copy-start | bytes 3145732
  0.1 27.0 %collective-permute-start.1 = (f32[262144]{0:T(1024)S(1)}, f32[262144]{0:T(1024)S(1)}, u32[]{:S(2)}, u32[]{:S(2)}) collective-permute-start(f32[262144]{0:T(1024)S(1)} %broadcast_in_dim.190), channel_id=1, source_target_pairs={{0,16},{8,24},{16,0},{24,8},{1,17},{9,25},{17,1},{25,9},{2,18},{10... | collective-permute-start | bytes 3145736 | tf_op jit(solution)/shard_map/ppermute | solution.py:15
  3.1 45.7 %collective-permute-start = (f32[262144]{0:T(1024)}, f32[262144]{0:T(1024)}, u32[]{:S(2)}, u32[]{:S(2)}) collective-permute-start(f32[262144]{0:T(1024)} %param.5), channel_id=1, source_target_pairs={{0,16},{8,24},{16,0},{24,8},{1,17},{9,25},{17,1},{25,9},{2,18},{10... | collective-permute-start | bytes 3145736 | tf_op jit(solution)/shard_map/ppermute | solution.py:15
  50.7 3.4 copy-start.1
  50.7 3.4 collective-permute-start.2
  50.8 4.4 %collective-permute-start.3 = (f32[262144]{0:T(1024)S(1)}, f32[262144]{0:T(1024)}, u32[]{:S(2)}, u32[]{:S(2)}) collective-permute-start(f32[262144]{0:T(1024)S(1)} %get-tuple-element.22), channel_id=1, source_target_pairs={{0,8},{8,0},{16,24},{24,16},{1,9},{9,1},{17,25},{25,17},{2,10},{10... | collective-permute-start | bytes 3145736 | tf_op jit(solution)/shard_map/ppermute | solution.py:15
  51.5 9.2 %copy-start.14 = (s32[128]{0:T(128)S(1)}, s32[128]{0:T(128)}, u32[]{:S(2)}) copy-start(s32[128]{0:T(128)} %param.9) | copy-start | bytes 1540
  54.2 1.0 copy-start.9
  57.5 71.9 %copy-start = (f32[262144]{0:T(1024)}, f32[262144]{0:T(1024)S(1)}, u32[]{:S(2)}) copy-start(f32[262144]{0:T(1024)S(1)} %get-tuple-element.20) | copy-start | bytes 3145732
  57.5 71.9 %collective-permute-start.4 = (f32[262144]{0:T(1024)S(1)}, f32[262144]{0:T(1024)S(1)}, u32[]{:S(2)}, u32[]{:S(2)}) collective-permute-start(f32[262144]{0:T(1024)S(1)} %get-tuple-element.19), channel_id=1, source_target_pairs={{0,4},{1,5},{2,6},{3,7},{4,0},{5,1},{6,2},{7,3},{8,12},{9,13},{10,... | collective-permute-start | bytes 3145736 | tf_op jit(solution)/shard_map/ppermute | solution.py:15
  60.4 91.0 %collective-permute-start.5 = (f32[262144]{0:T(1024)S(1)}, f32[262144]{0:T(1024)}, u32[]{:S(2)}, u32[]{:S(2)}) collective-permute-start(f32[262144]{0:T(1024)S(1)} %get-tuple-element.20), channel_id=1, source_target_pairs={{0,4},{1,5},{2,6},{3,7},{4,0},{5,1},{6,2},{7,3},{8,12},{9,13},{10,... | collective-permute-start | bytes 3145736 | tf_op jit(solution)/shard_map/ppermute | solution.py:15
  60.7 95.4 %copy-start.11 = (s32[64]{0:T(128)S(1)}, s32[64]{0:T(128)}, u32[]{:S(2)}) copy-start(s32[64]{0:T(128)} %param.7) | copy-start | bytes 772
  60.7 95.4 %copy-start.12 = (s32[64]{0:T(128)S(1)}, s32[64]{0:T(128)}, u32[]{:S(2)}) copy-start(s32[64]{0:T(128)} %param.6) | copy-start | bytes 772
  60.7 95.5 %copy-start.13 = (f32[64]{0:T(128)S(1)}, f32[64]{0:T(128)}, u32[]{:S(2)}) copy-start(f32[64]{0:T(128)} %param.8) | copy-start | bytes 772
  129.4 1.0 copy-start.8
  153.7 26.2 %collective-permute-start.6 = (f32[262144]{0:T(1024)S(1)}, f32[262144]{0:T(1024)S(1)}, u32[]{:S(2)}, u32[]{:S(2)}) collective-permute-start(f32[262144]{0:T(1024)S(1)} %get-tuple-element.17), channel_id=1, source_target_pairs={{0,2},{1,3},{2,0},{3,1},{4,6},{5,7},{6,4},{7,5},{8,10},{9,11},{10,... | collective-permute-start | bytes 3145736 | tf_op jit(solution)/shard_map/ppermute | solution.py:15
  154.4 46.6 %collective-permute-start.7 = (f32[262144]{0:T(1024)S(1)}, f32[262144]{0:T(1024)}, u32[]{:S(2)}, u32[]{:S(2)}) collective-permute-start(f32[262144]{0:T(1024)S(1)} %get-tuple-element.18), channel_id=1, source_target_pairs={{0,2},{1,3},{2,0},{3,1},{4,6},{5,7},{6,4},{7,5},{8,10},{9,11},{10,... | collective-permute-start | bytes 3145736 | tf_op jit(solution)/shard_map/ppermute | solution.py:15
  203.9 8.2 %copy-start.2 = (f32[262144]{0:T(1024)}, f32[262144]{0:T(1024)S(1)}, u32[]{:S(2)}) copy-start(f32[262144]{0:T(1024)S(1)} %get-tuple-element.15) | copy-start | bytes 3145732
  203.9 26.1 %collective-permute-start.8 = (f32[262144]{0:T(1024)S(1)}, f32[262144]{0:T(1024)S(1)}, u32[]{:S(2)}, u32[]{:S(2)}) collective-permute-start(f32[262144]{0:T(1024)S(1)} %get-tuple-element.15), channel_id=1, source_target_pairs={{0,1},{1,0},{2,3},{3,2},{4,5},{5,4},{6,7},{7,6},{8,9},{9,8},{10,11... | collective-permute-start | bytes 3145736 | tf_op jit(solution)/shard_map/ppermute | solution.py:15
  205.3 44.9 %collective-permute-start.9 = (f32[262144]{0:T(1024)}, f32[262144]{0:T(1024)}, u32[]{:S(2)}, u32[]{:S(2)}) collective-permute-start(f32[262144]{0:T(1024)} %get-tuple-element.16), channel_id=1, source_target_pairs={{0,1},{1,0},{2,3},{3,2},{4,5},{5,4},{6,7},{7,6},{8,9},{9,8},{10,11... | collective-permute-start | bytes 3145736 | tf_op jit(solution)/shard_map/ppermute | solution.py:15
  271.2 5.7 %copy-start.15 = (f32[512,512]{1,0:T(8,128)S(1)}, f32[512,512]{1,0:T(8,128)}, u32[]{:S(2)}) copy-start(f32[512,512]{1,0:T(8,128)} %fusion.44) | copy-start | bytes 3145732
  276.9 5.7 %copy-start.4 = (f32[512,512]{1,0:T(8,128)S(1)}, f32[512,512]{1,0:T(8,128)}, u32[]{:S(2)}) copy-start(f32[512,512]{1,0:T(8,128)} %reshape.642) | copy-start | bytes 3145732
  341.0 17.5 %all-to-all-start = ((f32[32,4,512]{2,1,0:T(4,128)}), f32[32,4,512]{2,1,0:T(4,128)S(1)}, u32[]{:S(2)}, u32[]{:S(2)}) async-start(f32[32,4,512]{2,1,0:T(4,128)} %reshape.645), calls=%async_computation | async-start | bytes 524288 | tf_op jit(solution)/shard_map/all_to_all | solution.py:151
  364.9 5.2 %copy-start.16 = (f32[4,32,512]{2,1,0:T(8,128)S(1)}, f32[4,32,512]{2,1,0:T(8,128)}, u32[]{:S(2)}) copy-start(f32[4,32,512]{2,1,0:T(8,128)} %fusion.16) | copy-start | bytes 786436
  (5 other events, 4.5 us)
where the time goes:
time: 382 us; the launch traced here: 379 us
  waiting for transfers between devices  227 us (59%)
  matrix products  96 us (25%)
  other arithmetic  24.4 us (6%)
  starting transfers between devices  17.6 us (5%)
  local copies, waits for them, and re-layouts  11.6 us (3%)
    ppermute x10, waiting for transfers between devices, partner(): lax.ppermute(array, axis, [(i, i ^ 1 << distance) for i in range(lax.axis...  217 us
    dot_general x8, matrix products, apply_right(): jnp.einsum('...ab,bc->...ac', values, matrix, precision=lax.Precision.HIG...  47.9 us
    dot_general x8, matrix products, apply_left(): jnp.einsum('ab,...bc->...ac', matrix, values, precision=lax.Precision.HIG...  47.1 us
    ppermute x10, starting transfers between devices, partner(): lax.ppermute(array, axis, [(i, i ^ 1 << distance) for i in range(lax.axis...  10.8 us
    all_to_all x1, waiting for transfers between devices, body(): lax.all_to_all(outgoing, ('tx', 'ty'), split_axis=0, concat_axis=0, tiled...  10.5 us
    select_n x4, other arithmetic, body(): jnp.where(is_upper, diff_real * phase_cos + diff_imag * phase_sin, real_p...  9.49 us
  transfers between devices with their start and end apart: 11, of which 10 were waited for; matrix products, arithmetic and copies ran while one was open for 2% of the time, Pallas kernels for 0%

commit v1 on v0

v1 whole, which is shorter than its diff:
```python
import math

import jax
import jax.numpy as jnp
import numpy as np
from jax import lax
from jax.sharding import PartitionSpec as P

BL = 16384
RAD = 256
VL = BL // RAD

two_pi = 2.0 * math.pi
AXES = ("tx", "ty")


def grid(first, second, modulus):
    return (two_pi / modulus) * (np.outer(first, second) % modulus)


def const(array):
    return jnp.asarray(np.ascontiguousarray(array, dtype=np.float32))


def dot(spec, left, right):
    return jnp.einsum(spec, left, right, precision=lax.Precision.HIGH)


def exchange(blocks):
    return lax.all_to_all(blocks, AXES, split_axis=0, concat_axis=0, tiled=True)


def lookup(values_table, positions):
    one_hot = positions[:, None] == jnp.arange(values_table.shape[0], dtype=jnp.int32)[None, :]
    return jnp.sum(
        jnp.where(one_hot, values_table[None, :], jnp.zeros((), values_table.dtype)), axis=1
    )


def row_bases(devices):
    half = RAD // (2 * devices)
    base = np.zeros((devices, 2, half), np.int64)
    for f in range(devices):
        for i in range(half):
            base[f, :, i] = f + 2 * devices * i if f else devices * i
    base[0, 1, 0] = RAD // 2
    return base


def body(signal, band_start, band_width, band_gain, slot_band):
    devices = lax.axis_size("tx") * lax.axis_size("ty")
    device = lax.axis_index("tx") * lax.axis_size("ty") + lax.axis_index("ty")
    length = signal.shape[0]
    total = length * devices
    own = length // (RAD * RAD)
    cols = own * devices
    chunk = length // cols
    base = row_bases(devices)
    half = base.shape[2]
    span = np.arange(RAD)

    turned = signal.reshape(chunk, cols).T.reshape(devices, own, chunk)
    column = exchange(turned)
    column = column.reshape(devices, own, chunk // RAD, RAD).transpose(1, 0, 2, 3).reshape(own, RAD, RAD)

    angle = grid(base.reshape(-1), span, RAD)
    section_real = dot("rp,cpz->crz", const(np.cos(angle)), column)
    section_imag = dot("rp,cpz->crz", const(-np.sin(angle)), column)
    angle = grid(base.reshape(-1), span, RAD * RAD)
    twist_cos, twist_sin = const(np.cos(angle)), const(np.sin(angle))
    turned_real = section_real * twist_cos + section_imag * twist_sin
    turned_imag = section_imag * twist_cos - section_real * twist_sin
    both = jnp.concatenate([turned_real, turned_imag], axis=2).reshape(own, devices, 2, half, 2 * RAD)
    angle = grid(span, span, RAD)
    cos_m, sin_m = np.cos(angle), np.sin(angle)
    minus = np.concatenate([cos_m + sin_m, sin_m - cos_m], axis=0)
    plus = np.concatenate([cos_m - sin_m, cos_m + sin_m], axis=0)
    bins = dot("cfhiz,hzq->fchiq", both, const(np.stack([minus, plus]) / math.sqrt(total)))

    value = exchange(bins).reshape(cols, 2, half, RAD)

    is_first = device == 0
    swap0 = np.zeros((RAD, RAD))
    swap0[(-span) % RAD, span] = 1.0
    swap1 = np.zeros((RAD, RAD))
    swap1[RAD - 1 - span, span] = 1.0
    own0 = jnp.einsum("cq,qr->cr", value[:, 0, 0], const(swap0), precision=lax.Precision.HIGHEST)
    own1 = jnp.einsum("cq,qr->cr", value[:, 1, 0], const(swap1), precision=lax.Precision.HIGHEST)
    other = value[:, ::-1]
    other = other.at[:, 0, 0].set(jnp.where(is_first, own0, other[:, 0, 0]))
    other = other.at[:, 1, 0].set(jnp.where(is_first, own1, other[:, 1, 0]))
    my_base = lax.dynamic_index_in_dim(jnp.asarray(base.astype(np.int32)), device, 0, keepdims=False)
    col = np.arange(cols)
    beta = (jnp.asarray(col.astype(np.int32))[:, None, None] * my_base[None]).astype(jnp.float32) * (two_pi / total)
    beta_cos, beta_sin = jnp.cos(beta)[..., None], jnp.sin(beta)[..., None]
    alpha = grid(col, RAD * span, total)
    alpha_cos, alpha_sin = const(np.cos(alpha))[:, None, None], const(np.sin(alpha))[:, None, None]
    theta_cos = alpha_cos * beta_cos - alpha_sin * beta_sin
    theta_sin = alpha_sin * beta_cos + alpha_cos * beta_sin
    sign = const(np.array([1.0, -1.0]))[None, :, None, None]
    signed = sign * other
    lead = theta_cos * value + theta_sin * signed
    trail = theta_cos * signed - theta_sin * value
    angle = grid(col, col, cols)
    table = dot("gc,chiq->hgqi", const(np.cos(angle)), lead) + dot(
        "gc,chiq->hgqi", const(np.sin(angle)), trail
    )

    rows = total // RAD
    slot_index = jnp.maximum(slot_band, 0)
    starts = lookup(band_start, slot_index)
    first = starts // RAD
    remain = starts % RAD
    table = table.reshape(2, rows, half)
    begin = jnp.stack([first, rows - 1 - first - VL])
    take = lambda part, at: lax.dynamic_slice(part, (at, 0), (VL + 1, half))
    window = jax.vmap(lambda part, at: jax.vmap(lambda a: take(part, a))(at))(table, begin)
    residue = (my_base * jnp.asarray([[1], [-1]], jnp.int32)) % RAD
    wraps = residue[:, None, :] < remain[None, :, None]
    ahead = jnp.concatenate([jnp.where(wraps[0], window[0, :, VL], window[0, :, 0])[:, None], window[0, :, 1:VL]], axis=1)
    back = jnp.concatenate([window[1, :, 1:VL], jnp.where(wraps[1], window[1, :, 0], window[1, :, VL])[:, None]], axis=1)
    slots = slot_band.shape[0] // devices
    outgoing = jnp.stack([ahead, back], axis=1).transpose(0, 1, 3, 2).reshape(devices, slots, 2, half, VL)
    incoming = exchange(outgoing)

    mine = lambda array: lax.dynamic_slice_in_dim(array, device * slots, slots)
    my_slots = mine(slot_band)
    my_index = jnp.maximum(my_slots, 0)
    my_start, my_remain = mine(starts), mine(remain)
    my_width = lookup(band_width, my_index).astype(jnp.float32)
    my_gain = lookup(band_gain, my_index)
    all_residue = (base * np.array([1, -1])[None, :, None]) % RAD
    step = np.stack([np.arange(VL), VL - 1 - np.arange(VL)])
    place = step[None, :, None, :] * RAD + all_residue[..., None]
    position = (jnp.asarray(place.astype(np.int32))[:, None] - my_remain[None, :, None, None, None]) % BL
    position = position.astype(jnp.float32)
    wide = my_width[None, :, None, None, None]
    taper_gain = jnp.where(
        position < wide, 0.5 - 0.5 * jnp.cos(two_pi * (position + 0.5) / wide), 0.0
    )
    tapered = incoming * taper_gain
    angle = np.stack([grid(step[0], np.arange(VL), VL), grid(step[1], np.arange(VL), VL)])
    part_real = dot("fshiv,hvt->sfhit", tapered, const(np.cos(angle)))
    part_imag = dot("fshiv,hvt->sfhit", tapered, const(-np.sin(angle)))
    angle = grid(all_residue.reshape(-1), np.arange(VL), BL).reshape(base.shape + (VL,))
    twist_cos, twist_sin = const(np.cos(angle)), const(np.sin(angle))
    turned_real = (part_real * twist_cos + part_imag * twist_sin).reshape(slots, RAD, VL)
    turned_imag = (part_imag * twist_cos - part_real * twist_sin).reshape(slots, RAD, VL)
    stacked = jnp.concatenate([turned_real, turned_imag], axis=1)
    angle = grid(span, all_residue.reshape(-1), RAD)
    cos_m, sin_m = np.cos(angle), np.sin(angle)
    real = dot("ur,srt->sut", const(np.concatenate([cos_m, sin_m], axis=1)), stacked)
    imag = dot("ur,srt->sut", const(np.concatenate([-sin_m, cos_m], axis=1)), stacked)
    when = jnp.arange(BL, dtype=jnp.int32).reshape(RAD, VL)
    phase = (my_remain[:, None, None] * when[None] % BL).astype(jnp.float32) * (two_pi / BL)
    phase_cos, phase_sin = jnp.cos(phase), jnp.sin(phase)
    result = real * (phase_cos - phase_sin) - imag * (phase_sin + phase_cos)
    scale = jnp.where(my_slots >= 0, my_gain / jnp.sqrt(my_width), 0.0)
    return (result * scale[:, None, None]).reshape(slots, BL)


def solution(mesh):
    return jax.shard_map(
        body,
        mesh=mesh,
        in_specs=(P(AXES), P(), P(), P(), P()),
        out_specs=P(AXES, None),
        check_vma=False,
    )
```

time: 382 us -> 174 us (0.46)
  waiting for transfers between devices: 227 us -> 34.7 us
  matrix products: 96 us -> 16.9 us
  local copies, waits for them, and re-layouts: 11.6 us -> 74.2 us
  blocking collectives: 0 us -> 34.7 us
  other arithmetic: 24.4 us -> 6.04 us
  starting transfers between devices: 17.6 us -> 5.67 us
    ppermute x10 -> x0, waiting for transfers between devices: 217 us -> none  [partner(): lax.ppermute(array, axis, [(i, i ^ 1 << distance) for i in range(lax.axis...]
    dot_general x17 -> x11, matrix products: 96 us -> 16.9 us  [the longest x9 14.4 us: dot(): return jnp.einsum(spec, left, right, precision=lax.Precision.HIGH)]
    all_to_all x0 -> x1, blocking collectives: none -> 34.7 us  [exchange(): return lax.all_to_all(blocks, AXES, split_axis=0, concat_axis=0, tiled=True)]
    all_to_all x1 -> x2, waiting for transfers between devices: 10.5 us -> 34.7 us  [exchange(): return lax.all_to_all(blocks, AXES, split_axis=0, concat_axis=0, tiled=True)]
    reshape x4 -> x8, local copies, waits for them, and re-layouts: 2.28 us -> 25.8 us  [the longest x1 23.1 us: body(): table = table.reshape(2, rows, half)]
    gather x2 -> x1, local copies, waits for them, and re-layouts: 1.51 us -> 21.9 us  [body(): take = lambda part, at: lax.dynamic_slice(part, (at, 0), (VL + 1, half))]
    ppermute x10 -> x0, starting transfers between devices: 10.8 us -> none  [partner(): lax.ppermute(array, axis, [(i, i ^ 1 << distance) for i in range(lax.axis...]
    select_n x15 -> x4, other arithmetic: 11.5 us -> 0.86 us  [the longest x1 0.76 us: body(): residue = my_base * jnp.asarray([[1], [-1]], jnp.int32) % RAD]
  transfers between devices with their start and end apart: 11 -> 2, of which waited for: 10 -> 2; matrix products, arithmetic and copies ran while one was open for 2% -> 2% of each run, Pallas kernels for 0% -> 0%
where the time goes in v1:
time: 174 us; the launch traced here: 173 us
  local copies, waits for them, and re-layouts  74.2 us (43%)
  blocking collectives  34.7 us (20%)
  waiting for transfers between devices  34.7 us (20%)
  matrix products  16.9 us (10%)
  other arithmetic  6.04 us (3%)
  starting transfers between devices  5.67 us (3%)
    all_to_all x2, waiting for transfers between devices, exchange(): return lax.all_to_all(blocks, AXES, split_axis=0, concat_axis=0, tiled=True)  34.7 us
    all_to_all x1, blocking collectives, exchange(): return lax.all_to_all(blocks, AXES, split_axis=0, concat_axis=0, tiled=True)  34.7 us
    reshape x1, local copies, waits for them, and re-layouts, body(): table = table.reshape(2, rows, half)  23.1 us
    gather x1, local copies, waits for them, and re-layouts, body(): take = lambda part, at: lax.dynamic_slice(part, (at, 0), (VL + 1, half))  21.9 us
    dot_general x9, matrix products, dot(): return jnp.einsum(spec, left, right, precision=lax.Precision.HIGH)  14.4 us
    unnamed x56, local copies, waits for them, and re-layouts  9.71 us
    slice x1, local copies, waits for them, and re-layouts, body(): window[0, :, 1:VL]  7.72 us
    all_to_all x2, starting transfers between devices, exchange(): return lax.all_to_all(blocks, AXES, split_axis=0, concat_axis=0, tiled=True)  5.67 us
  transfers between devices with their start and end apart: 2, of which 2 were waited for; matrix products, arithmetic and copies ran while one was open for 2% of the time, Pallas kernels for 0%

profile of v1, /device:TPU:0, one launch (start us, length us, event | category | flops | bytes accessed | tf_op | source)
XLA Modules:
  0.0 172.8 jit_solution(7511747339865294954)
XLA Ops:
  0.0 1.6 copy.186
  2.0 34.7 %all_to_all.15 = f32[32,4,2048]{2,1,0:T(4,128)S(1)} all-to-all(f32[32,4,2048]{2,1,0:T(4,128)S(1)} %reshape.364), channel_id=1, replica_groups=mesh['tx'=4,'ty'=8] {'tx','ty'}, dimensions={0} | all-to-all | bytes 2097152 | tf_op jit(solution)/shard_map/all_to_all | solution.py:30
  38.2 1.2 add_bitcast_fusion
  39.6 2.0 %copy.190 = f32[4,256,512]{2,0,1:T(4,128)} copy(f32[4,256,512]{1,2,0:T(8,128)S(1)} %pad_maximum_fusion) | data formatting | bytes 4194304 | tf_op jit(solution)/shard_map/concatenate | solution.py:73
  41.6 3.7 %fusion.2 = f32[32,4,2,4,256]{4,0,3,1,2:T(8,128)S(1)} fusion(f32[2,512,256,1,1]{2,1,4,3,0:T(8,128)S(1)} %copy-done, f32[4,32,2,4,512]{4,0,3,2,1:T(4,128)} %bitcast.148), kind=kOutput, calls=%fused_computation.4 | convolution fusion | flops 805306368 | bytes 4194304 | tf_op jit(solution)/shard_map/cfhiz,hzq->fchiq/dot_general | solution.py:26
  45.3 1.7 copy.192
  47.0 2.8 %all-to-all-start.1 = ((f32[32,4,2,4,256]{4,3,1,2,0:T(4,128)}), f32[32,4,2,4,256]{4,3,1,2,0:T(4,128)S(1)}, u32[]{:S(2)}, u32[]{:S(2)}) async-start(f32[32,4,2,4,256]{4,3,1,2,0:T(4,128)} %copy.192), calls=%async_computation.1 | async-start | bytes 2097152 | tf_op jit(solution)/shard_map/all_to_all | solution.py:30
  52.3 24.9 %all-to-all-done.1 = f32[32,4,2,4,256]{4,3,1,2,0:T(4,128)S(1)} async-done(((f32[32,4,2,4,256]{4,3,1,2,0:T(4,128)}), f32[32,4,2,4,256]{4,3,1,2,0:T(4,128)S(1)}, u32[]{:S(2)}, u32[]{:S(2)}) %all-to-all-start.1) | async-done | bytes 1048608 | tf_op jit(solution)/shard_map/all_to_all | solution.py:30
  78.0 1.3 fusion.13
  79.3 1.2 fusion.11
  80.6 2.6 %fusion.21 = f32[2,4,256,128]{3,2,1,0:T(8,128)S(1)} fusion(f32[128,128,1,1]{1,0,3,2:T(8,128)} %constant.254, f32[128,2,4,256]{3,0,2,1:T(8,128)S(1)} %fusion.11, f32[2]{0:T(128)} %constant.216.clone, f32[128,2,4]{0,2,1:T(4,128)S(1)} %get-tuple-element.42, f32[128,256]{1,0:T(8,128)S(1)} %copy-done.2, f32[128,2,4]{0,2,1:T(4,128)S(1)} %get-tuple-element.41, ...), kind=kOutput, calls=%fused_computation.30 | convolution fusion | flops 203948032 | bytes 3481608 | tf_op jit(solution)/shard_map/gc,chiq->hgqi/dot_general | solution.py:26
  83.1 2.4 %fusion.5 = f32[2,128,256,4]{1,2,3,0:T(8,128)S(1)} fusion(f32[2,4,256,128]{3,2,1,0:T(8,128)S(1)} %fusion.21, f32[128,128,1,1]{1,0,3,2:T(8,128)S(1)} %copy-done.10, f32[128,2,4,256]{3,0,2,1:T(8,128)S(1)} %fusion.11, f32[2]{0:T(128)} %constant.216.clone, f32[128,2,4]{0,2,1:T(4,128)S(1)} %get-tuple-element.42, f32[128,256]{1,0:T(8,128)S(1)} %copy-done.2, ...), kind=kOutput, calls=%fused_computation.6 | convolution fusion | flops 204210176 | bytes 4530184 | tf_op jit(solution)/shard_map/gc,chiq->hgqi/dot_general | solution.py:26
  85.5 23.1 %copy.229 = f32[2,128,256,4]{3,0,2,1:T(2,128)} copy(f32[2,128,256,4]{1,2,3,0:T(8,128)S(1)} %fusion.5) | data formatting | bytes 2097152 | tf_op jit(solution)/shard_map/reshape | solution.py:114
  108.7 21.9 %gather_fusion = f32[256,65,4]{2,0,1:T(8,128)} fusion(f32[2,32768,4]{2,0,1:T(2,128)} %bitcast.140, s32[256]{0:T(256)S(1)} %bitcast.147), kind=kCustom, calls=%fused_computation | custom fusion | bytes 535552 | tf_op jit(solution)/shard_map/vmap(vmap())/gather | solution.py:116
  131.5 7.7 %fusion.65 = (f32[1,128,63,4]{3,1,0,2:T(8,128)}, f32[1,128,63,4]{3,1,0,2:T(8,128)}) fusion(f32[2,128,65,4]{3,1,0,2:T(8,128)} %bitcast.142), kind=kLoop, calls=%fused_computation.124 | loop fusion | bytes 516096 | tf_op jit(solution)/shard_map/slice | solution.py:120
  139.9 3.9 %copy.234 = f32[1,128,63,4]{2,1,3,0:T(8,128)S(1)} copy(f32[1,128,63,4]{3,1,0,2:T(8,128)} %get-tuple-element.33) | data formatting | bytes 258048
  143.8 3.9 %copy.235 = f32[1,128,63,4]{2,1,3,0:T(8,128)S(1)} copy(f32[1,128,63,4]{3,1,0,2:T(8,128)} %get-tuple-element.34) | data formatting | bytes 258048
  148.2 1.2 reshape.392
  149.4 2.8 %all-to-all-start.2 = ((f32[32,1,2048]{2,1,0:T(1,128)}), f32[32,1,2048]{2,1,0:T(1,128)S(1)}, u32[]{:S(2)}, u32[]{:S(2)}) async-start(f32[32,1,2048]{2,1,0:T(1,128)} %reshape.392), calls=%async_computation.2 | async-start | bytes 524288 | tf_op jit(solution)/shard_map/all_to_all | solution.py:30
  152.8 9.8 %all-to-all-done.2 = f32[32,1,2048]{2,1,0:T(1,128)S(1)} async-done(((f32[32,1,2048]{2,1,0:T(1,128)}), f32[32,1,2048]{2,1,0:T(1,128)S(1)}, u32[]{:S(2)}, u32[]{:S(2)}) %all-to-all-start.2) | async-done | bytes 262176 | tf_op jit(solution)/shard_map/all_to_all | solution.py:30
  163.1 1.3 reduce.4
  164.8 2.2 %copy_multiply_fusion = f32[32,4,2,4,64]{4,0,3,2,1:T(8,128)S(1)} fusion(f32[32,4,2,4,64]{4,1,3,2,0:T(4,128)S(1)} %bitcast.149, f32[4]{0:T(128)S(1)} %convert_element_type.25, s32[4]{0:T(128)S(1)} %dynamic_slice.11, s32[32,2,4,64]{3,0,2,1:T(8,128)S(1)} %copy-done.9), kind=kLoop, calls=%fused_computation.49 | loop fusion | flops 1376256 | bytes 589856 | tf_op jit(solution)/shard_map/mul | solution.py:141
  168.9 1.3 fusion.6
  170.3 1.3 fusion.9
  (94 shorter events, 11.6 us)
Async XLA Ops:
  0.0 37.2 %copy-start.3 = (f32[256,256,1]{1,0,2:T(8,128)S(1)}, f32[256,256,1]{1,0,2:T(8,128)}, u32[]{:S(2)}) copy-start(f32[256,256,1]{1,0,2:T(8,128)} %constant.252) | copy-start | bytes 786436
  1.6 36.6 %copy-start.4 = (f32[256,256]{0,1:T(8,128)S(1)}, f32[256,256]{0,1:T(8,128)}, u32[]{:S(2)}) copy-start(f32[256,256]{0,1:T(8,128)} %constant.208.clone) | copy-start | bytes 786436
  1.6 36.6 %copy-start.5 = (f32[256,256]{0,1:T(8,128)S(1)}, f32[256,256]{0,1:T(8,128)}, u32[]{:S(2)}) copy-start(f32[256,256]{0,1:T(8,128)} %constant.209.clone) | copy-start | bytes 786436
  1.6 36.6 %copy-start.6 = (f32[256,256,1]{1,0,2:T(8,128)S(1)}, f32[256,256,1]{1,0,2:T(8,128)}, u32[]{:S(2)}) copy-start(f32[256,256,1]{1,0,2:T(8,128)} %constant.251) | copy-start | bytes 786436
  41.6 8.3 %copy-start.13 = (s32[128]{0:T(128)S(1)}, s32[128]{0:T(128)}, u32[]{:S(2)}) copy-start(s32[128]{0:T(128)} %param.35) | copy-start | bytes 1540
  41.6 9.6 %copy-start.18 = (s32[64]{0:T(128)S(1)}, s32[64]{0:T(128)}, u32[]{:S(2)}) copy-start(s32[64]{0:T(128)} %param.32) | copy-start | bytes 772
  41.6 9.8 %copy-start.17 = (s32[2]{0:T(128)S(1)}, s32[2]{0:T(128)}, u32[]{:S(2)}) copy-start(s32[2]{0:T(128)} %constant.229) | copy-start | bytes 28
  47.0 30.2 %all-to-all-start.1 = ((f32[32,4,2,4,256]{4,3,1,2,0:T(4,128)}), f32[32,4,2,4,256]{4,3,1,2,0:T(4,128)S(1)}, u32[]{:S(2)}, u32[]{:S(2)}) async-start(f32[32,4,2,4,256]{4,3,1,2,0:T(4,128)} %copy.192), calls=%async_computation.1 | async-start | bytes 2097152 | tf_op jit(solution)/shard_map/all_to_all | solution.py:30
  49.8 30.7 %copy-start.1 = (f32[128,256]{1,0:T(8,128)S(1)}, f32[128,256]{1,0:T(8,128)}, u32[]{:S(2)}) copy-start(f32[128,256]{1,0:T(8,128)} %constant.214.clone) | copy-start | bytes 393220
  49.8 30.7 %copy-start.2 = (f32[128,256]{1,0:T(8,128)S(1)}, f32[128,256]{1,0:T(8,128)}, u32[]{:S(2)}) copy-start(f32[128,256]{1,0:T(8,128)} %constant.215.clone) | copy-start | bytes 393220
  51.4 26.1 %copy-start.15 = (s32[128]{0:T(128)}, s32[128]{0:T(128)S(1)}, u32[]{:S(2)}) copy-start(s32[128]{0:T(128)S(1)} %and_select_fusion.1) | copy-start | bytes 1540
  78.0 5.1 %copy-start.10 = (f32[128,128,1,1]{1,0,3,2:T(8,128)S(1)}, f32[128,128,1,1]{1,0,3,2:T(8,128)}, u32[]{:S(2)}) copy-start(f32[128,128,1,1]{1,0,3,2:T(8,128)} %constant.255) | copy-start | bytes 196612
  143.8 8.4 %copy-start.19 = (s32[64]{0:T(128)S(1)}, s32[64]{0:T(128)}, u32[]{:S(2)}) copy-start(s32[64]{0:T(128)} %param.33) | copy-start | bytes 772
  143.8 8.4 %copy-start.23 = (s32[4]{0:T(128)S(1)}, s32[4]{0:T(128)}, u32[]{:S(2)}) copy-start(s32[4]{0:T(128)} %broadcast_maximum_fusion) | copy-start | bytes 52
  143.8 8.6 %copy-start.16 = (s32[128]{0:T(128)S(1)}, s32[128]{0:T(128)}, u32[]{:S(2)}) copy-start(s32[128]{0:T(128)} %copy-done.15) | copy-start | bytes 1540
  143.8 8.7 %copy-start.20 = (f32[64]{0:T(128)S(1)}, f32[64]{0:T(128)}, u32[]{:S(2)}) copy-start(f32[64]{0:T(128)} %param.34) | copy-start | bytes 772
  143.8 8.9 %copy-start.14 = (s32[128]{0:T(128)S(1)}, s32[128]{0:T(128)}, u32[]{:S(2)}) copy-start(s32[128]{0:T(128)} %param.35) | copy-start | bytes 1540
  147.7 17.0 %copy-start.9 = (s32[32,2,4,64]{3,0,2,1:T(8,128)S(1)}, s32[32,2,4,64]{3,0,2,1:T(8,128)}, u32[]{:S(2)}) copy-start(s32[32,2,4,64]{3,0,2,1:T(8,128)} %constant.220.clone) | copy-start | bytes 196612
  147.7 19.2 %copy-start.12 = (f32[2,64,64,1,1]{2,1,4,3,0:T(8,128)S(1)}, f32[2,64,64,1,1]{2,1,4,3,0:T(8,128)}, u32[]{:S(2)}) copy-start(f32[2,64,64,1,1]{2,1,4,3,0:T(8,128)} %constant.256) | copy-start | bytes 98308
  147.7 19.6 %copy-start.7 = (f32[32,2,4,64]{3,0,2,1:T(8,128)S(1)}, f32[32,2,4,64]{3,0,2,1:T(8,128)}, u32[]{:S(2)}) copy-start(f32[32,2,4,64]{3,0,2,1:T(8,128)} %constant.223.clone) | copy-start | bytes 196612
  147.7 19.6 %copy-start.8 = (f32[32,2,4,64]{3,0,2,1:T(8,128)S(1)}, f32[32,2,4,64]{3,0,2,1:T(8,128)}, u32[]{:S(2)}) copy-start(f32[32,2,4,64]{3,0,2,1:T(8,128)} %constant.224.clone) | copy-start | bytes 196612
  147.8 19.6 %copy-start.11 = (f32[2,64,64,1,1]{2,1,4,3,0:T(8,128)S(1)}, f32[2,64,64,1,1]{2,1,4,3,0:T(8,128)}, u32[]{:S(2)}) copy-start(f32[2,64,64,1,1]{2,1,4,3,0:T(8,128)} %constant.257) | copy-start | bytes 98308
  149.4 13.2 %all-to-all-start.2 = ((f32[32,1,2048]{2,1,0:T(1,128)}), f32[32,1,2048]{2,1,0:T(1,128)S(1)}, u32[]{:S(2)}, u32[]{:S(2)}) async-start(f32[32,1,2048]{2,1,0:T(1,128)} %reshape.392), calls=%async_computation.2 | async-start | bytes 524288 | tf_op jit(solution)/shard_map/all_to_all | solution.py:30
  164.7 4.2 %copy-start.22 = (f32[256,512,1]{1,0,2:T(8,128)S(1)}, f32[256,512,1]{1,0,2:T(8,128)}, u32[]{:S(2)}) copy-start(f32[256,512,1]{1,0,2:T(8,128)} %constant.258) | copy-start | bytes 1572868
  (2 other events, 5.0 us)

commit v2 on v1

v2 whole, which is shorter than its diff:
```python
import math

import jax
import jax.numpy as jnp
import numpy as np
from jax import lax
from jax.experimental import pallas as pl
from jax.experimental.pallas import tpu as pltpu
from jax.sharding import PartitionSpec as P

BL = 16384
RAD = 256
VL = BL // RAD

two_pi = 2.0 * math.pi
AXES = ("tx", "ty")


def grid(first, second, modulus):
    return (two_pi / modulus) * (np.outer(first, second) % modulus)


def const(array):
    return jnp.asarray(np.ascontiguousarray(array, dtype=np.float32))


def dot(spec, left, right):
    return jnp.einsum(spec, left, right, precision=lax.Precision.HIGH)


def exchange(blocks):
    return lax.all_to_all(blocks, AXES, split_axis=0, concat_axis=0, tiled=True)


def lookup(values_table, positions):
    one_hot = positions[:, None] == jnp.arange(values_table.shape[0], dtype=jnp.int32)[None, :]
    return jnp.sum(
        jnp.where(one_hot, values_table[None, :], jnp.zeros((), values_table.dtype)), axis=1
    )


def row_bases(devices):
    half = RAD // (2 * devices)
    base = np.zeros((devices, 2, half), np.int64)
    for f in range(devices):
        for i in range(half):
            base[f, :, i] = f + 2 * devices * i if f else devices * i
    base[0, 1, 0] = RAD // 2
    return base


def split(array):
    high = array.astype(jnp.bfloat16)
    return high, (array - high.astype(jnp.float32)).astype(jnp.bfloat16)


def const_split(array):
    array = np.ascontiguousarray(array, dtype=np.float32)
    high = array.astype(jnp.bfloat16)
    return jnp.asarray(np.stack([high, (array - high.astype(np.float32)).astype(jnp.bfloat16)]))


def product(left, right):
    (left_high, left_low), (right_high, right_low) = left, right
    one = lambda a, b: jnp.dot(a, b, preferred_element_type=jnp.float32)
    return one(left_high, right_high) + (one(left_high, right_low) + one(left_low, right_high))


def combine_kernel(
    own, half, total, device_ref, start_ref, value_ref, alpha_ref, beta_ref, mix_ref, swap_ref, residue_ref,
    out_ref, table_ref,
):
    rows = total // RAD
    count = value_ref.shape[0]
    cols = count // 2
    tiles = rows // (2 * VL)
    is_upper = lax.broadcasted_iota(jnp.int32, (count, RAD), 0) // own % 2 == 1

    def exchange_rows(block):
        cut = block.reshape(count // (2 * own), 2, own, RAD)
        return jnp.concatenate([cut[:, 1:], cut[:, :1]], axis=1).reshape(count, RAD)

    def twist(block, at):
        beta_cos, beta_sin = beta_ref[0, :, at : at + 1], beta_ref[1, :, at : at + 1]
        theta_cos = alpha_ref[0] * beta_cos - alpha_ref[1] * beta_sin
        theta_sin = alpha_ref[1] * beta_cos + alpha_ref[0] * beta_sin
        return theta_cos * block + theta_sin * exchange_rows(block)

    mix = mix_ref[0], mix_ref[1]

    def put(result, h, i):
        for side in range(2):
            at = pl.ds(8 * side + h * half + i, cols, stride=16)
            table_ref[at, :] = result[:, side * 128 : (side + 1) * 128]

    for i in range(half):
        result = product(mix, split(twist(value_ref[:, i * RAD : (i + 1) * RAD], i)))
        for h in range(2):
            put(result[h * cols : (h + 1) * cols], h, i)

    @pl.when(device_ref[0] == 0)
    def _():
        block = value_ref[:, :RAD]
        high, low = split(block)
        for h in range(2):
            turn = lambda part: jnp.dot(part, swap_ref[h], preferred_element_type=jnp.float32)
            mirror = exchange_rows(turn(high) + turn(low))
            keep = is_upper if h else ~is_upper
            spun = split(twist(jnp.where(keep, block, mirror), h * half))
            rows_of = slice(h * cols, (h + 1) * cols)
            put(product((mix_ref[0, rows_of], mix_ref[1, rows_of]), spun), h, 0)

    shape = (2 * half, 128)
    lane = lax.broadcasted_iota(jnp.int32, shape, 1)
    is_low = lane < VL
    is_back = lax.broadcasted_iota(jnp.int32, shape, 0) >= half
    residue = residue_ref[...]

    def load(tile):
        return table_ref[pl.ds(pl.multiple_of(tile * 8, 8), 8), :][: 2 * half]

    def window(slot):
        start = start_ref[slot]
        block = start // BL
        back = rows // VL - 2 - block
        tiles_of = [block // 2, (block + 1) // 2, back // 2, (back + 1) // 2]
        ahead_high, ahead_low, back_high, back_low = [load(t) for t in tiles_of]
        picked = jnp.where(is_low, jnp.where(is_back, back_low, ahead_low), jnp.where(is_back, back_high, ahead_high))
        ahead_at = 128 * jnp.where(is_low, tiles_of[1], tiles_of[0]) + lane
        back_at = rows - 1 - (128 * jnp.where(is_low, tiles_of[3], tiles_of[2]) + lane)
        place = RAD * jnp.where(is_back, back_at, ahead_at) + residue - start
        picked = jnp.where((place >= 0) & (place < BL), picked, 0.0)
        return picked + pltpu.roll(picked, VL, 1)

    def step(pair, carry):
        out_ref[pair] = jnp.where(is_low, window(2 * pair), window(2 * pair + 1))
        return carry

    lax.fori_loop(0, out_ref.shape[0], step, 0, unroll=4)


def combine(value, starts, device, base, own, total):
    devices, _, half = base.shape
    count = value.shape[0]
    cols = count // 2
    span = np.arange(RAD)
    col = np.arange(cols)
    sign = np.array([1.0, -1.0])[None, :, None]

    def rows_of(angle):
        part = angle.reshape(devices, 1, own, -1)
        put = lambda array: np.broadcast_to(array, (devices, 2, own, part.shape[-1])).reshape(count, -1)
        return np.stack([put(np.cos(part)), put(sign[..., None] * np.sin(part))]).astype(np.float32)

    alpha = rows_of(grid(col, RAD * span, total))
    at = np.concatenate([base[:, 0], base[:, 1, :1]], axis=1).astype(np.int32)
    at = lax.dynamic_index_in_dim(jnp.asarray(at), device, 0, keepdims=False)
    col_of = np.broadcast_to(col.reshape(devices, 1, own), (devices, 2, own)).reshape(count, 1)
    sign_of = np.broadcast_to(np.array([1.0, -1.0])[:, None], (devices, 2, own)).reshape(count, 1)
    angle = (jnp.asarray(col_of.astype(np.int32)) * at[None]).astype(jnp.float32) * (two_pi / total)
    beta = jnp.stack([jnp.cos(angle), const(sign_of) * jnp.sin(angle)])
    angle = grid(col, col, cols).reshape(cols, devices, 1, own)
    ahead = np.concatenate([np.cos(angle), np.sin(angle)], axis=2)
    back = np.concatenate([-np.sin(angle), np.cos(angle)], axis=2)
    mix = np.stack([ahead, back]).reshape(count, count)
    swap = np.zeros((2, RAD, RAD))
    swap[0, (-span) % RAD, span] = 1.0
    swap[1, RAD - 1 - span, span] = 1.0
    residue = ((base * np.array([1, -1])[None, :, None]) % RAD).reshape(devices, 2 * half, 1)
    residue = jnp.asarray(np.broadcast_to(residue, (devices, 2 * half, 128)).astype(np.int32))
    residue = lax.dynamic_index_in_dim(residue, device, 0, keepdims=False)
    smem = pl.BlockSpec(memory_space=pltpu.SMEM)
    vmem = pl.BlockSpec(memory_space=pltpu.VMEM)
    rows = total // RAD
    return pl.pallas_call(
        lambda *refs: combine_kernel(own, half, total, *refs),
        out_shape=jax.ShapeDtypeStruct((starts.shape[0] // 2, 2 * half, 128), jnp.float32),
        in_specs=[smem, smem] + [vmem] * 6,
        out_specs=vmem,
        scratch_shapes=[pltpu.VMEM((rows // 16, 128), jnp.float32)],
        compiler_params=pltpu.CompilerParams(vmem_limit_bytes=48 * 1024 * 1024),
        name="combine",
    )(
        device.reshape(1).astype(jnp.int32), starts, value, const(alpha), beta, const_split(mix),
        jnp.asarray(swap.astype(np.float32).astype(jnp.bfloat16)), residue,
    )


def body(signal, band_start, band_width, band_gain, slot_band):
    devices = lax.axis_size("tx") * lax.axis_size("ty")
    device = lax.axis_index("tx") * lax.axis_size("ty") + lax.axis_index("ty")
    length = signal.shape[0]
    total = length * devices
    own = length // (RAD * RAD)
    cols = own * devices
    chunk = length // cols
    base = row_bases(devices)
    half = base.shape[2]
    span = np.arange(RAD)

    turned = signal.reshape(chunk, cols).T.reshape(devices, own, chunk)
    column = exchange(turned)
    column = column.reshape(devices, own, chunk // RAD, RAD).transpose(1, 0, 2, 3).reshape(own, RAD, RAD)

    angle = grid(base.reshape(-1), span, RAD)
    section_real = dot("rp,cpz->crz", const(np.cos(angle)), column)
    section_imag = dot("rp,cpz->crz", const(-np.sin(angle)), column)
    angle = grid(base.reshape(-1), span, RAD * RAD)
    twist_cos, twist_sin = const(np.cos(angle)), const(np.sin(angle))
    turned_real = section_real * twist_cos + section_imag * twist_sin
    turned_imag = section_imag * twist_cos - section_real * twist_sin
    both = jnp.concatenate([turned_real, turned_imag], axis=2).reshape(own, devices, 2, half, 2 * RAD)
    angle = grid(span, span, RAD)
    cos_m, sin_m = np.cos(angle), np.sin(angle)
    minus = np.concatenate([cos_m + sin_m, sin_m - cos_m], axis=0)
    plus = np.concatenate([cos_m - sin_m, cos_m + sin_m], axis=0)
    bins = dot("cfhiz,hzq->fhciq", both, const(np.stack([minus, plus]) / math.sqrt(total)))

    value = exchange(bins).reshape(2 * cols, half * RAD)

    slot_index = jnp.maximum(slot_band, 0)
    starts = lookup(band_start, slot_index)
    outgoing = combine(value, starts, device, base, own, total)
    slots = slot_band.shape[0] // devices
    incoming = exchange(outgoing.reshape(devices, slots // 2, 2 * half, 2 * VL))
    incoming = incoming.reshape(devices, slots // 2, 2, half, 2, VL)

    mine = lambda array: lax.dynamic_slice_in_dim(array, device * slots, slots)
    my_slots = mine(slot_band)
    my_index = jnp.maximum(my_slots, 0)
    my_remain = mine(starts) % BL
    my_width = lookup(band_width, my_index).astype(jnp.float32)
    my_gain = lookup(band_gain, my_index)
    all_residue = (base * np.array([1, -1])[None, :, None]) % RAD
    step = np.stack([np.arange(VL), VL - 1 - np.arange(VL)])
    place = step[None, :, None, :] * RAD + all_residue[..., None]
    place = jnp.asarray(place.astype(np.int32))[:, None, :, :, None]
    pairs = lambda array: array.reshape(1, slots // 2, 1, 1, 2, 1)
    position = ((place - pairs(my_remain)) % BL).astype(jnp.float32)
    wide = pairs(my_width)
    taper_gain = jnp.where(
        position < wide, 0.5 - 0.5 * jnp.cos(two_pi * (position + 0.5) / wide), 0.0
    )
    tapered = incoming * taper_gain
    angle = np.stack([grid(step[0], np.arange(VL), VL), grid(step[1], np.arange(VL), VL)])
    part_real = dot("fphibv,hvt->pbfhit", tapered, const(np.cos(angle)))
    part_imag = dot("fphibv,hvt->pbfhit", tapered, const(-np.sin(angle)))
    angle = grid(all_residue.reshape(-1), np.arange(VL), BL).reshape(base.shape + (VL,))
    twist_cos, twist_sin = const(np.cos(angle)), const(np.sin(angle))
    turned_real = (part_real * twist_cos + part_imag * twist_sin).reshape(slots, RAD, VL)
    turned_imag = (part_imag * twist_cos - part_real * twist_sin).reshape(slots, RAD, VL)
    stacked = jnp.concatenate([turned_real, turned_imag], axis=1)
    angle = grid(span, all_residue.reshape(-1), RAD)
    cos_m, sin_m = np.cos(angle), np.sin(angle)
    real = dot("ur,srt->sut", const(np.concatenate([cos_m, sin_m], axis=1)), stacked)
    imag = dot("ur,srt->sut", const(np.concatenate([-sin_m, cos_m], axis=1)), stacked)
    when = jnp.arange(BL, dtype=jnp.int32).reshape(RAD, VL)
    phase = (my_remain[:, None, None] * when[None] % BL).astype(jnp.float32) * (two_pi / BL)
    phase_cos, phase_sin = jnp.cos(phase), jnp.sin(phase)
    result = real * (phase_cos - phase_sin) - imag * (phase_sin + phase_cos)
    scale = jnp.where(my_slots >= 0, my_gain / jnp.sqrt(my_width), 0.0)
    return (result * scale[:, None, None]).reshape(slots, BL)


def solution(mesh):
    return jax.shard_map(
        body,
        mesh=mesh,
        in_specs=(P(AXES), P(), P(), P(), P()),
        out_specs=P(AXES, None),
        check_vma=False,
    )
```

time: 174 us -> 114 us (0.66)
  local copies, waits for them, and re-layouts: 74.2 us -> 10.5 us
  Pallas kernels: 0 us -> 7.21 us
  matrix products: 16.9 us -> 9.93 us
  other arithmetic: 6.04 us -> 9.46 us
    reshape x3 -> x1, local copies, waits for them, and re-layouts: 23.6 us -> 0.32 us  [body(): incoming = incoming.reshape(devices, slots // 2, 2, half, 2, VL)]
    gather x1 -> x0, local copies, waits for them, and re-layouts: 21.9 us -> none  [body(): take = lambda part, at: lax.dynamic_slice(part, (at, 0), (VL + 1, half))]
    unnamed x56 -> x43, local copies, waits for them, and re-layouts: 9.71 us -> 0.31 us
    slice x3 -> x0, local copies, waits for them, and re-layouts: 8.77 us -> none  [the longest x1 7.72 us: body(): window[0, :, 1:VL]]
    pallas_call x0 -> x1, Pallas kernels: none -> 7.21 us  [combine(): pl.pallas_call(lambda *refs: combine_kernel(own, half, total, *refs), out...]
    mul x1, other arithmetic: 2.2 us -> 8.36 us  [body(): tapered = incoming * taper_gain]
    dot_general x9 -> x7, matrix products: 14.4 us -> 9.93 us  [dot(): return jnp.einsum(spec, left, right, precision=lax.Precision.HIGH)]
    dot_general x2 -> x0, matrix products: 2.5 us -> none  [the longest x1 1.27 us: body(): jnp.einsum('cq,qr->cr', value[:, 0, 0], const(swap0), precision=lax.Preci...]
where the time goes in v2:
time: 114 us; the launch traced here: 113 us
  waiting for transfers between devices  35.3 us (31%)
  blocking collectives  34.7 us (30%)
  local copies, waits for them, and re-layouts  10.5 us (9%)
  matrix products  9.93 us (9%)
  other arithmetic  9.46 us (8%)
  Pallas kernels  7.21 us (6%)
  starting transfers between devices  5.67 us (5%)
    all_to_all x2, waiting for transfers between devices, exchange(): return lax.all_to_all(blocks, AXES, split_axis=0, concat_axis=0, tiled=True)  35.3 us
    all_to_all x1, blocking collectives, exchange(): return lax.all_to_all(blocks, AXES, split_axis=0, concat_axis=0, tiled=True)  34.7 us
    dot_general x7, matrix products, dot(): return jnp.einsum(spec, left, right, precision=lax.Precision.HIGH)  9.93 us
    mul x1, other arithmetic, body(): tapered = incoming * taper_gain  8.36 us
    pallas_call x1, Pallas kernels, combine(): pl.pallas_call(lambda *refs: combine_kernel(own, half, total, *refs), out...  7.21 us
    all_to_all x2, starting transfers between devices, exchange(): return lax.all_to_all(blocks, AXES, split_axis=0, concat_axis=0, tiled=True)  5.67 us
  transfers between devices with their start and end apart: 2, of which 2 were waited for; matrix products, arithmetic and copies ran while one was open for 2% of the time, Pallas kernels for 0%

profile of v2, /device:TPU:0, one launch (start us, length us, event | category | flops | bytes accessed | tf_op | source)
XLA Modules:
  0.0 113.2 jit_solution(12431052049938286697)
XLA Ops:
  0.0 1.6 %copy.69 = f32[128,2048]{1,0:T(8,128)S(1)} copy(f32[128,2048]{0,1:T(8,128)} %bitcast.73) | data formatting | bytes 2097152 | tf_op jit(solution)/shard_map/transpose | solution.py:201
  1.9 34.7 %all_to_all.15 = f32[32,4,2048]{2,1,0:T(4,128)S(1)} all-to-all(f32[32,4,2048]{2,1,0:T(4,128)S(1)} %reshape.219), channel_id=1, replica_groups=mesh['tx'=4,'ty'=8] {'tx','ty'}, dimensions={0} | all-to-all | bytes 2097152 | tf_op jit(solution)/shard_map/all_to_all | solution.py:32
  36.6 0.5 reshape.236
  37.1 1.0 fusion.9
  38.2 1.2 %add_bitcast_fusion = (f32[4,256,256]{1,2,0:T(8,128)S(1)}, f32[4,256,256]{1,2,0:T(8,128)S(1)}) fusion(f32[256,4,256]{0,2,1:T(8,128)S(1)} %fusion.9, f32[256,256]{0,1:T(8,128)S(1)} %copy-done.5, f32[256,256]{0,1:T(8,128)S(1)} %copy-done.6, f32[256,256,1]{1,0,2:T(8,128)S(1)} %copy-done.7, f32[32,4,8,256]{3,2,1,0:T(8,128)S(1)} %reshape.236), kind=kOutput, calls=%fused_computation.19 | convolution fusion | flops 404226048 | bytes 4980736 | tf_op jit(solution)/shard_map/rp,cpz->crz/dot_general | solution.py:28
  39.5 2.0 %copy.73 = f32[4,256,512]{2,0,1:T(4,128)} copy(f32[4,256,512]{1,2,0:T(8,128)S(1)} %pad_maximum_fusion) | data formatting | bytes 4194304 | tf_op jit(solution)/shard_map/concatenate | solution.py:212
  41.5 3.7 %fusion.2 = f32[32,2,4,4,256]{4,0,3,2,1:T(8,128)S(1)} fusion(f32[2,512,256,1,1]{2,1,4,3,0:T(8,128)S(1)} %copy-done.3, f32[4,32,2,4,512]{4,0,3,2,1:T(4,128)} %bitcast.69), kind=kOutput, calls=%fused_computation.3 | convolution fusion | flops 805306368 | bytes 4194304 | tf_op jit(solution)/shard_map/cfhiz,hzq->fhciq/dot_general | solution.py:28
  45.3 1.7 %copy.75 = f32[32,2,4,4,256]{4,3,2,1,0:T(4,128)} copy(f32[32,2,4,4,256]{4,0,3,2,1:T(8,128)S(1)} %fusion.2) | data formatting | bytes 2097152 | tf_op jit(solution)/shard_map/cfhiz,hzq->fhciq/transpose | solution.py:28
  47.0 2.8 %all-to-all-start.1 = ((f32[32,2,4,4,256]{4,3,2,1,0:T(4,128)}), f32[32,2,4,4,256]{4,3,2,1,0:T(4,128)S(1)}, u32[]{:S(2)}, u32[]{:S(2)}) async-start(f32[32,2,4,4,256]{4,3,2,1,0:T(4,128)} %copy.75), calls=%async_computation.1 | async-start | bytes 2097152 | tf_op jit(solution)/shard_map/all_to_all | solution.py:32
  49.7 0.7 dynamic-slice_bitcast_fusion.1
  51.2 0.7 dynamic-slice_bitcast_fusion.refs_7_
  52.0 25.3 %all-to-all-done.1 = f32[32,2,4,4,256]{4,3,2,1,0:T(4,128)S(1)} async-done(((f32[32,2,4,4,256]{4,3,2,1,0:T(4,128)}), f32[32,2,4,4,256]{4,3,2,1,0:T(4,128)S(1)}, u32[]{:S(2)}, u32[]{:S(2)}) %all-to-all-start.1) | async-done | bytes 1048608 | tf_op jit(solution)/shard_map/all_to_all | solution.py:32
  77.6 7.2 %combine.1 = f32[64,8,128]{2,1,0:T(8,128)} custom-call(s32[1]{0:T(128)} %bitcast.refs_0_, s32[128]{0:T(128)S(1)} %select_reduce_fusion.refs_1_, f32[256,1024]{1,0:T(8,128)S(1)} %bitcast.68, f32[2,256,256]{2,1,0:T(8,128)S(1)} %copy-done, f32[2,256,5]{2,1,0:T(8,128)S(1)} %copy.76.refs_4_, bf16[2,256,256]{2,1,0:T(8,128)(2,1)S(1)} %copy-done.1, ...), custom_call_target="tpu_custom_call" | custom-call | tf_op jit(solution)/shard_map/combine/pallas_call | solution.py:175
  84.8 2.9 %all-to-all-start.2 = ((f32[32,2,8,128]{3,2,1,0:T(8,128)}), f32[32,2,8,128]{3,2,1,0:T(8,128)S(1)}, u32[]{:S(2)}, u32[]{:S(2)}) async-start(f32[32,2,8,128]{3,2,1,0:T(8,128)} %bitcast.16), calls=%async_computation.2 | async-start | bytes 524288 | tf_op jit(solution)/shard_map/all_to_all | solution.py:32
  88.2 10.0 %all-to-all-done.2 = f32[32,2,8,128]{3,2,1,0:T(8,128)S(1)} async-done(((f32[32,2,8,128]{3,2,1,0:T(8,128)}), f32[32,2,8,128]{3,2,1,0:T(8,128)S(1)}, u32[]{:S(2)}, u32[]{:S(2)}) %all-to-all-start.2) | async-done | bytes 262176 | tf_op jit(solution)/shard_map/all_to_all | solution.py:32
  98.2 0.3 reshape.225
  98.5 8.4 %fusion.17 = f32[32,2,2,4,2,64]{5,4,3,2,1,0:T(2,128)S(1)} fusion(f32[32,2,2,4,2,64]{5,4,3,2,1,0:T(2,128)S(1)} %reshape.225, f32[2,2]{1,0:T(2,128)S(1)} %convert_element_type.33, s32[2,2]{1,0:T(2,128)S(1)} %sub.32, s32[32,2,4,64]{3,2,1,0:T(4,128)S(1)} %copy-done.10), kind=kLoop, calls=%fused_computation.27 | loop fusion | flops 1376256 | bytes 589856 | tf_op jit(solution)/shard_map/mul | solution.py:244
  106.9 0.6 convolution_bitcast_fusion.1
  107.6 0.7 multiply_add_fusion
  108.3 0.3 copy.80
  108.9 0.3 copy.79
  109.4 1.3 %fusion.5 = f32[4,256,64]{1,2,0:T(8,128)S(1)} fusion(f32[256,512,1]{1,0,2:T(8,128)S(1)} %copy-done.20, f32[4,256,64]{1,2,0:T(8,128)S(1)} %copy.82, f32[4,256,64]{1,2,0:T(8,128)S(1)} %copy.81, s32[256,64]{0,1:T(8,128)S(1)} %multiply_add_fusion.1, s32[4]{0:T(128)S(1)} %and_select_fusion.1), kind=kOutput, calls=%fused_computation.8 | convolution fusion | flops 202506240 | bytes 1376272 | tf_op jit(solution)/shard_map/ur,srt->sut/dot_general | solution.py:28
  110.7 1.3 %fusion.8 = f32[4,256,64]{1,2,0:T(8,128)S(1)} fusion(f32[4,256,64]{1,2,0:T(8,128)S(1)} %fusion.5, f32[256,512,1]{1,0,2:T(8,128)S(1)} %copy-done.19, f32[4,256,64]{1,2,0:T(8,128)S(1)} %copy.82, f32[4,256,64]{1,2,0:T(8,128)S(1)} %copy.81, f32[4]{0:T(128)S(1)} %compare_select_fusion.5, s32[256,64]{0,1:T(8,128)S(1)} %multiply_add_fusion.1, ...), kind=kOutput, calls=%fused_computation.11 | convolution fusion | flops 202637312 | bytes 1638432 | tf_op jit(solution)/shard_map/ur,srt->sut/dot_general | solution.py:28
  112.3 0.9 reshape.228
  (62 shorter events, 2.6 us)
Async XLA Ops:
  1.9 35.3 %copy-start.4 = (f32[256,256,1]{1,0,2:T(8,128)S(1)}, f32[256,256,1]{1,0,2:T(8,128)}, u32[]{:S(2)}) copy-start(f32[256,256,1]{1,0,2:T(8,128)} %constant.129) | copy-start | bytes 786436
  36.6 1.6 %copy-start.5 = (f32[256,256]{0,1:T(8,128)S(1)}, f32[256,256]{0,1:T(8,128)}, u32[]{:S(2)}) copy-start(f32[256,256]{0,1:T(8,128)} %constant.110.clone) | copy-start | bytes 786436
  36.6 1.6 %copy-start.6 = (f32[256,256]{0,1:T(8,128)S(1)}, f32[256,256]{0,1:T(8,128)}, u32[]{:S(2)}) copy-start(f32[256,256]{0,1:T(8,128)} %constant.109.clone) | copy-start | bytes 786436
  36.6 1.6 %copy-start.7 = (f32[256,256,1]{1,0,2:T(8,128)S(1)}, f32[256,256,1]{1,0,2:T(8,128)}, u32[]{:S(2)}) copy-start(f32[256,256,1]{1,0,2:T(8,128)} %constant.128) | copy-start | bytes 786436
  39.5 2.0 %copy-start.3 = (f32[2,512,256,1,1]{2,1,4,3,0:T(8,128)S(1)}, f32[2,512,256,1,1]{2,1,4,3,0:T(8,128)}, u32[]{:S(2)}) copy-start(f32[2,512,256,1,1]{2,1,4,3,0:T(8,128)} %constant.130) | copy-start | bytes 3145732
  45.2 5.2 %copy-start.13 = (s32[256]{0:T(256)S(1)}, s32[256]{0:T(256)}, u32[]{:S(2)}) copy-start(s32[256]{0:T(256)} %constant.126) | copy-start | bytes 3076
  45.2 5.2 %copy-start.14 = (f32[256]{0:T(256)S(1)}, f32[256]{0:T(256)}, u32[]{:S(2)}) copy-start(f32[256]{0:T(256)} %constant.127) | copy-start | bytes 3076
  45.3 5.6 %copy-start.15 = (s32[128]{0:T(128)S(1)}, s32[128]{0:T(128)}, u32[]{:S(2)}) copy-start(s32[128]{0:T(128)} %param.28) | copy-start | bytes 1540
  45.3 5.7 %copy-start.16 = (s32[64]{0:T(128)S(1)}, s32[64]{0:T(128)}, u32[]{:S(2)}) copy-start(s32[64]{0:T(128)} %param.26) | copy-start | bytes 772
  45.3 6.6 %copy-start.17 = (s32[64]{0:T(128)S(1)}, s32[64]{0:T(128)}, u32[]{:S(2)}) copy-start(s32[64]{0:T(128)} %param.25) | copy-start | bytes 772
  46.9 30.6 %copy-start = (f32[2,256,256]{2,1,0:T(8,128)S(1)}, f32[2,256,256]{2,1,0:T(8,128)}, u32[]{:S(2)}) copy-start(f32[2,256,256]{2,1,0:T(8,128)} %constant.116.clone.refs_3_) | copy-start | bytes 1572868
  46.9 30.6 %copy-start.1 = (bf16[2,256,256]{2,1,0:T(8,128)(2,1)S(1)}, bf16[2,256,256]{2,1,0:T(8,128)(2,1)}, u32[]{:S(2)}) copy-start(bf16[2,256,256]{2,1,0:T(8,128)(2,1)} %constant.117.clone.refs_5_) | copy-start | bytes 786436
  46.9 30.6 %copy-start.2 = (bf16[2,256,256]{2,1,0:T(8,128)(2,1)S(1)}, bf16[2,256,256]{2,1,0:T(8,128)(2,1)}, u32[]{:S(2)}) copy-start(bf16[2,256,256]{2,1,0:T(8,128)(2,1)} %constant.118.clone.refs_6_) | copy-start | bytes 786436
  47.0 30.4 %all-to-all-start.1 = ((f32[32,2,4,4,256]{4,3,2,1,0:T(4,128)}), f32[32,2,4,4,256]{4,3,2,1,0:T(4,128)S(1)}, u32[]{:S(2)}, u32[]{:S(2)}) async-start(f32[32,2,4,4,256]{4,3,2,1,0:T(4,128)} %copy.75), calls=%async_computation.1 | async-start | bytes 2097152 | tf_op jit(solution)/shard_map/all_to_all | solution.py:32
  77.5 10.4 %copy-start.18 = (f32[64]{0:T(128)S(1)}, f32[64]{0:T(128)}, u32[]{:S(2)}) copy-start(f32[64]{0:T(128)} %param.27) | copy-start | bytes 772
  77.5 21.0 %copy-start.10 = (s32[32,2,4,64]{3,2,1,0:T(4,128)S(1)}, s32[32,2,4,64]{3,2,1,0:T(4,128)}, u32[]{:S(2)}) copy-start(s32[32,2,4,64]{3,2,1,0:T(4,128)} %constant.119.clone) | copy-start | bytes 196612
  77.6 29.3 %copy-start.12 = (f32[2,64,64,1,1,1]{2,1,5,4,3,0:T(8,128)S(1)}, f32[2,64,64,1,1,1]{2,1,5,4,3,0:T(8,128)}, u32[]{:S(2)}) copy-start(f32[2,64,64,1,1,1]{2,1,5,4,3,0:T(8,128)} %constant.131) | copy-start | bytes 98308
  84.8 22.7 %copy-start.8 = (f32[32,2,4,64]{3,0,2,1:T(8,128)S(1)}, f32[32,2,4,64]{3,0,2,1:T(8,128)}, u32[]{:S(2)}) copy-start(f32[32,2,4,64]{3,0,2,1:T(8,128)} %constant.123.clone) | copy-start | bytes 196612
  84.8 22.7 %copy-start.9 = (f32[32,2,4,64]{3,0,2,1:T(8,128)S(1)}, f32[32,2,4,64]{3,0,2,1:T(8,128)}, u32[]{:S(2)}) copy-start(f32[32,2,4,64]{3,0,2,1:T(8,128)} %constant.122.clone) | copy-start | bytes 196612
  84.8 22.8 %copy-start.11 = (f32[2,64,64,1,1,1]{2,1,5,4,3,0:T(8,128)S(1)}, f32[2,64,64,1,1,1]{2,1,5,4,3,0:T(8,128)}, u32[]{:S(2)}) copy-start(f32[2,64,64,1,1,1]{2,1,5,4,3,0:T(8,128)} %constant.132) | copy-start | bytes 98308
  84.8 13.4 %all-to-all-start.2 = ((f32[32,2,8,128]{3,2,1,0:T(8,128)}), f32[32,2,8,128]{3,2,1,0:T(8,128)S(1)}, u32[]{:S(2)}, u32[]{:S(2)}) async-start(f32[32,2,8,128]{3,2,1,0:T(8,128)} %bitcast.16), calls=%async_computation.2 | async-start | bytes 524288 | tf_op jit(solution)/shard_map/all_to_all | solution.py:32
  108.3 1.1 copy-start.20
  108.7 2.1 %copy-start.19 = (f32[256,512,1]{1,0,2:T(8,128)S(1)}, f32[256,512,1]{1,0,2:T(8,128)}, u32[]{:S(2)}) copy-start(f32[256,512,1]{1,0,2:T(8,128)} %constant.134) | copy-start | bytes 1572868

commit v3 on v2

--- a/solution.py
+++ b/solution.py
@@ -26,10 +26,6 @@
 
 def dot(spec, left, right):
     return jnp.einsum(spec, left, right, precision=lax.Precision.HIGH)
-
-
-def exchange(blocks):
-    return lax.all_to_all(blocks, AXES, split_axis=0, concat_axis=0, tiled=True)
 
 
 def lookup(values_table, positions):
@@ -66,14 +62,110 @@
     return one(left_high, right_high) + (one(left_high, right_low) + one(left_low, right_high))
 
 
+def meet(size_x, size_y, send_sem, recv_sem):
+    devices = size_x * size_y
+    me = lax.axis_index("tx") * size_y + lax.axis_index("ty")
+    barrier = pltpu.get_barrier_semaphore()
+
+    def greet(j, carry):
+        to = lax.rem(me + j, devices)
+        pl.semaphore_signal(
+            barrier, inc=1, device_id=(to // size_y, lax.rem(to, size_y)), device_id_type=pl.DeviceIdType.MESH
+        )
+        return carry
+
+    lax.fori_loop(1, devices, greet, 0)
+    pl.semaphore_wait(barrier, devices - 1)
+
+    def send(stage, source, target, to):
+        pltpu.make_async_remote_copy(
+            src_ref=source, dst_ref=target, send_sem=send_sem.at[stage], recv_sem=recv_sem.at[stage],
+            device_id=(to // size_y, lax.rem(to, size_y)), device_id_type=pl.DeviceIdType.MESH,
+        ).start()
+
+    def wait(ref, sem):
+        pltpu.make_async_copy(ref, ref, sem).wait()
+
+    return devices, me, send, wait
+
+
+def transform_kernel(
+    size_x, size_y, own, half,
+    turned_ref, first_ref, twist_ref, second_ref,
+    value_ref, column_ref, high_ref, low_ref, pass_ref, send_sem, recv_sem,
+):
+    devices, me, send, wait = meet(size_x, size_y, send_sem, recv_sem)
+    others = devices - 1
+    high_rows = 2 * own
+    span = 2 * half * high_rows
+
+    def send_columns(j, carry):
+        to = lax.rem(me + j, devices)
+        send(0, turned_ref.at[to], column_ref.at[me], to)
+        return carry
+
+    lax.fori_loop(1, devices, send_columns, 0)
+    column_ref[me] = turned_ref[me]
+    wait(column_ref.at[pl.ds(0, others)], recv_sem.at[0])
+    for c in range(own):
+        high, low = split(column_ref[:, c].reshape(RAD, RAD))
+        high_ref[:, c * RAD : (c + 1) * RAD] = high
+        low_ref[:, c * RAD : (c + 1) * RAD] = low
+
+    group = first_ref.shape[0]
+    height = half * 8
+
+    def transform(b, carry):
+        at = lax.rem(b + me // 8, group)
+        section = product((first_ref[at, 0], first_ref[at, 1]), (high_ref[...], low_ref[...]))
+        twist_cos, twist_sin = twist_ref[at, 0], twist_ref[at, 1]
+        turned = []
+        for c in range(own):
+            real = section[: 2 * height, c * RAD : (c + 1) * RAD]
+            imag = section[2 * height :, c * RAD : (c + 1) * RAD]
+            turned.append(
+                jnp.concatenate([real * twist_cos + imag * twist_sin, imag * twist_cos - real * twist_sin], axis=1)
+            )
+        for h in range(2):
+            left = jnp.concatenate([part[h * height : (h + 1) * height] for part in turned], axis=0)
+            bins = product(split(left), (second_ref[0, h], second_ref[1, h]))
+            for c in range(own):
+                for i in range(half):
+                    row = c * height + i * 8
+                    for side in range(2):
+                        tile = (2 * i + side) * high_rows
+                        pass_ref[pl.ds(at * 8 * span + tile + h * own + c, 8, stride=span), :] = bins[
+                            row : row + 8, side * 128 : side * 128 + 128
+                        ]
+        for j in range(8):
+            to = at * 8 + lax.rem(me + j, 8)
+
+            @pl.when(to != me)
+            def _():
+                part = lambda ref, k: ref.at[pl.ds(pl.multiple_of(k * span, span), span)]
+                send(1, part(pass_ref, to), part(value_ref, me), to)
+
+        return carry
+
+    lax.fori_loop(0, group, transform, 0)
+    mine = pl.ds(pl.multiple_of(me * span, span), span)
+    value_ref[mine, :] = pass_ref[mine, :]
+    wait(value_ref.at[pl.ds(0, others * span)], recv_sem.at[1])
+
+    wait(turned_ref.at[pl.ds(0, others)], send_sem.at[0])
+    wait(pass_ref.at[pl.ds(0, others * span)], send_sem.at[1])
+
+
 def combine_kernel(
-    own, half, total, device_ref, start_ref, value_ref, alpha_ref, beta_ref, mix_ref, swap_ref, residue_ref,
-    out_ref, table_ref,
+    devices, own, half, total,
+    device_ref, start_ref, value_ref, alpha_ref, beta_ref, mix_ref, swap_ref, residue_ref,
+    leave_ref, table_ref,
 ):
     rows = total // RAD
-    count = value_ref.shape[0]
+    count = alpha_ref.shape[1]
     cols = count // 2
-    tiles = rows // (2 * VL)
+    high_rows = 2 * own
+
     is_upper = lax.broadcasted_iota(jnp.int32, (count, RAD), 0) // own % 2 == 1
 
     def exchange_rows(block):
@@ -88,19 +180,23 @@
 
     mix = mix_ref[0], mix_ref[1]
 
+    def values(i):
+        part = value_ref[...].reshape(devices, 2 * half, high_rows, 128)
+        return jnp.concatenate([part[:, 2 * i + side].reshape(count, 128) for side in range(2)], axis=1)
+
     def put(result, h, i):
         for side in range(2):
             at = pl.ds(8 * side + h * half + i, cols, stride=16)
             table_ref[at, :] = result[:, side * 128 : (side + 1) * 128]
 
     for i in range(half):
-        result = product(mix, split(twist(value_ref[:, i * RAD : (i + 1) * RAD], i)))
+        result = product(mix, split(twist(values(i), i)))
         for h in range(2):
             put(result[h * cols : (h + 1) * cols], h, i)
 
     @pl.when(device_ref[0] == 0)
     def _():
-        block = value_ref[:, :RAD]
+        block = values(0)
         high, low = split(block)
         for h in range(2):
             turn = lambda part: jnp.dot(part, swap_ref[h], preferred_element_type=jnp.float32)
@@ -132,17 +228,37 @@
         picked = jnp.where((place >= 0) & (place < BL), picked, 0.0)
         return picked + pltpu.roll(picked, VL, 1)
 
-    def step(pair, carry):
-        out_ref[pair] = jnp.where(is_low, window(2 * pair), window(2 * pair + 1))
+    pairs = leave_ref.shape[1]
+
+    def step(to, carry):
+        for k in range(pairs):
+            slot = 2 * (to * pairs + k)
+            leave_ref[to, k] = jnp.where(is_low, window(slot), window(slot + 1))
         return carry
 
-    lax.fori_loop(0, out_ref.shape[0], step, 0, unroll=4)
-
-
-def combine(value, starts, device, base, own, total):
+    lax.fori_loop(0, devices, step, 0, unroll=2)
+
+
+def deliver_kernel(size_x, size_y, leave_ref, out_ref, send_sem, recv_sem):
+    devices, me, send, wait = meet(size_x, size_y, send_sem, recv_sem)
+
+    def step(j, carry):
+        to = lax.rem(me + j, devices)
+        send(0, leave_ref.at[to], out_ref.at[me], to)
+        return carry
+
+    lax.fori_loop(1, devices, step, 0)
+    out_ref[me] = leave_ref[me]
+    wait(leave_ref.at[pl.ds(0, devices - 1)], send_sem.at[0])
+    wait(out_ref.at[pl.ds(0, devices - 1)], recv_sem.at[0])
+
+
+def spectrum(turned, starts, device, base, total):
+    size_x, size_y = lax.axis_size("tx"), lax.axis_size("ty")
     devices, _, half = base.shape
-    count = value.shape[0]
-    cols = count // 2
+    own = turned.shape[1]
+    cols = devices * own
+    count = 2 * cols
     span = np.arange(RAD)
     col = np.arange(cols)
     sign = np.array([1.0, -1.0])[None, :, None]
@@ -169,21 +285,60 @@
     residue = ((base * np.array([1, -1])[None, :, None]) % RAD).reshape(devices, 2 * half, 1)
     residue = jnp.asarray(np.broadcast_to(residue, (devices, 2 * half, 128)).astype(np.int32))
     residue = lax.dynamic_index_in_dim(residue, device, 0, keepdims=False)
+    order = base.reshape(devices // 8, 8, 2, half).transpose(0, 2, 3, 1).reshape(devices // 8, -1)
+    angle = grid(order.reshape(-1), span, RAD).reshape(order.shape + (RAD,))
+    first = np.concatenate([np.cos(angle), -np.sin(angle)], axis=1)
+    angle = grid(order.reshape(-1), span, RAD * RAD).reshape(order.shape + (RAD,))
+    twist = np.stack([np.cos(angle), np.sin(angle)], axis=1)
+    angle = grid(span, span, RAD)
+    cos_m, sin_m = np.cos(angle), np.sin(angle)
+    minus = np.concatenate([cos_m + sin_m, sin_m - cos_m], axis=0)
+    plus = np.concatenate([cos_m - sin_m, cos_m + sin_m], axis=0)
+    second = np.stack([minus, plus]) / math.sqrt(total)
     smem = pl.BlockSpec(memory_space=pltpu.SMEM)
     vmem = pl.BlockSpec(memory_space=pltpu.VMEM)
     rows = total // RAD
-    return pl.pallas_call(
-        lambda *refs: combine_kernel(own, half, total, *refs),
-        out_shape=jax.ShapeDtypeStruct((starts.shape[0] // 2, 2 * half, 128), jnp.float32),
+    pairs = starts.shape[0] // (2 * devices)
+    shape = (devices, pairs, 2 * half, 128)
+    f32, bf16 = jnp.float32, jnp.bfloat16
+    sems = lambda n: [pltpu.SemaphoreType.DMA((n,)), pltpu.SemaphoreType.DMA((n,))]
+    limit = 48 * 1024 * 1024
+    remote = lambda k: pltpu.CompilerParams(vmem_limit_bytes=limit, collective_id=k, has_side_effects=True)
+    value = pl.pallas_call(
+        lambda *refs: transform_kernel(size_x, size_y, own, half, *refs),
+        out_shape=jax.ShapeDtypeStruct((count * half * 2, 128), f32),
+        in_specs=[vmem] * 4,
+        out_specs=vmem,
+        scratch_shapes=[
+            pltpu.VMEM(turned.shape, f32),
+            pltpu.VMEM((RAD, own * RAD), bf16),
+            pltpu.VMEM((RAD, own * RAD), bf16),
+            pltpu.VMEM((count * half * 2, 128), f32),
+        ] + sems(2),
+        compiler_params=remote(0),
+        name="transform",
+    )(turned, const_split(first).swapaxes(0, 1), const(twist), const_split(second))
+    leaving = pl.pallas_call(
+        lambda *refs: combine_kernel(devices, own, half, total, *refs),
+        out_shape=jax.ShapeDtypeStruct(shape, f32),
         in_specs=[smem, smem] + [vmem] * 6,
         out_specs=vmem,
-        scratch_shapes=[pltpu.VMEM((rows // 16, 128), jnp.float32)],
-        compiler_params=pltpu.CompilerParams(vmem_limit_bytes=48 * 1024 * 1024),
+        scratch_shapes=[pltpu.VMEM((rows // 16, 128), f32)],
+        compiler_params=pltpu.CompilerParams(vmem_limit_bytes=limit),
         name="combine",
     )(
-        device.reshape(1).astype(jnp.int32), starts, value, const(alpha), beta, const_split(mix),
-        jnp.asarray(swap.astype(np.float32).astype(jnp.bfloat16)), residue,
+        device.reshape(1).astype(jnp.int32), starts, value, const(alpha), beta,
+        const_split(mix), jnp.asarray(swap.astype(np.float32).astype(jnp.bfloat16)), residue,
     )
+    return pl.pallas_call(
+        lambda *refs: deliver_kernel(size_x, size_y, *refs),
+        out_shape=jax.ShapeDtypeStruct(shape, f32),
+        in_specs=[vmem],
+        out_specs=vmem,
+        scratch_shapes=sems(1),
+        compiler_params=remote(1),
+        name="deliver",
+    )(leaving)
 
 
 def body(signal, band_start, band_width, band_gain, slot_band):
@@ -196,34 +351,13 @@
     chunk = length // cols
     base = row_bases(devices)
     half = base.shape[2]
-    span = np.arange(RAD)
-
-    turned = signal.reshape(chunk, cols).T.reshape(devices, own, chunk)
-    column = exchange(turned)
-    column = column.reshape(devices, own, chunk // RAD, RAD).transpose(1, 0, 2, 3).reshape(own, RAD, RAD)
-
-    angle = grid(base.reshape(-1), span, RAD)
-    section_real = dot("rp,cpz->crz", const(np.cos(angle)), column)
-    section_imag = dot("rp,cpz->crz", const(-np.sin(angle)), column)
-    angle = grid(base.reshape(-1), span, RAD * RAD)
-    twist_cos, twist_sin = const(np.cos(angle)), const(np.sin(angle))
-    turned_real = section_real * twist_cos + section_imag * twist_sin
-    turned_imag = section_imag * twist_cos - section_real * twist_sin
-    both = jnp.concatenate([turned_real, turned_imag], axis=2).reshape(own, devices, 2, half, 2 * RAD)
-    angle = grid(span, span, RAD)
-    cos_m, sin_m = np.cos(angle), np.sin(angle)
-    minus = np.concatenate([cos_m + sin_m, sin_m - cos_m], axis=0)
-    plus = np.concatenate([cos_m - sin_m, cos_m + sin_m], axis=0)
-    bins = dot("cfhiz,hzq->fhciq", both, const(np.stack([minus, plus]) / math.sqrt(total)))
-
-    value = exchange(bins).reshape(2 * cols, half * RAD)
-
+
+    turned = signal.reshape(chunk // RAD, RAD, cols).transpose(2, 0, 1)
+    turned = turned.reshape(devices, own, chunk // RAD, RAD)
     slot_index = jnp.maximum(slot_band, 0)
     starts = lookup(band_start, slot_index)
-    outgoing = combine(value, starts, device, base, own, total)
+    incoming = spectrum(turned, starts, device, base, total)
     slots = slot_band.shape[0] // devices
-    incoming = exchange(outgoing.reshape(devices, slots // 2, 2 * half, 2 * VL))
-    incoming = incoming.reshape(devices, slots // 2, 2, half, 2, VL)
 
     mine = lambda array: lax.dynamic_slice_in_dim(array, device * slots, slots)
     my_slots = mine(slot_band)
@@ -232,34 +366,39 @@
     my_width = lookup(band_width, my_index).astype(jnp.float32)
     my_gain = lookup(band_gain, my_index)
     all_residue = (base * np.array([1, -1])[None, :, None]) % RAD
-    step = np.stack([np.arange(VL), VL - 1 - np.arange(VL)])
+    lane = np.arange(VL)
+    step = np.stack([lane, VL - 1 - lane])
     place = step[None, :, None, :] * RAD + all_residue[..., None]
-    place = jnp.asarray(place.astype(np.int32))[:, None, :, :, None]
-    pairs = lambda array: array.reshape(1, slots // 2, 1, 1, 2, 1)
-    position = ((place - pairs(my_remain)) % BL).astype(jnp.float32)
-    wide = pairs(my_width)
+    place = np.tile(place.reshape(devices, 1, 2 * half, VL), (1, 1, 1, 2))
+    lanes = lambda array: jnp.repeat(array.reshape(1, slots // 2, 1, 2), VL, axis=3)
+    position = ((jnp.asarray(place.astype(np.int32)) - lanes(my_remain)) % BL).astype(jnp.float32)
+    wide = lanes(my_width)
     taper_gain = jnp.where(
         position < wide, 0.5 - 0.5 * jnp.cos(two_pi * (position + 0.5) / wide), 0.0
     )
-    tapered = incoming * taper_gain
-    angle = np.stack([grid(step[0], np.arange(VL), VL), grid(step[1], np.arange(VL), VL)])
-    part_real = dot("fphibv,hvt->pbfhit", tapered, const(np.cos(angle)))
-    part_imag = dot("fphibv,hvt->pbfhit", tapered, const(-np.sin(angle)))
-    angle = grid(all_residue.reshape(-1), np.arange(VL), BL).reshape(base.shape + (VL,))
+    tapered = (incoming * taper_gain).reshape(devices, slots // 2, 2, half, 2 * VL)
+    angle = np.stack([grid(step[0], lane, VL), grid(step[1], lane, VL)])
+    twice = lambda array: np.einsum("bd,hvt->hbvdt", np.eye(2), array).reshape(2, 2 * VL, 2 * VL)
+    part_real = dot("fphiv,hvt->pfhit", tapered, const(twice(np.cos(angle))))
+    part_imag = dot("fphiv,hvt->pfhit", tapered, const(twice(-np.sin(angle))))
+    angle = np.tile(grid(all_residue.reshape(-1), lane, BL).reshape(base.shape + (VL,)), (1, 1, 1, 2))
     twist_cos, twist_sin = const(np.cos(angle)), const(np.sin(angle))
-    turned_real = (part_real * twist_cos + part_imag * twist_sin).reshape(slots, RAD, VL)
-    turned_imag = (part_imag * twist_cos - part_real * twist_sin).reshape(slots, RAD, VL)
+    flat = lambda array: array.reshape(slots // 2, RAD, 2 * VL)
+    turned_real = flat(part_real * twist_cos + part_imag * twist_sin)
+    turned_imag = flat(part_imag * twist_cos - part_real * twist_sin)
     stacked = jnp.concatenate([turned_real, turned_imag], axis=1)
-    angle = grid(span, all_residue.reshape(-1), RAD)
+    angle = grid(np.arange(RAD), all_residue.reshape(-1), RAD)
     cos_m, sin_m = np.cos(angle), np.sin(angle)
-    real = dot("ur,srt->sut", const(np.concatenate([cos_m, sin_m], axis=1)), stacked)
-    imag = dot("ur,srt->sut", const(np.concatenate([-sin_m, cos_m], axis=1)), stacked)
-    when = jnp.arange(BL, dtype=jnp.int32).reshape(RAD, VL)
-    phase = (my_remain[:, None, None] * when[None] % BL).astype(jnp.float32) * (two_pi / BL)
+    real = dot("ur,prt->put", const(np.concatenate([cos_m, sin_m], axis=1)), stacked)
+    imag = dot("ur,prt->put", const(np.concatenate([-sin_m, cos_m], axis=1)), stacked)
+    when = np.tile(np.arange(BL).reshape(1, RAD, VL), (1, 1, 2))
+    lanes = lambda array: jnp.repeat(array.reshape(slots // 2, 1, 2), VL, axis=2)
+    phase = (lanes(my_remain) * jnp.asarray(when.astype(np.int32)) % BL).astype(jnp.float32) * (two_pi / BL)
     phase_cos, phase_sin = jnp.cos(phase), jnp.sin(phase)
-    result = real * (phase_cos - phase_sin) - imag * (phase_sin + phase_cos)
     scale = jnp.where(my_slots >= 0, my_gain / jnp.sqrt(my_width), 0.0)
-    return (result * scale[:, None, None]).reshape(slots, BL)
+    result = (real * (phase_cos - phase_sin) - imag * (phase_sin + phase_cos)) * lanes(scale)
+    result = result.reshape(slots // 2, RAD, 2, VL).transpose(0, 2, 1, 3)
+    return result.reshape(slots, BL)
 
 
 def solution(mesh):

time: 114 us -> 91.4 us (0.80)
  Pallas kernels: 7.21 us -> 73.1 us
  waiting for transfers between devices: 35.3 us -> 0 us
  blocking collectives: 34.7 us -> 0 us
  other arithmetic: 9.46 us -> 1.89 us
  matrix products: 9.93 us -> 3.33 us
  starting transfers between devices: 5.67 us -> 0 us
  local copies, waits for them, and re-layouts: 10.5 us -> 12.5 us
    pallas_call x1 -> x3, Pallas kernels: 7.21 us -> 73.1 us  [the longest x1 55 us: spectrum(): pl.pallas_call(lambda *refs: transform_kernel(size_x, size_y, own, half,...]
    all_to_all x2 -> x0, waiting for transfers between devices: 35.3 us -> none  [exchange(): return lax.all_to_all(blocks, AXES, split_axis=0, concat_axis=0, tiled=True)]
    all_to_all x1 -> x0, blocking collectives: 34.7 us -> none  [exchange(): return lax.all_to_all(blocks, AXES, split_axis=0, concat_axis=0, tiled=True)]
    mul x1, other arithmetic: 8.36 us -> 1.02 us  [body(): incoming * taper_gain]
    dot_general x7 -> x4, matrix products: 9.93 us -> 3.33 us  [dot(): return jnp.einsum(spec, left, right, precision=lax.Precision.HIGH)]
    unnamed x43 -> x40, local copies, waits for them, and re-layouts: 0.31 us -> 6.65 us
    all_to_all x2 -> x0, starting transfers between devices: 5.67 us -> none  [exchange(): return lax.all_to_all(blocks, AXES, split_axis=0, concat_axis=0, tiled=True)]
    concatenate x1 -> x0, local copies, waits for them, and re-layouts: 1.98 us -> none  [body(): jnp.concatenate([turned_real, turned_imag], axis=2)]
  transfers between devices with their start and end apart: 2 -> 0, of which waited for: 2 -> 0; matrix products, arithmetic and copies ran while one was open for 2% -> 0% of each run, Pallas kernels for 0% -> 0%
where the time goes in v3:
time: 91.4 us; the launch traced here: 91 us
  Pallas kernels  73.1 us (80%)
  local copies, waits for them, and re-layouts  12.5 us (14%)
  matrix products  3.33 us (4%)
  other arithmetic  1.89 us (2%)
    pallas_call x1, Pallas kernels, spectrum(): pl.pallas_call(lambda *refs: transform_kernel(size_x, size_y, own, half,...  55 us
    pallas_call x1, Pallas kernels, spectrum(): pl.pallas_call(lambda *refs: deliver_kernel(size_x, size_y, *refs), out_s...  11.6 us
    unnamed x40, local copies, waits for them, and re-layouts  6.65 us
    pallas_call x1, Pallas kernels, spectrum(): pl.pallas_call(lambda *refs: combine_kernel(devices, own, half, total, *r...  6.5 us
    dot_general x4, matrix products, dot(): return jnp.einsum(spec, left, right, precision=lax.Precision.HIGH)  3.33 us

profile of v3, /device:TPU:0, one launch (start us, length us, event | category | flops | bytes accessed | tf_op | source)
XLA Modules:
  0.0 91.0 jit_solution(7042611370697030464)
XLA Ops:
  0.0 0.7 copy-done.11
  0.7 0.7 copy-done.14
  1.4 1.8 %copy.44 = f32[128,8,256]{2,1,0:T(8,128)S(1)} copy(f32[128,8,256]{0,2,1:T(8,128)} %bitcast.48) | data formatting | bytes 2097152 | tf_op jit(solution)/shard_map/transpose | solution.py:355
  3.2 1.0 %copy-done.2 = bf16[4,2,128,256]{3,2,1,0:T(8,128)(2,1)S(1)} copy-done((bf16[4,2,128,256]{3,2,1,0:T(8,128)(2,1)S(1)}, bf16[4,2,128,256]{3,2,1,0:T(8,128)(2,1)}, u32[]{:S(2)}) %copy-start.2) | copy-done | bytes 524312
  4.3 1.0 %copy-done.3 = f32[4,2,64,256]{3,2,1,0:T(8,128)S(1)} copy-done((f32[4,2,64,256]{3,2,1,0:T(8,128)S(1)}, f32[4,2,64,256]{3,2,1,0:T(8,128)}, u32[]{:S(2)}) %copy-start.3) | copy-done | bytes 524312
  5.3 55.0 %transform.1.refs_2_ = f32[2048,128]{1,0:T(8,128)S(1)} custom-call(f32[32,4,8,256]{3,2,1,0:T(8,128)S(1)} %bitcast.44, bf16[4,2,128,256]{3,2,1,0:T(8,128)(2,1)S(1)} %copy-done.2, f32[4,2,64,256]{3,2,1,0:T(8,128)S(1)} %copy-done.3, bf16[2,2,512,256]{3,2,1,0:T(8,128)(2,1)S(1)} %copy-done), custom_call_target="tpu_custom_call" | custom-call | tf_op jit(solution)/shard_map/transform/pallas_call | solution.py:307
  60.3 0.7 dynamic-slice_bitcast_fusion.1
  61.1 0.2 fusion.13
  61.5 0.7 dynamic-slice_bitcast_fusion.refs_7_
  62.2 1.0 %copy-done.1 = f32[2,256,256]{2,1,0:T(8,128)S(1)} copy-done((f32[2,256,256]{2,1,0:T(8,128)S(1)}, f32[2,256,256]{2,1,0:T(8,128)}, u32[]{:S(2)}) %copy-start.1) | copy-done | bytes 524312
  63.2 6.5 %combine.1.refs_0_ = f32[32,2,8,128]{3,2,1,0:T(8,128)S(1)} custom-call(s32[1]{0:T(128)} %bitcast.refs_0_, s32[128]{0:T(128)S(1)} %select_reduce_fusion.refs_1_, f32[2048,128]{1,0:T(8,128)S(1)} %transform.1.refs_2_, f32[2,256,256]{2,1,0:T(8,128)S(1)} %copy-done.1, f32[2,256,5]{2,1,0:T(8,128)S(1)} %copy.45.refs_4_, bf16[2,256,256]{2,1,0:T(8,128)(2,1)S(1)} %copy-done.4, ...), custom_call_target="tpu_custom_call" | custom-call | tf_op jit(solution)/shard_map/combine/pallas_call | solution.py:321
  69.7 11.6 %deliver.1 = f32[32,2,8,128]{3,2,1,0:T(8,128)S(1)} custom-call(f32[32,2,8,128]{3,2,1,0:T(8,128)S(1)} %combine.1.refs_0_), custom_call_target="tpu_custom_call" | custom-call | tf_op jit(solution)/shard_map/deliver/pallas_call | solution.py:333
  81.4 0.7 copy-done.15
  82.1 0.2 select_reduce_fusion.2
  82.8 1.0 %select_multiply_fusion = f32[32,2,8,128]{3,2,1,0:T(8,128)S(1)} fusion(f32[32,2,8,128]{3,2,1,0:T(8,128)S(1)} %deliver.1, f32[2,128]{1,0:T(2,128)S(1)} %broadcast_in_dim.81, s32[2,128]{1,0:T(2,128)S(1)} %broadcast_in_dim.77, s32[32,8,128]{2,1,0:T(8,128)S(1)} %copy-done.7), kind=kLoop, calls=%fused_computation.26 | loop fusion | flops 1376256 | bytes 657408 | tf_op jit(solution)/shard_map/mul | solution.py:379
  83.8 0.3 convolution_bitcast_fusion.3
  84.1 0.6 copy-done.8
  84.8 0.3 multiply_add_fusion
  85.8 0.7 copy-done.18
  86.6 1.3 %fusion = f32[2,256,128]{1,2,0:T(8,128)S(1)} fusion(f32[256,512,1]{1,0,2:T(8,128)S(1)} %copy-done.18, f32[2,256,128]{1,2,0:T(8,128)S(1)} %copy.51, f32[2,256,128]{1,2,0:T(8,128)S(1)} %copy.50, s32[256,128]{0,1:T(8,128)S(1)} %copy-done.19, s32[2,128]{1,0:T(2,128)S(1)} %broadcast_in_dim.77), kind=kOutput, calls=%fused_computation.4 | convolution fusion | flops 202506240 | bytes 1442816 | tf_op jit(solution)/shard_map/ur,prt->put/dot_general | solution.py:28
  88.0 0.2 select_reduce_fusion.1
  88.5 1.4 %fusion.3 = f32[2,256,128]{1,2,0:T(8,128)S(1)} fusion(f32[2,256,128]{1,2,0:T(8,128)S(1)} %fusion, f32[256,512,1]{1,0,2:T(8,128)S(1)} %copy-done.17, f32[2,256,128]{1,2,0:T(8,128)S(1)} %copy.51, f32[2,256,128]{1,2,0:T(8,128)S(1)} %copy.50, f32[2,128]{1,0:T(2,128)S(1)} %broadcast_in_dim.87, s32[256,128]{0,1:T(8,128)S(1)} %copy-done.19, ...), kind=kOutput, calls=%fused_computation.7 | convolution fusion | flops 202637312 | bytes 1705984 | tf_op jit(solution)/shard_map/ur,prt->put/dot_general | solution.py:28
  89.9 0.2 copy.52
  90.1 0.9 %reshape.224 = f32[4,16384]{1,0:T(4,128)} reshape(f32[2,2,256,64]{3,2,1,0:T(8,128)S(1)} %bitcast.47) | data formatting | bytes 524288 | tf_op jit(solution)/shard_map/reshape | solution.py:401
  (52 shorter events, 2.0 us)
Async XLA Ops:
  0.0 0.7 copy-start.11
  0.7 0.7 copy-start.14
  1.4 1.8 %copy-start = (bf16[2,2,512,256]{3,2,1,0:T(8,128)(2,1)S(1)}, bf16[2,2,512,256]{3,2,1,0:T(8,128)(2,1)}, u32[]{:S(2)}) copy-start(bf16[2,2,512,256]{3,2,1,0:T(8,128)(2,1)} %constant.109.clone.refs_3_) | copy-start | bytes 3145732
  3.2 1.0 %copy-start.2 = (bf16[4,2,128,256]{3,2,1,0:T(8,128)(2,1)S(1)}, bf16[4,2,128,256]{3,2,1,0:T(8,128)(2,1)}, u32[]{:S(2)}) copy-start(bf16[4,2,128,256]{3,2,1,0:T(8,128)(2,1)} %constant.121.refs_1_) | copy-start | bytes 1572868
  4.3 1.0 %copy-start.3 = (f32[4,2,64,256]{3,2,1,0:T(8,128)S(1)}, f32[4,2,64,256]{3,2,1,0:T(8,128)}, u32[]{:S(2)}) copy-start(f32[4,2,64,256]{3,2,1,0:T(8,128)} %constant.108.clone.refs_2_) | copy-start | bytes 1572868
  5.3 55.8 %copy-start.12 = (s32[256]{0:T(256)S(1)}, s32[256]{0:T(256)}, u32[]{:S(2)}) copy-start(s32[256]{0:T(256)} %constant.122) | copy-start | bytes 3076
  5.3 55.8 %copy-start.13 = (f32[256]{0:T(256)S(1)}, f32[256]{0:T(256)}, u32[]{:S(2)}) copy-start(f32[256]{0:T(256)} %constant.123) | copy-start | bytes 3076
  5.3 56.9 %copy-start.5 = (bf16[2,256,256]{2,1,0:T(8,128)(2,1)S(1)}, bf16[2,256,256]{2,1,0:T(8,128)(2,1)}, u32[]{:S(2)}) copy-start(bf16[2,256,256]{2,1,0:T(8,128)(2,1)} %constant.112.clone.refs_6_) | copy-start | bytes 786436
  60.3 1.9 %copy-start.4 = (bf16[2,256,256]{2,1,0:T(8,128)(2,1)S(1)}, bf16[2,256,256]{2,1,0:T(8,128)(2,1)}, u32[]{:S(2)}) copy-start(bf16[2,256,256]{2,1,0:T(8,128)(2,1)} %constant.111.clone.refs_5_) | copy-start | bytes 786436
  62.2 1.0 %copy-start.1 = (f32[2,256,256]{2,1,0:T(8,128)S(1)}, f32[2,256,256]{2,1,0:T(8,128)}, u32[]{:S(2)}) copy-start(f32[2,256,256]{2,1,0:T(8,128)} %constant.110.clone.refs_3_) | copy-start | bytes 1572868
  69.7 13.0 %copy-start.7 = (s32[32,8,128]{2,1,0:T(8,128)S(1)}, s32[32,8,128]{2,1,0:T(8,128)}, u32[]{:S(2)}) copy-start(s32[32,8,128]{2,1,0:T(8,128)} %constant.124) | copy-start | bytes 393220
  81.4 0.7 copy-start.15
  82.8 1.0 %copy-start.6 = (f32[2,128,128,1,1]{2,1,4,3,0:T(8,128)S(1)}, f32[2,128,128,1,1]{2,1,4,3,0:T(8,128)}, u32[]{:S(2)}) copy-start(f32[2,128,128,1,1]{2,1,4,3,0:T(8,128)} %constant.126) | copy-start | bytes 393220
  83.8 0.9 copy-start.8
  83.8 1.0 %copy-start.9 = (f32[32,2,4,128]{3,0,2,1:T(8,128)S(1)}, f32[32,2,4,128]{3,0,2,1:T(8,128)}, u32[]{:S(2)}) copy-start(f32[32,2,4,128]{3,0,2,1:T(8,128)} %constant.116.clone) | copy-start | bytes 393220
  83.8 1.0 %copy-start.10 = (f32[2,128,128,1,1]{2,1,4,3,0:T(8,128)S(1)}, f32[2,128,128,1,1]{2,1,4,3,0:T(8,128)}, u32[]{:S(2)}) copy-start(f32[2,128,128,1,1]{2,1,4,3,0:T(8,128)} %constant.127) | copy-start | bytes 393220
  85.5 1.0 %copy-start.18 = (f32[256,512,1]{1,0,2:T(8,128)S(1)}, f32[256,512,1]{1,0,2:T(8,128)}, u32[]{:S(2)}) copy-start(f32[256,512,1]{1,0,2:T(8,128)} %constant.128) | copy-start | bytes 1572868
  85.7 0.9 %copy-start.19 = (s32[256,128]{0,1:T(8,128)S(1)}, s32[256,128]{0,1:T(8,128)}, u32[]{:S(2)}) copy-start(s32[256,128]{0,1:T(8,128)} %constant.125) | copy-start | bytes 393220
  86.6 1.3 %copy-start.16 = (f32[64]{0:T(128)S(1)}, f32[64]{0:T(128)}, u32[]{:S(2)}) copy-start(f32[64]{0:T(128)} %param.26) | copy-start | bytes 772
  86.6 1.8 %copy-start.17 = (f32[256,512,1]{1,0,2:T(8,128)S(1)}, f32[256,512,1]{1,0,2:T(8,128)}, u32[]{:S(2)}) copy-start(f32[256,512,1]{1,0,2:T(8,128)} %constant.129) | copy-start | bytes 1572868

commit v4 on v3

--- a/solution.py
+++ b/solution.py
@@ -22,10 +22,6 @@
 
 def const(array):
     return jnp.asarray(np.ascontiguousarray(array, dtype=np.float32))
-
-
-def dot(spec, left, right):
-    return jnp.einsum(spec, left, right, precision=lax.Precision.HIGH)
 
 
 def lookup(values_table, positions):
@@ -89,10 +85,18 @@
     return devices, me, send, wait
 
 
+def fetch(sem, *pairs):
+    loads = [pltpu.make_async_copy(source, target, sem.at[k]) for k, (source, target) in enumerate(pairs)]
+    for load in loads:
+        load.start()
+    return loads
+
+
 def transform_kernel(
     size_x, size_y, own, half,
-    turned_ref, first_ref, twist_ref, second_ref,
-    value_ref, column_ref, high_ref, low_ref, pass_ref, send_sem, recv_sem,
+    turned_ref, first_hbm, twist_hbm, second_hbm,
+    value_ref, column_ref, high_ref, low_ref, pass_ref, first_ref, twist_ref, second_ref,
+    send_sem, recv_sem, load_sem,
 ):
     devices, me, send, wait = meet(size_x, size_y, send_sem, recv_sem)
     others = devices - 1
@@ -105,7 +109,12 @@
         return carry
 
     lax.fori_loop(1, devices, send_columns, 0)
-    column_ref[me] = turned_ref[me]
+    loads = fetch(
+        load_sem, (turned_ref.at[me], column_ref.at[me]),
+        (first_hbm, first_ref), (twist_hbm, twist_ref), (second_hbm, second_ref),
+    )
+    for load in loads:
+        load.wait()
     wait(column_ref.at[pl.ds(0, others)], recv_sem.at[0])
     for c in range(own):
         high, low = split(column_ref[:, c].reshape(RAD, RAD))
@@ -239,21 +248,61 @@
     lax.fori_loop(0, devices, step, 0, unroll=2)
 
 
-def deliver_kernel(size_x, size_y, leave_ref, out_ref, send_sem, recv_sem):
+def deliver_kernel(
+    size_x, size_y,
+    shift_ref, width_ref, rate_ref, scale_ref, leave_ref, place_hbm, inner_hbm, twist_hbm, outer_hbm, when_hbm,
+    out_ref, land_ref, gain_ref, phase_ref, place_ref, inner_ref, twist_ref, outer_ref, when_ref,
+    send_sem, recv_sem, load_sem,
+):
     devices, me, send, wait = meet(size_x, size_y, send_sem, recv_sem)
+    pairs, height = leave_ref.shape[1:3]
 
     def step(j, carry):
         to = lax.rem(me + j, devices)
-        send(0, leave_ref.at[to], out_ref.at[me], to)
+        send(0, leave_ref.at[to], land_ref.at[me], to)
         return carry
 
     lax.fori_loop(1, devices, step, 0)
-    out_ref[me] = leave_ref[me]
+    loads = fetch(
+        load_sem, (place_hbm, place_ref), (when_hbm, when_ref), (inner_hbm, inner_ref), (twist_hbm, twist_ref),
+        (outer_hbm, outer_ref),
+    )
+    land_ref[me] = leave_ref[me]
+    for load in loads:
+        load.wait()
+
+    is_low = lax.broadcasted_iota(jnp.int32, (1, 128), 1) < VL
+    for p in range(pairs):
+        of = lambda ref: jnp.where(is_low, ref[2 * p], ref[2 * p + 1])
+        shift = of(shift_ref)
+        position = (place_ref[...] - shift) & (BL - 1)
+        turn = (position.astype(jnp.float32) + 0.5) * of(rate_ref)
+        gain_ref[p] = jnp.where(position < of(width_ref), 0.5 - 0.5 * jnp.cos(turn), 0.0)
+        angle = ((when_ref[...] * shift) & (BL - 1)).astype(jnp.float32) * (two_pi / BL)
+        phase_cos, phase_sin = jnp.cos(angle), jnp.sin(angle)
+        phase_ref[p, 0] = (phase_cos - phase_sin) * of(scale_ref)
+        phase_ref[p, 1] = (phase_cos + phase_sin) * of(scale_ref)
+
+    wait(land_ref.at[pl.ds(0, devices - 1)], recv_sem.at[0])
+    is_back = lax.broadcasted_iota(jnp.int32, (RAD, 1), 0) % height >= height // 2
+    stacked = []
+    for p in range(pairs):
+        tapered = land_ref[:, p].reshape(RAD, 128) * gain_ref[p]
+        part = product(split(tapered), (inner_ref[0], inner_ref[1]))
+        part = jnp.where(is_back, part[:, 256:], part[:, :256])
+        real, imag = part[:, :128], part[:, 128:]
+        twist_cos, twist_sin = twist_ref[0], twist_ref[1]
+        stacked.append(
+            jnp.concatenate([real * twist_cos + imag * twist_sin, imag * twist_cos - real * twist_sin], axis=0)
+        )
+    result = product((outer_ref[0], outer_ref[1]), split(jnp.concatenate(stacked, axis=1)))
+    for p in range(pairs):
+        lanes = slice(p * 128, (p + 1) * 128)
+        out_ref[p] = result[:RAD, lanes] * phase_ref[p, 0] - result[RAD:, lanes] * phase_ref[p, 1]
     wait(leave_ref.at[pl.ds(0, devices - 1)], send_sem.at[0])
-    wait(out_ref.at[pl.ds(0, devices - 1)], recv_sem.at[0])
-
-
-def spectrum(turned, starts, device, base, total):
+
+
+def spectrum(turned, starts, slots, device, base, total):
     size_x, size_y = lax.axis_size("tx"), lax.axis_size("ty")
     devices, _, half = base.shape
     own = turned.shape[1]
@@ -301,23 +350,26 @@
     pairs = starts.shape[0] // (2 * devices)
     shape = (devices, pairs, 2 * half, 128)
     f32, bf16 = jnp.float32, jnp.bfloat16
+    hbm = pl.BlockSpec(memory_space=pl.ANY)
+    first, twist, second = const_split(first).swapaxes(0, 1), const(twist), const_split(second)
+    room = lambda *arrays: [pltpu.VMEM(array.shape, array.dtype) for array in arrays]
     sems = lambda n: [pltpu.SemaphoreType.DMA((n,)), pltpu.SemaphoreType.DMA((n,))]
-    limit = 48 * 1024 * 1024
+    limit = 56 * 1024 * 1024
     remote = lambda k: pltpu.CompilerParams(vmem_limit_bytes=limit, collective_id=k, has_side_effects=True)
     value = pl.pallas_call(
         lambda *refs: transform_kernel(size_x, size_y, own, half, *refs),
         out_shape=jax.ShapeDtypeStruct((count * half * 2, 128), f32),
-        in_specs=[vmem] * 4,
+        in_specs=[hbm] * 4,
         out_specs=vmem,
         scratch_shapes=[
             pltpu.VMEM(turned.shape, f32),
             pltpu.VMEM((RAD, own * RAD), bf16),
             pltpu.VMEM((RAD, own * RAD), bf16),
             pltpu.VMEM((count * half * 2, 128), f32),
-        ] + sems(2),
+        ] + room(first, twist, second) + sems(2) + [pltpu.SemaphoreType.DMA((4,))],
         compiler_params=remote(0),
         name="transform",
-    )(turned, const_split(first).swapaxes(0, 1), const(twist), const_split(second))
+    )(turned, first, twist, second)
     leaving = pl.pallas_call(
         lambda *refs: combine_kernel(devices, own, half, total, *refs),
         out_shape=jax.ShapeDtypeStruct(shape, f32),
@@ -330,15 +382,34 @@
         device.reshape(1).astype(jnp.int32), starts, value, const(alpha), beta,
         const_split(mix), jnp.asarray(swap.astype(np.float32).astype(jnp.bfloat16)), residue,
     )
+
+    all_residue = (base * np.array([1, -1])[None, :, None]) % RAD
+    lane = np.arange(VL)
+    back = np.stack([lane, VL - 1 - lane])
+    place = back[None, :, None, :] * RAD + all_residue[..., None]
+    place = jnp.asarray(np.tile(place.reshape(RAD, VL), (1, 2)).astype(np.int32))
+    angle = np.stack([grid(back[0], lane, VL), grid(back[1], lane, VL)])
+    both = np.stack([np.cos(angle), -np.sin(angle)])
+    inner = const_split(np.einsum("bd,chvt->bvhcdt", np.eye(2), both).reshape(2 * VL, 8 * VL))
+    angle = np.tile(grid(all_residue.reshape(-1), lane, BL), (1, 2))
+    spin = const(np.stack([np.cos(angle), np.sin(angle)]))
+    angle = grid(span, all_residue.reshape(-1), RAD)
+    cos_m, sin_m = np.cos(angle), np.sin(angle)
+    outer = const_split(np.block([[cos_m, sin_m], [-sin_m, cos_m]]))
+    when = jnp.asarray(np.tile(np.arange(BL).reshape(RAD, VL), (1, 2)).astype(np.int32))
     return pl.pallas_call(
         lambda *refs: deliver_kernel(size_x, size_y, *refs),
-        out_shape=jax.ShapeDtypeStruct(shape, f32),
-        in_specs=[vmem],
+        out_shape=jax.ShapeDtypeStruct((pairs, RAD, 128), f32),
+        in_specs=[smem] * 4 + [vmem] + [hbm] * 5,
         out_specs=vmem,
-        scratch_shapes=sems(1),
+        scratch_shapes=[
+            pltpu.VMEM(shape, f32),
+            pltpu.VMEM((pairs, RAD, 128), f32),
+            pltpu.VMEM((pairs, 2, RAD, 128), f32),
+        ] + room(place, inner, spin, outer, when) + sems(1) + [pltpu.SemaphoreType.DMA((5,))],
         compiler_params=remote(1),
         name="deliver",
-    )(leaving)
+    )(*slots, leaving, place, inner, spin, outer, when)
 
 
 def body(signal, band_start, band_width, band_gain, slot_band):
@@ -356,47 +427,16 @@
     turned = turned.reshape(devices, own, chunk // RAD, RAD)
     slot_index = jnp.maximum(slot_band, 0)
     starts = lookup(band_start, slot_index)
-    incoming = spectrum(turned, starts, device, base, total)
     slots = slot_band.shape[0] // devices
-
     mine = lambda array: lax.dynamic_slice_in_dim(array, device * slots, slots)
     my_slots = mine(slot_band)
     my_index = jnp.maximum(my_slots, 0)
-    my_remain = mine(starts) % BL
-    my_width = lookup(band_width, my_index).astype(jnp.float32)
-    my_gain = lookup(band_gain, my_index)
-    all_residue = (base * np.array([1, -1])[None, :, None]) % RAD
-    lane = np.arange(VL)
-    step = np.stack([lane, VL - 1 - lane])
-    place = step[None, :, None, :] * RAD + all_residue[..., None]
-    place = np.tile(place.reshape(devices, 1, 2 * half, VL), (1, 1, 1, 2))
-    lanes = lambda array: jnp.repeat(array.reshape(1, slots // 2, 1, 2), VL, axis=3)
-    position = ((jnp.asarray(place.astype(np.int32)) - lanes(my_remain)) % BL).astype(jnp.float32)
-    wide = lanes(my_width)
-    taper_gain = jnp.where(
-        position < wide, 0.5 - 0.5 * jnp.cos(two_pi * (position + 0.5) / wide), 0.0
-    )
-    tapered = (incoming * taper_gain).reshape(devices, slots // 2, 2, half, 2 * VL)
-    angle = np.stack([grid(step[0], lane, VL), grid(step[1], lane, VL)])
-    twice = lambda array: np.einsum("bd,hvt->hbvdt", np.eye(2), array).reshape(2, 2 * VL, 2 * VL)
-    part_real = dot("fphiv,hvt->pfhit", tapered, const(twice(np.cos(angle))))
-    part_imag = dot("fphiv,hvt->pfhit", tapered, const(twice(-np.sin(angle))))
-    angle = np.tile(grid(all_residue.reshape(-1), lane, BL).reshape(base.shape + (VL,)), (1, 1, 1, 2))
-    twist_cos, twist_sin = const(np.cos(angle)), const(np.sin(angle))
-    flat = lambda array: array.reshape(slots // 2, RAD, 2 * VL)
-    turned_real = flat(part_real * twist_cos + part_imag * twist_sin)
-    turned_imag = flat(part_imag * twist_cos - part_real * twist_sin)
-    stacked = jnp.concatenate([turned_real, turned_imag], axis=1)
-    angle = grid(np.arange(RAD), all_residue.reshape(-1), RAD)
-    cos_m, sin_m = np.cos(angle), np.sin(angle)
-    real = dot("ur,prt->put", const(np.concatenate([cos_m, sin_m], axis=1)), stacked)
-    imag = dot("ur,prt->put", const(np.concatenate([-sin_m, cos_m], axis=1)), stacked)
-    when = np.tile(np.arange(BL).reshape(1, RAD, VL), (1, 1, 2))
-    lanes = lambda array: jnp.repeat(array.reshape(slots // 2, 1, 2), VL, axis=2)
-    phase = (lanes(my_remain) * jnp.asarray(when.astype(np.int32)) % BL).astype(jnp.float32) * (two_pi / BL)
-    phase_cos, phase_sin = jnp.cos(phase), jnp.sin(phase)
-    scale = jnp.where(my_slots >= 0, my_gain / jnp.sqrt(my_width), 0.0)
-    result = (real * (phase_cos - phase_sin) - imag * (phase_sin + phase_cos)) * lanes(scale)
+    my_width = lookup(band_width, my_index)
+    wide = my_width.astype(jnp.float32)
+    scale = jnp.where(my_slots >= 0, lookup(band_gain, my_index) / jnp.sqrt(wide), 0.0)
+    result = spectrum(
+        turned, starts, (mine(starts) % BL, my_width, two_pi / wide, scale), device, base, total
+    )
     result = result.reshape(slots // 2, RAD, 2, VL).transpose(0, 2, 1, 3)
     return result.reshape(slots, BL)
 

time: 91.4 us -> 91.7 us (level)
  Pallas kernels: 73.1 us -> 78.8 us
  matrix products: 3.33 us -> 0 us
  local copies, waits for them, and re-layouts: 12.5 us -> 9.87 us
    unnamed x40 -> x16, local copies, waits for them, and re-layouts: 6.65 us -> 2.17 us
    dot_general x4 -> x0, matrix products: 3.33 us -> none  [dot(): return jnp.einsum(spec, left, right, precision=lax.Precision.HIGH)]
    pallas_call x1, Pallas kernels: 11.6 us -> 14.4 us  [spectrum(): pl.pallas_call(lambda *refs: deliver_kernel(size_x, size_y, *refs), out_s...]
    pallas_call x1, Pallas kernels: 6.5 us -> 8.27 us  [spectrum(): pl.pallas_call(lambda *refs: combine_kernel(devices, own, half, total, *r...]
    pallas_call x1, Pallas kernels: 55 us -> 56.1 us  [spectrum(): pl.pallas_call(lambda *refs: transform_kernel(size_x, size_y, own, half,...]
    pallas_call x0 -> x1, local copies, waits for them, and re-layouts: none -> 1.08 us  [spectrum(): pl.pallas_call(lambda *refs: deliver_kernel(size_x, size_y, *refs), out_s...]
    mul x1 -> x0, other arithmetic: 1.02 us -> none  [body(): incoming * taper_gain]
    select_n x2, other arithmetic: 0.16 us -> 1.15 us  [the longest x1 0.6 us: body(): jnp.where(my_slots >= 0, lookup(band_gain, my_index) / jnp.sqrt(wide), 0.0)]
where the time goes in v4:
time: 91.7 us; the launch traced here: 91.3 us
  Pallas kernels  78.8 us (86%)
  local copies, waits for them, and re-layouts  9.87 us (11%)
  other arithmetic  2.52 us (3%)
    pallas_call x1, Pallas kernels, spectrum(): pl.pallas_call(lambda *refs: transform_kernel(size_x, size_y, own, half,...  56.1 us
    pallas_call x1, Pallas kernels, spectrum(): pl.pallas_call(lambda *refs: deliver_kernel(size_x, size_y, *refs), out_s...  14.4 us
    pallas_call x1, Pallas kernels, spectrum(): pl.pallas_call(lambda *refs: combine_kernel(devices, own, half, total, *r...  8.27 us
    transpose x1, local copies, waits for them, and re-layouts, body(): turned = signal.reshape(chunk // RAD, RAD, cols).transpose(2, 0, 1)  2.65 us
    unnamed x16, local copies, waits for them, and re-layouts  2.17 us

profile of v4, /device:TPU:0, one launch (start us, length us, event | category | flops | bytes accessed | tf_op | source)
XLA Modules:
  0.0 91.3 jit_solution(6889920914569916916)
XLA Ops:
  0.0 0.7 broadcast_maximum_fusion.1
  0.7 0.1 select_reduce_fusion.refs_1_
  0.8 0.0 copy-start.1
  0.8 0.6 copy-done
  1.3 0.1 copy-done.1
  1.4 0.6 and_select_fusion
  2.0 0.7 copy-done.6
  2.7 0.2 select_reduce_fusion.2.refs_1_
  2.8 0.5 copy-done.7
  3.3 0.2 select_reduce_fusion.1
  3.5 0.4 copy-done.2
  3.9 0.6 compare_select_fusion.2
  4.5 2.6 %copy.29 = f32[128,8,256]{2,1,0:T(8,128)} copy(f32[128,8,256]{0,2,1:T(8,128)} %bitcast.16) | data formatting | bytes 2097152 | tf_op jit(solution)/shard_map/transpose | solution.py:426
  7.1 56.1 %transform.1.refs_2_ = f32[2048,128]{1,0:T(8,128)} custom-call(f32[32,4,8,256]{3,2,1,0:T(8,128)} %bitcast.14, bf16[4,2,128,256]{3,2,1,0:T(8,128)(2,1)} %constant.92.refs_1_, f32[4,2,64,256]{3,2,1,0:T(8,128)} %constant.82.clone.refs_2_, bf16[2,2,512,256]{3,2,1,0:T(8,128)(2,1)} %constant.83.clone.refs_3_), custom_call_target="tpu_custom_call" | custom-call | tf_op jit(solution)/shard_map/transform/pallas_call | solution.py:359
  63.3 0.0 copy-start.3
  63.3 0.7 dynamic-slice_bitcast_fusion.1
  64.0 0.2 fusion
  64.2 0.9 copy.30.refs_4_
  65.1 1.3 %dynamic-slice_bitcast_fusion.refs_7_ = s32[8,128]{1,0:T(8,128)} fusion(s32[32,8,128]{2,1,0:T(8,128)} %constant.80.clone, s32[]{:T(128)S(6)} %select_n.39), kind=kLoop, calls=%fused_computation.5 | loop fusion | bytes 8196 | tf_op jit(solution)/shard_map/jit(dynamic_index_in_dim)/squeeze | solution.py:336
  66.4 8.3 %combine.1.refs_4_ = f32[32,2,8,128]{3,2,1,0:T(8,128)} custom-call(s32[1]{0:T(128)} %bitcast.refs_0_, s32[128]{0:T(128)} %copy-done, f32[2048,128]{1,0:T(8,128)} %transform.1.refs_2_, f32[2,256,256]{2,1,0:T(8,128)} %constant.84.clone.refs_3_, f32[2,256,5]{2,1,0:T(8,128)} %copy.30.refs_4_, bf16[2,256,256]{2,1,0:T(8,128)(2,1)} %constant.85.clone.refs_5_, ...), custom_call_target="tpu_custom_call" | custom-call | tf_op jit(solution)/shard_map/combine/pallas_call | solution.py:373
  74.6 14.4 %deliver.1 = f32[2,256,128]{2,1,0:T(8,128)} custom-call(s32[4]{0:T(128)} %get-tuple-element.9.refs_0_, s32[4]{0:T(128)} %copy-done.2, f32[4]{0:T(128)} %get-tuple-element.8.refs_2_, f32[4]{0:T(128)} %get-tuple-element.7.refs_3_, f32[32,2,8,128]{3,2,1,0:T(8,128)} %combine.1.refs_4_, s32[256,128]{1,0:T(8,128)} %constant.87.clone.refs_5_, ...), custom_call_target="tpu_custom_call" | custom-call | tf_op jit(solution)/shard_map/deliver/pallas_call | solution.py:400
  89.1 1.1 %copy.31 = f32[2,256,128]{1,2,0:T(8,128)S(1)} copy(f32[2,256,128]{2,1,0:T(8,128)} %deliver.1) | data formatting | bytes 524288 | tf_op jit(solution)/shard_map/deliver/pallas_call | solution.py:400
  90.1 0.2 copy.32
  90.3 0.9 %reshape.174 = f32[4,16384]{1,0:T(4,128)} reshape(f32[2,2,256,64]{3,2,1,0:T(8,128)S(1)} %copy.32) | data formatting | bytes 524288 | tf_op jit(solution)/shard_map/reshape | solution.py:441
  (10 shorter events, 0.0 us)
Async XLA Ops:
  0.0 0.7 copy-start.5
  0.8 0.6 copy-start
  0.8 0.7 copy-start.1
  2.0 0.7 copy-start.6
  2.7 0.7 copy-start.7
  3.3 0.6 copy-start.2
  7.1 56.8 %copy-start.4 = (f32[256]{0:T(256)S(1)}, f32[256]{0:T(256)}, u32[]{:S(2)}) copy-start(f32[256]{0:T(256)} %constant.94) | copy-start | bytes 3076
  63.3 0.7 copy-start.3

commit v5 on v4

--- a/solution.py
+++ b/solution.py
@@ -22,13 +22,6 @@
 
 def const(array):
     return jnp.asarray(np.ascontiguousarray(array, dtype=np.float32))
-
-
-def lookup(values_table, positions):
-    one_hot = positions[:, None] == jnp.arange(values_table.shape[0], dtype=jnp.int32)[None, :]
-    return jnp.sum(
-        jnp.where(one_hot, values_table[None, :], jnp.zeros((), values_table.dtype)), axis=1
-    )
 
 
 def row_bases(devices):
@@ -93,9 +86,10 @@
 
 
 def transform_kernel(
-    size_x, size_y, own, half,
-    turned_ref, first_hbm, twist_hbm, second_hbm,
-    value_ref, column_ref, high_ref, low_ref, pass_ref, first_ref, twist_ref, second_ref,
+    size_x, size_y, own, half, total,
+    turned_ref, first_hbm, twist_hbm, second_hbm, alpha_hbm, mix_hbm, swap_hbm,
+    table_ref, value_ref, column_ref, high_ref, low_ref, pass_ref, beta_ref,
+    first_ref, twist_ref, second_ref, alpha_ref, mix_ref, swap_ref,
     send_sem, recv_sem, load_sem,
 ):
     devices, me, send, wait = meet(size_x, size_y, send_sem, recv_sem)
@@ -112,6 +106,7 @@
     loads = fetch(
         load_sem, (turned_ref.at[me], column_ref.at[me]),
         (first_hbm, first_ref), (twist_hbm, twist_ref), (second_hbm, second_ref),
+        (alpha_hbm, alpha_ref), (mix_hbm, mix_ref), (swap_hbm, swap_ref),
     )
     for load in loads:
         load.wait()
@@ -159,21 +154,17 @@
     lax.fori_loop(0, group, transform, 0)
     mine = pl.ds(pl.multiple_of(me * span, span), span)
     value_ref[mine, :] = pass_ref[mine, :]
-    wait(value_ref.at[pl.ds(0, others * span)], recv_sem.at[1])
-
-    wait(turned_ref.at[pl.ds(0, others)], send_sem.at[0])
-    wait(pass_ref.at[pl.ds(0, others * span)], send_sem.at[1])
-
-
-def combine_kernel(
-    devices, own, half, total,
-    device_ref, start_ref, value_ref, alpha_ref, beta_ref, mix_ref, swap_ref, residue_ref,
-    leave_ref, table_ref,
-):
-    rows = total // RAD
+
     count = alpha_ref.shape[1]
     cols = count // 2
-    high_rows = 2 * own
+    row = lax.broadcasted_iota(jnp.int32, (count, 128), 0)
+    lane = lax.broadcasted_iota(jnp.int32, (count, 128), 1)
+    at = jnp.where(me == 0, jnp.where(lane == half, RAD // 2, devices * lane), me + 2 * devices * lane)
+    angle = (row // high_rows * own + row % own) * at
+    angle = angle.astype(jnp.float32) * (two_pi / total)
+    beta_ref[0] = jnp.cos(angle)
+    beta_ref[1] = jnp.where(row // own % 2 == 1, -1.0, 1.0) * jnp.sin(angle)
+    wait(value_ref.at[pl.ds(0, others * span)], recv_sem.at[1])
 
     is_upper = lax.broadcasted_iota(jnp.int32, (count, RAD), 0) // own % 2 == 1
 
@@ -203,7 +194,7 @@
         for h in range(2):
             put(result[h * cols : (h + 1) * cols], h, i)
 
-    @pl.when(device_ref[0] == 0)
+    @pl.when(me == 0)
     def _():
         block = values(0)
         high, low = split(block)
@@ -215,17 +206,38 @@
             rows_of = slice(h * cols, (h + 1) * cols)
             put(product((mix_ref[0, rows_of], mix_ref[1, rows_of]), spun), h, 0)
 
+    wait(turned_ref.at[pl.ds(0, others)], send_sem.at[0])
+    wait(pass_ref.at[pl.ds(0, others * span)], send_sem.at[1])
+
+
+def deliver_kernel(
+    size_x, size_y, half, total,
+    start_ref, width_ref, gains_ref, slot_ref, table_ref, place_hbm, inner_hbm, twist_hbm, outer_hbm, when_hbm,
+    out_ref, leave_ref, land_ref, gain_ref, phase_ref, place_ref, inner_ref, twist_ref, outer_ref, when_ref,
+    send_sem, recv_sem, load_sem,
+):
+    devices, me, send, wait = meet(size_x, size_y, send_sem, recv_sem)
+    pairs, height = leave_ref.shape[1:3]
+    rows = total // RAD
+    loads = fetch(
+        load_sem, (place_hbm, place_ref), (when_hbm, when_ref), (inner_hbm, inner_ref), (twist_hbm, twist_ref),
+        (outer_hbm, outer_ref),
+    )
     shape = (2 * half, 128)
     lane = lax.broadcasted_iota(jnp.int32, shape, 1)
     is_low = lane < VL
     is_back = lax.broadcasted_iota(jnp.int32, shape, 0) >= half
-    residue = residue_ref[...]
+    row = lax.broadcasted_iota(jnp.int32, shape, 0)
+    index = jnp.where(is_back, row - half, row)
+    residue = jnp.where(me == 0, devices * index, me + 2 * devices * index)
+    residue = jnp.where((me == 0) & (row == half), RAD // 2, residue)
+    residue = jnp.where(is_back, RAD - residue, residue)
 
     def load(tile):
-        return table_ref[pl.ds(pl.multiple_of(tile * 8, 8), 8), :][: 2 * half]
+        return table_ref[tile][: 2 * half]
 
     def window(slot):
-        start = start_ref[slot]
+        start = start_ref[jnp.maximum(slot_ref[slot], 0)]
         block = start // BL
         back = rows // VL - 2 - block
         tiles_of = [block // 2, (block + 1) // 2, back // 2, (back + 1) // 2]
@@ -237,51 +249,38 @@
         picked = jnp.where((place >= 0) & (place < BL), picked, 0.0)
         return picked + pltpu.roll(picked, VL, 1)
 
-    pairs = leave_ref.shape[1]
-
-    def step(to, carry):
+    def step(j, carry):
+        to = lax.rem(me + j, devices)
         for k in range(pairs):
             slot = 2 * (to * pairs + k)
             leave_ref[to, k] = jnp.where(is_low, window(slot), window(slot + 1))
+
+        @pl.when(to != me)
+        def _():
+            send(0, leave_ref.at[to], land_ref.at[me], to)
+
         return carry
 
-    lax.fori_loop(0, devices, step, 0, unroll=2)
-
-
-def deliver_kernel(
-    size_x, size_y,
-    shift_ref, width_ref, rate_ref, scale_ref, leave_ref, place_hbm, inner_hbm, twist_hbm, outer_hbm, when_hbm,
-    out_ref, land_ref, gain_ref, phase_ref, place_ref, inner_ref, twist_ref, outer_ref, when_ref,
-    send_sem, recv_sem, load_sem,
-):
-    devices, me, send, wait = meet(size_x, size_y, send_sem, recv_sem)
-    pairs, height = leave_ref.shape[1:3]
-
-    def step(j, carry):
-        to = lax.rem(me + j, devices)
-        send(0, leave_ref.at[to], land_ref.at[me], to)
-        return carry
-
-    lax.fori_loop(1, devices, step, 0)
-    loads = fetch(
-        load_sem, (place_hbm, place_ref), (when_hbm, when_ref), (inner_hbm, inner_ref), (twist_hbm, twist_ref),
-        (outer_hbm, outer_ref),
-    )
+    lax.fori_loop(1, devices + 1, step, 0)
     land_ref[me] = leave_ref[me]
     for load in loads:
         load.wait()
 
     is_low = lax.broadcasted_iota(jnp.int32, (1, 128), 1) < VL
     for p in range(pairs):
-        of = lambda ref: jnp.where(is_low, ref[2 * p], ref[2 * p + 1])
-        shift = of(shift_ref)
+        slots = [slot_ref[(me * pairs + p) * 2 + k] for k in range(2)]
+        of = lambda ref: jnp.where(is_low, *[ref[jnp.maximum(slot, 0)] for slot in slots])
+        shift = of(start_ref) & (BL - 1)
+        width = of(width_ref)
+        rate = two_pi / width.astype(jnp.float32)
+        scale = jnp.where(jnp.where(is_low, *slots) >= 0, of(gains_ref) / jnp.sqrt(width.astype(jnp.float32)), 0.0)
         position = (place_ref[...] - shift) & (BL - 1)
-        turn = (position.astype(jnp.float32) + 0.5) * of(rate_ref)
-        gain_ref[p] = jnp.where(position < of(width_ref), 0.5 - 0.5 * jnp.cos(turn), 0.0)
+        turn = (position.astype(jnp.float32) + 0.5) * rate
+        gain_ref[p] = jnp.where(position < width, 0.5 - 0.5 * jnp.cos(turn), 0.0)
         angle = ((when_ref[...] * shift) & (BL - 1)).astype(jnp.float32) * (two_pi / BL)
         phase_cos, phase_sin = jnp.cos(angle), jnp.sin(angle)
-        phase_ref[p, 0] = (phase_cos - phase_sin) * of(scale_ref)
-        phase_ref[p, 1] = (phase_cos + phase_sin) * of(scale_ref)
+        phase_ref[p, 0] = (phase_cos - phase_sin) * scale
+        phase_ref[p, 1] = (phase_cos + phase_sin) * scale
 
     wait(land_ref.at[pl.ds(0, devices - 1)], recv_sem.at[0])
     is_back = lax.broadcasted_iota(jnp.int32, (RAD, 1), 0) % height >= height // 2
@@ -302,7 +301,7 @@
     wait(leave_ref.at[pl.ds(0, devices - 1)], send_sem.at[0])
 
 
-def spectrum(turned, starts, slots, device, base, total):
+def spectrum(turned, bands, base, total):
     size_x, size_y = lax.axis_size("tx"), lax.axis_size("ty")
     devices, _, half = base.shape
     own = turned.shape[1]
@@ -318,12 +317,6 @@
         return np.stack([put(np.cos(part)), put(sign[..., None] * np.sin(part))]).astype(np.float32)
 
     alpha = rows_of(grid(col, RAD * span, total))
-    at = np.concatenate([base[:, 0], base[:, 1, :1]], axis=1).astype(np.int32)
-    at = lax.dynamic_index_in_dim(jnp.asarray(at), device, 0, keepdims=False)
-    col_of = np.broadcast_to(col.reshape(devices, 1, own), (devices, 2, own)).reshape(count, 1)
-    sign_of = np.broadcast_to(np.array([1.0, -1.0])[:, None], (devices, 2, own)).reshape(count, 1)
-    angle = (jnp.asarray(col_of.astype(np.int32)) * at[None]).astype(jnp.float32) * (two_pi / total)
-    beta = jnp.stack([jnp.cos(angle), const(sign_of) * jnp.sin(angle)])
     angle = grid(col, col, cols).reshape(cols, devices, 1, own)
     ahead = np.concatenate([np.cos(angle), np.sin(angle)], axis=2)
     back = np.concatenate([-np.sin(angle), np.cos(angle)], axis=2)
@@ -331,9 +324,6 @@
     swap = np.zeros((2, RAD, RAD))
     swap[0, (-span) % RAD, span] = 1.0
     swap[1, RAD - 1 - span, span] = 1.0
-    residue = ((base * np.array([1, -1])[None, :, None]) % RAD).reshape(devices, 2 * half, 1)
-    residue = jnp.asarray(np.broadcast_to(residue, (devices, 2 * half, 128)).astype(np.int32))
-    residue = lax.dynamic_index_in_dim(residue, device, 0, keepdims=False)
     order = base.reshape(devices // 8, 8, 2, half).transpose(0, 2, 3, 1).reshape(devices // 8, -1)
     angle = grid(order.reshape(-1), span, RAD).reshape(order.shape + (RAD,))
     first = np.concatenate([np.cos(angle), -np.sin(angle)], axis=1)
@@ -347,41 +337,34 @@
     smem = pl.BlockSpec(memory_space=pltpu.SMEM)
     vmem = pl.BlockSpec(memory_space=pltpu.VMEM)
     rows = total // RAD
-    pairs = starts.shape[0] // (2 * devices)
+    pairs = bands[3].shape[0] // (2 * devices)
     shape = (devices, pairs, 2 * half, 128)
     f32, bf16 = jnp.float32, jnp.bfloat16
     hbm = pl.BlockSpec(memory_space=pl.ANY)
     first, twist, second = const_split(first).swapaxes(0, 1), const(twist), const_split(second)
     room = lambda *arrays: [pltpu.VMEM(array.shape, array.dtype) for array in arrays]
     sems = lambda n: [pltpu.SemaphoreType.DMA((n,)), pltpu.SemaphoreType.DMA((n,))]
-    limit = 56 * 1024 * 1024
+    limit = 48 * 1024 * 1024
     remote = lambda k: pltpu.CompilerParams(vmem_limit_bytes=limit, collective_id=k, has_side_effects=True)
-    value = pl.pallas_call(
-        lambda *refs: transform_kernel(size_x, size_y, own, half, *refs),
-        out_shape=jax.ShapeDtypeStruct((count * half * 2, 128), f32),
-        in_specs=[hbm] * 4,
+    alpha, mix = const(alpha), const_split(mix)
+    swap = jnp.asarray(swap.astype(np.float32).astype(bf16))
+    table = pl.pallas_call(
+        lambda *refs: transform_kernel(size_x, size_y, own, half, total, *refs),
+        out_shape=jax.ShapeDtypeStruct((rows // 16, 128), f32),
+        in_specs=[hbm] * 7,
         out_specs=vmem,
         scratch_shapes=[
+            pltpu.VMEM((count * half * 2, 128), f32),
             pltpu.VMEM(turned.shape, f32),
             pltpu.VMEM((RAD, own * RAD), bf16),
             pltpu.VMEM((RAD, own * RAD), bf16),
             pltpu.VMEM((count * half * 2, 128), f32),
-        ] + room(first, twist, second) + sems(2) + [pltpu.SemaphoreType.DMA((4,))],
+            pltpu.VMEM((2, count, 128), f32),
+        ] + room(first, twist, second, alpha, mix, swap) + sems(2) + [pltpu.SemaphoreType.DMA((7,))],
         compiler_params=remote(0),
         name="transform",
-    )(turned, first, twist, second)
-    leaving = pl.pallas_call(
-        lambda *refs: combine_kernel(devices, own, half, total, *refs),
-        out_shape=jax.ShapeDtypeStruct(shape, f32),
-        in_specs=[smem, smem] + [vmem] * 6,
-        out_specs=vmem,
-        scratch_shapes=[pltpu.VMEM((rows // 16, 128), f32)],
-        compiler_params=pltpu.CompilerParams(vmem_limit_bytes=limit),
-        name="combine",
-    )(
-        device.reshape(1).astype(jnp.int32), starts, value, const(alpha), beta,
-        const_split(mix), jnp.asarray(swap.astype(np.float32).astype(jnp.bfloat16)), residue,
-    )
+    )(turned, first, twist, second, alpha, mix, swap)
+    table = table.reshape(rows // 128, 8, 128)
 
     all_residue = (base * np.array([1, -1])[None, :, None]) % RAD
     lane = np.arange(VL)
@@ -398,23 +381,23 @@
     outer = const_split(np.block([[cos_m, sin_m], [-sin_m, cos_m]]))
     when = jnp.asarray(np.tile(np.arange(BL).reshape(RAD, VL), (1, 2)).astype(np.int32))
     return pl.pallas_call(
-        lambda *refs: deliver_kernel(size_x, size_y, *refs),
+        lambda *refs: deliver_kernel(size_x, size_y, half, total, *refs),
         out_shape=jax.ShapeDtypeStruct((pairs, RAD, 128), f32),
         in_specs=[smem] * 4 + [vmem] + [hbm] * 5,
         out_specs=vmem,
         scratch_shapes=[
+            pltpu.VMEM(shape, f32),
             pltpu.VMEM(shape, f32),
             pltpu.VMEM((pairs, RAD, 128), f32),
             pltpu.VMEM((pairs, 2, RAD, 128), f32),
         ] + room(place, inner, spin, outer, when) + sems(1) + [pltpu.SemaphoreType.DMA((5,))],
         compiler_params=remote(1),
         name="deliver",
-    )(*slots, leaving, place, inner, spin, outer, when)
+    )(*bands, table, place, inner, spin, outer, when)
 
 
 def body(signal, band_start, band_width, band_gain, slot_band):
     devices = lax.axis_size("tx") * lax.axis_size("ty")
-    device = lax.axis_index("tx") * lax.axis_size("ty") + lax.axis_index("ty")
     length = signal.shape[0]
     total = length * devices
     own = length // (RAD * RAD)
@@ -425,18 +408,8 @@
 
     turned = signal.reshape(chunk // RAD, RAD, cols).transpose(2, 0, 1)
     turned = turned.reshape(devices, own, chunk // RAD, RAD)
-    slot_index = jnp.maximum(slot_band, 0)
-    starts = lookup(band_start, slot_index)
     slots = slot_band.shape[0] // devices
-    mine = lambda array: lax.dynamic_slice_in_dim(array, device * slots, slots)
-    my_slots = mine(slot_band)
-    my_index = jnp.maximum(my_slots, 0)
-    my_width = lookup(band_width, my_index)
-    wide = my_width.astype(jnp.float32)
-    scale = jnp.where(my_slots >= 0, lookup(band_gain, my_index) / jnp.sqrt(wide), 0.0)
-    result = spectrum(
-        turned, starts, (mine(starts) % BL, my_width, two_pi / wide, scale), device, base, total
-    )
+    result = spectrum(turned, (band_start, band_width, band_gain, slot_band), base, total)
     result = result.reshape(slots // 2, RAD, 2, VL).transpose(0, 2, 1, 3)
     return result.reshape(slots, BL)
 

time: 91.7 us -> 78.3 us (0.85)
  Pallas kernels: 78.8 us -> 71.2 us
  local copies, waits for them, and re-layouts: 9.87 us -> 6.68 us
  other arithmetic: 2.52 us -> 0 us
    pallas_call x2 -> x1, Pallas kernels: 22.7 us -> 14.1 us  [spectrum(): pl.pallas_call(lambda *refs: deliver_kernel(size_x, size_y, half, total,...]
    unnamed x16 -> x30, local copies, waits for them, and re-layouts: 2.17 us -> 3.58 us
    squeeze x1 -> x0, local copies, waits for them, and re-layouts: 1.28 us -> none  [spectrum(): residue = lax.dynamic_index_in_dim(residue, device, 0, keepdims=False)]
    select_n x2 -> x0, other arithmetic: 1.15 us -> none  [the longest x1 0.6 us: body(): jnp.where(my_slots >= 0, lookup(band_gain, my_index) / jnp.sqrt(wide), 0.0)]
    pallas_call x1, Pallas kernels: 56.1 us -> 57.2 us  [spectrum(): pl.pallas_call(lambda *refs: transform_kernel(size_x, size_y, own, half,...]
    pallas_call x1, local copies, waits for them, and re-layouts: 1.08 us -> 0.13 us  [spectrum(): pl.pallas_call(lambda *refs: deliver_kernel(size_x, size_y, half, total,...]
where the time goes in v5:
time: 78.3 us; the launch traced here: 78.1 us
  Pallas kernels  71.2 us (91%)
  local copies, waits for them, and re-layouts  6.68 us (9%)
    pallas_call x1, Pallas kernels, spectrum(): pl.pallas_call(lambda *refs: transform_kernel(size_x, size_y, own, half,...  57.2 us
    pallas_call x1, Pallas kernels, spectrum(): pl.pallas_call(lambda *refs: deliver_kernel(size_x, size_y, half, total,...  14.1 us
    unnamed x30, local copies, waits for them, and re-layouts  3.58 us
    transpose x1, local copies, waits for them, and re-layouts, body(): turned = signal.reshape(chunk // RAD, RAD, cols).transpose(2, 0, 1)  1.84 us

profile of v5, /device:TPU:0, one launch (start us, length us, event | category | flops | bytes accessed | tf_op | source)
XLA Modules:
  0.0 78.1 jit_solution(1018206566650893787)
XLA Ops:
  0.0 1.8 %copy.18 = f32[128,8,256]{2,1,0:T(8,128)S(1)} copy(f32[128,8,256]{0,2,1:T(8,128)} %bitcast.13) | data formatting | bytes 2097152 | tf_op jit(solution)/shard_map/transpose | solution.py:409
  1.9 0.0 copy-done
  1.9 0.0 copy-done.2
  1.9 0.0 copy-done.3
  1.9 0.0 copy-start.4
  1.9 1.0 %copy-done.4 = f32[4,2,64,256]{3,2,1,0:T(8,128)S(1)} copy-done((f32[4,2,64,256]{3,2,1,0:T(8,128)S(1)}, f32[4,2,64,256]{3,2,1,0:T(8,128)}, u32[]{:S(2)}) %copy-start.4) | copy-done | bytes 524312
  2.9 0.9 %copy-done.5 = bf16[2,256,256]{2,1,0:T(8,128)(2,1)S(1)} copy-done((bf16[2,256,256]{2,1,0:T(8,128)(2,1)S(1)}, bf16[2,256,256]{2,1,0:T(8,128)(2,1)}, u32[]{:S(2)}) %copy-start.5) | copy-done | bytes 262168
  3.9 0.9 %copy-done.6 = bf16[2,256,256]{2,1,0:T(8,128)(2,1)S(1)} copy-done((bf16[2,256,256]{2,1,0:T(8,128)(2,1)S(1)}, bf16[2,256,256]{2,1,0:T(8,128)(2,1)}, u32[]{:S(2)}) %copy-start.6) | copy-done | bytes 262168
  4.8 0.0 copy-start.10
  4.9 0.0 copy-start.14
  4.9 57.2 %transform.1 = f32[2048,128]{1,0:T(8,128)S(1)} custom-call(f32[32,4,8,256]{3,2,1,0:T(8,128)S(1)} %bitcast.10, bf16[4,2,128,256]{3,2,1,0:T(8,128)(2,1)S(1)} %copy-done.2, f32[4,2,64,256]{3,2,1,0:T(8,128)S(1)} %copy-done.4, bf16[2,2,512,256]{3,2,1,0:T(8,128)(2,1)S(1)} %copy-done, f32[2,256,256]{2,1,0:T(8,128)S(1)} %copy-done.3, ...), custom_call_target="tpu_custom_call" | custom-call | tf_op jit(solution)/shard_map/transform/pallas_call | solution.py:351
  62.1 0.0 copy-start.11
  62.1 0.0 copy-start.12
  62.1 0.0 copy-start.13
  62.1 0.0 copy-done.1
  62.1 0.0 copy-done.7
  62.1 0.0 copy-done.8
  62.2 0.6 copy-done.11
  62.7 0.0 copy-done.12
  62.7 0.0 copy-done.13
  62.8 14.1 %deliver.1 = f32[2,256,128]{2,1,0:T(8,128)S(1)} custom-call(s32[64]{0:T(128)S(1)} %copy-done.11, s32[64]{0:T(128)S(1)} %copy-done.12, f32[64]{0:T(128)S(1)} %copy-done.13, s32[128]{0:T(128)S(1)} %copy-done.14, f32[256,8,128]{2,1,0:T(8,128)S(1)} %bitcast.11, s32[256,128]{1,0:T(8,128)S(1)} %copy-done.10, bf16[2,128,512]{2,1,0:T(8,128)(2,1)S(1)} %copy-done.8, ...), custom_call_target="tpu_custom_call" | custom-call | tf_op jit(solution)/shard_map/deliver/pallas_call | solution.py:383
  76.8 0.1 copy.19
  77.0 0.2 copy.20
  77.2 0.9 %reshape.19 = f32[4,16384]{1,0:T(4,128)} reshape(f32[2,2,256,64]{3,2,1,0:T(8,128)S(1)} %copy.20) | data formatting | bytes 524288 | tf_op jit(solution)/shard_map/reshape | solution.py:414
  (12 shorter events, 0.0 us)
Async XLA Ops:
  0.0 1.9 %copy-start = (bf16[2,2,512,256]{3,2,1,0:T(8,128)(2,1)S(1)}, bf16[2,2,512,256]{3,2,1,0:T(8,128)(2,1)}, u32[]{:S(2)}) copy-start(bf16[2,2,512,256]{3,2,1,0:T(8,128)(2,1)} %constant.24.clone.refs_3_) | copy-start | bytes 3145732
  0.0 1.9 %copy-start.2 = (bf16[4,2,128,256]{3,2,1,0:T(8,128)(2,1)S(1)}, bf16[4,2,128,256]{3,2,1,0:T(8,128)(2,1)}, u32[]{:S(2)}) copy-start(bf16[4,2,128,256]{3,2,1,0:T(8,128)(2,1)} %constant.33.refs_1_) | copy-start | bytes 1572868
  0.0 1.9 %copy-start.3 = (f32[2,256,256]{2,1,0:T(8,128)S(1)}, f32[2,256,256]{2,1,0:T(8,128)}, u32[]{:S(2)}) copy-start(f32[2,256,256]{2,1,0:T(8,128)} %constant.25.clone.refs_4_) | copy-start | bytes 1572868
  1.9 1.0 %copy-start.4 = (f32[4,2,64,256]{3,2,1,0:T(8,128)S(1)}, f32[4,2,64,256]{3,2,1,0:T(8,128)}, u32[]{:S(2)}) copy-start(f32[4,2,64,256]{3,2,1,0:T(8,128)} %constant.23.clone.refs_2_) | copy-start | bytes 1572868
  2.9 0.9 %copy-start.5 = (bf16[2,256,256]{2,1,0:T(8,128)(2,1)S(1)}, bf16[2,256,256]{2,1,0:T(8,128)(2,1)}, u32[]{:S(2)}) copy-start(bf16[2,256,256]{2,1,0:T(8,128)(2,1)} %constant.27.clone.refs_6_) | copy-start | bytes 786436
  3.9 0.9 %copy-start.6 = (bf16[2,256,256]{2,1,0:T(8,128)(2,1)S(1)}, bf16[2,256,256]{2,1,0:T(8,128)(2,1)}, u32[]{:S(2)}) copy-start(bf16[2,256,256]{2,1,0:T(8,128)(2,1)} %constant.26.clone.refs_5_) | copy-start | bytes 786436
  4.8 57.3 %copy-start.1 = (bf16[2,512,512]{2,1,0:T(8,128)(2,1)S(1)}, bf16[2,512,512]{2,1,0:T(8,128)(2,1)}, u32[]{:S(2)}) copy-start(bf16[2,512,512]{2,1,0:T(8,128)(2,1)} %constant.31.clone.refs_8_) | copy-start | bytes 3145732
  4.8 57.3 %copy-start.7 = (f32[2,256,128]{2,1,0:T(8,128)S(1)}, f32[2,256,128]{2,1,0:T(8,128)}, u32[]{:S(2)}) copy-start(f32[2,256,128]{2,1,0:T(8,128)} %constant.30.clone.refs_7_) | copy-start | bytes 786436
  4.8 57.3 %copy-start.8 = (bf16[2,128,512]{2,1,0:T(8,128)(2,1)S(1)}, bf16[2,128,512]{2,1,0:T(8,128)(2,1)}, u32[]{:S(2)}) copy-start(bf16[2,128,512]{2,1,0:T(8,128)(2,1)} %constant.29.clone.refs_6_) | copy-start | bytes 786436
  4.8 57.3 %copy-start.9 = (s32[256,128]{1,0:T(8,128)S(1)}, s32[256,128]{1,0:T(8,128)}, u32[]{:S(2)}) copy-start(s32[256,128]{1,0:T(8,128)} %constant.32.clone.refs_9_) | copy-start | bytes 393220
  4.8 57.3 %copy-start.10 = (s32[256,128]{1,0:T(8,128)S(1)}, s32[256,128]{1,0:T(8,128)}, u32[]{:S(2)}) copy-start(s32[256,128]{1,0:T(8,128)} %constant.28.clone.refs_5_) | copy-start | bytes 393220
  4.9 57.3 %copy-start.14 = (s32[128]{0:T(128)S(1)}, s32[128]{0:T(128)}, u32[]{:S(2)}) copy-start(s32[128]{0:T(128)} %refs_3_.2) | copy-start | bytes 1540
  62.1 0.7 copy-start.11
  62.1 0.7 copy-start.12
  62.1 0.7 copy-start.13

commit v6 on v5

--- a/solution.py
+++ b/solution.py
@@ -98,7 +98,9 @@
     span = 2 * half * high_rows
 
     def send_columns(j, carry):
-        to = lax.rem(me + j, devices)
+        step = lax.rem(j, 2) * (size_y // 2) + lax.rem(j, size_y) // 2
+        across = lax.rem(me // size_y + j // size_y, size_x)
+        to = across * size_y + lax.rem(me + step, size_y)
         send(0, turned_ref.at[to], column_ref.at[me], to)
         return carry
 
@@ -142,7 +144,7 @@
                             row : row + 8, side * 128 : side * 128 + 128
                         ]
         for j in range(8):
-            to = at * 8 + lax.rem(me + j, 8)
+            to = at * 8 + lax.rem(me + j % 2 * 4 + j // 2, 8)
 
             @pl.when(to != me)
             def _():
@@ -189,10 +191,17 @@
             at = pl.ds(8 * side + h * half + i, cols, stride=16)
             table_ref[at, :] = result[:, side * 128 : (side + 1) * 128]
 
-    for i in range(half):
+    def general(i):
         result = product(mix, split(twist(values(i), i)))
         for h in range(2):
             put(result[h * cols : (h + 1) * cols], h, i)
+
+    for i in range(1, half):
+        general(i)
+
+    @pl.when(me != 0)
+    def _():
+        general(0)
 
     @pl.when(me == 0)
     def _():
@@ -344,8 +353,8 @@
     first, twist, second = const_split(first).swapaxes(0, 1), const(twist), const_split(second)
     room = lambda *arrays: [pltpu.VMEM(array.shape, array.dtype) for array in arrays]
     sems = lambda n: [pltpu.SemaphoreType.DMA((n,)), pltpu.SemaphoreType.DMA((n,))]
-    limit = 48 * 1024 * 1024
-    remote = lambda k: pltpu.CompilerParams(vmem_limit_bytes=limit, collective_id=k, has_side_effects=True)
+    mib = 1024 * 1024
+    remote = lambda k, limit: pltpu.CompilerParams(vmem_limit_bytes=limit, collective_id=k, has_side_effects=True)
     alpha, mix = const(alpha), const_split(mix)
     swap = jnp.asarray(swap.astype(np.float32).astype(bf16))
     table = pl.pallas_call(
@@ -361,7 +370,7 @@
             pltpu.VMEM((count * half * 2, 128), f32),
             pltpu.VMEM((2, count, 128), f32),
         ] + room(first, twist, second, alpha, mix, swap) + sems(2) + [pltpu.SemaphoreType.DMA((7,))],
-        compiler_params=remote(0),
+        compiler_params=remote(0, 60 * mib),
         name="transform",
     )(turned, first, twist, second, alpha, mix, swap)
     table = table.reshape(rows // 128, 8, 128)
@@ -391,7 +400,7 @@
             pltpu.VMEM((pairs, RAD, 128), f32),
             pltpu.VMEM((pairs, 2, RAD, 128), f32),
         ] + room(place, inner, spin, outer, when) + sems(1) + [pltpu.SemaphoreType.DMA((5,))],
-        compiler_params=remote(1),
+        compiler_params=remote(1, 48 * mib),
         name="deliver",
     )(*bands, table, place, inner, spin, outer, when)
 

time: 78.3 us -> 80.2 us (1.024)
  Pallas kernels: 71.2 us -> 74.1 us
  local copies, waits for them, and re-layouts: 6.68 us -> 5.7 us
    pallas_call x1, Pallas kernels: 57.2 us -> 61 us  [spectrum(): pl.pallas_call(lambda *refs: transform_kernel(size_x, size_y, own, half,...]
    unnamed x30 -> x20, local copies, waits for them, and re-layouts: 3.58 us -> 1.86 us
    pallas_call x1, Pallas kernels: 14.1 us -> 13.1 us  [spectrum(): pl.pallas_call(lambda *refs: deliver_kernel(size_x, size_y, half, total,...]
where the time goes in v6:
time: 80.2 us; the launch traced here: 80 us
  Pallas kernels  74.1 us (92%)
  local copies, waits for them, and re-layouts  5.7 us (7%)
    pallas_call x1, Pallas kernels, spectrum(): pl.pallas_call(lambda *refs: transform_kernel(size_x, size_y, own, half,...  61 us
    pallas_call x1, Pallas kernels, spectrum(): pl.pallas_call(lambda *refs: deliver_kernel(size_x, size_y, half, total,...  13.1 us
    transpose x1, local copies, waits for them, and re-layouts, body(): turned = signal.reshape(chunk // RAD, RAD, cols).transpose(2, 0, 1)  2.59 us
    unnamed x20, local copies, waits for them, and re-layouts  1.86 us

profile of v6, /device:TPU:0, one launch (start us, length us, event | category | flops | bytes accessed | tf_op | source)
XLA Modules:
  0.0 80.0 jit_solution(18093720602743420967)
XLA Ops:
  0.0 2.6 %copy.18 = f32[128,8,256]{2,1,0:T(8,128)} copy(f32[128,8,256]{0,2,1:T(8,128)} %bitcast.13) | data formatting | bytes 2097152 | tf_op jit(solution)/shard_map/transpose | solution.py:418
  2.6 0.0 copy-start.1
  2.6 0.0 copy-start.2
  2.6 0.0 copy-start.3
  2.6 0.0 copy-start.5
  2.6 0.0 copy-start.9
  2.6 61.0 %transform.1 = f32[2048,128]{1,0:T(8,128)} custom-call(f32[32,4,8,256]{3,2,1,0:T(8,128)} %bitcast.11, bf16[4,2,128,256]{3,2,1,0:T(8,128)(2,1)} %constant.33.refs_1_, f32[4,2,64,256]{3,2,1,0:T(8,128)} %constant.23.clone.refs_2_, bf16[2,2,512,256]{3,2,1,0:T(8,128)(2,1)} %constant.24.clone.refs_3_, f32[2,256,256]{2,1,0:T(8,128)} %constant.25.clone.refs_4_, ...), custom_call_target="tpu_custom_call" | custom-call | tf_op jit(solution)/shard_map/transform/pallas_call | solution.py:360
  63.7 0.0 copy-start.6
  63.7 0.0 copy-start.7
  63.7 0.0 copy-start.8
  63.7 0.0 copy-done.1
  63.7 0.0 copy-done.2
  63.7 0.0 copy-done.3
  63.7 0.0 copy-done.4
  63.8 0.0 copy-done.5
  63.8 0.0 copy-done.9
  63.8 0.6 copy-done.6
  64.3 0.0 copy-done.7
  64.3 0.0 copy-done.8
  64.4 1.2 %copy-done = f32[2048,128]{1,0:T(8,128)S(1)} copy-done((f32[2048,128]{1,0:T(8,128)S(1)}, f32[2048,128]{1,0:T(8,128)}, u32[]{:S(2)}) %copy-start) | copy-done | bytes 1048600
  65.6 13.1 %deliver.1 = f32[2,256,128]{2,1,0:T(8,128)S(1)} custom-call(s32[64]{0:T(128)S(1)} %copy-done.6, s32[64]{0:T(128)S(1)} %copy-done.7, f32[64]{0:T(128)S(1)} %copy-done.8, s32[128]{0:T(128)S(1)} %copy-done.9, f32[256,8,128]{2,1,0:T(8,128)S(1)} %bitcast.10, s32[256,128]{1,0:T(8,128)S(1)} %copy-done.5, bf16[2,128,512]{2,1,0:T(8,128)(2,1)S(1)} %copy-done.3, ...), custom_call_target="tpu_custom_call" | custom-call | tf_op jit(solution)/shard_map/deliver/pallas_call | solution.py:392
  78.7 0.1 copy.19
  78.8 0.2 copy.20
  79.0 0.9 %reshape.19 = f32[4,16384]{1,0:T(4,128)} reshape(f32[2,2,256,64]{3,2,1,0:T(8,128)S(1)} %copy.20) | data formatting | bytes 524288 | tf_op jit(solution)/shard_map/reshape | solution.py:423
  (2 shorter events, 0.0 us)
Async XLA Ops:
  2.6 61.1 %copy-start.1 = (bf16[2,512,512]{2,1,0:T(8,128)(2,1)S(1)}, bf16[2,512,512]{2,1,0:T(8,128)(2,1)}, u32[]{:S(2)}) copy-start(bf16[2,512,512]{2,1,0:T(8,128)(2,1)} %constant.31.clone.refs_8_) | copy-start | bytes 3145732
  2.6 61.1 %copy-start.2 = (f32[2,256,128]{2,1,0:T(8,128)S(1)}, f32[2,256,128]{2,1,0:T(8,128)}, u32[]{:S(2)}) copy-start(f32[2,256,128]{2,1,0:T(8,128)} %constant.30.clone.refs_7_) | copy-start | bytes 786436
  2.6 61.1 %copy-start.3 = (bf16[2,128,512]{2,1,0:T(8,128)(2,1)S(1)}, bf16[2,128,512]{2,1,0:T(8,128)(2,1)}, u32[]{:S(2)}) copy-start(bf16[2,128,512]{2,1,0:T(8,128)(2,1)} %constant.29.clone.refs_6_) | copy-start | bytes 786436
  2.6 61.1 %copy-start.4 = (s32[256,128]{1,0:T(8,128)S(1)}, s32[256,128]{1,0:T(8,128)}, u32[]{:S(2)}) copy-start(s32[256,128]{1,0:T(8,128)} %constant.32.clone.refs_9_) | copy-start | bytes 393220
  2.6 61.1 %copy-start.5 = (s32[256,128]{1,0:T(8,128)S(1)}, s32[256,128]{1,0:T(8,128)}, u32[]{:S(2)}) copy-start(s32[256,128]{1,0:T(8,128)} %constant.28.clone.refs_5_) | copy-start | bytes 393220
  2.6 61.1 %copy-start.9 = (s32[128]{0:T(128)S(1)}, s32[128]{0:T(128)}, u32[]{:S(2)}) copy-start(s32[128]{0:T(128)} %refs_3_.2) | copy-start | bytes 1540
  63.7 0.7 copy-start.6
  63.7 0.7 copy-start.7
  63.7 0.7 copy-start.8
  64.4 1.2 %copy-start = (f32[2048,128]{1,0:T(8,128)S(1)}, f32[2048,128]{1,0:T(8,128)}, u32[]{:S(2)}) copy-start(f32[2048,128]{1,0:T(8,128)} %transform.1) | copy-start | bytes 3145732

commit v7 on v6

--- a/solution.py
+++ b/solution.py
@@ -98,9 +98,7 @@
     span = 2 * half * high_rows
 
     def send_columns(j, carry):
-        step = lax.rem(j, 2) * (size_y // 2) + lax.rem(j, size_y) // 2
-        across = lax.rem(me // size_y + j // size_y, size_x)
-        to = across * size_y + lax.rem(me + step, size_y)
+        to = lax.rem(me + j, devices)
         send(0, turned_ref.at[to], column_ref.at[me], to)
         return carry
 
@@ -144,7 +142,7 @@
                             row : row + 8, side * 128 : side * 128 + 128
                         ]
         for j in range(8):
-            to = at * 8 + lax.rem(me + j % 2 * 4 + j // 2, 8)
+            to = at * 8 + lax.rem(me + j, 8)
 
             @pl.when(to != me)
             def _():
@@ -221,17 +219,17 @@
 
 def deliver_kernel(
     size_x, size_y, half, total,
-    start_ref, width_ref, gains_ref, slot_ref, table_ref, place_hbm, inner_hbm, twist_hbm, outer_hbm, when_hbm,
+    start_ref, width_ref, gains_ref, slot_ref, table_hbm, place_hbm, inner_hbm, twist_hbm, outer_hbm, when_hbm,
     out_ref, leave_ref, land_ref, gain_ref, phase_ref, place_ref, inner_ref, twist_ref, outer_ref, when_ref,
-    send_sem, recv_sem, load_sem,
+    table_ref, send_sem, recv_sem, load_sem,
 ):
+    loads = fetch(
+        load_sem, (table_hbm, table_ref), (place_hbm, place_ref), (when_hbm, when_ref), (inner_hbm, inner_ref), (twist_hbm, twist_ref),
+        (outer_hbm, outer_ref),
+    )
     devices, me, send, wait = meet(size_x, size_y, send_sem, recv_sem)
     pairs, height = leave_ref.shape[1:3]
     rows = total // RAD
-    loads = fetch(
-        load_sem, (place_hbm, place_ref), (when_hbm, when_ref), (inner_hbm, inner_ref), (twist_hbm, twist_ref),
-        (outer_hbm, outer_ref),
-    )
     shape = (2 * half, 128)
     lane = lax.broadcasted_iota(jnp.int32, shape, 1)
     is_low = lane < VL
@@ -270,10 +268,11 @@
 
         return carry
 
+    loads[0].wait()
     lax.fori_loop(1, devices + 1, step, 0)
     land_ref[me] = leave_ref[me]
-    for load in loads:
-        load.wait()
+    for copy in loads[1:]:
+        copy.wait()
 
     is_low = lax.broadcasted_iota(jnp.int32, (1, 128), 1) < VL
     for p in range(pairs):
@@ -392,14 +391,14 @@
     return pl.pallas_call(
         lambda *refs: deliver_kernel(size_x, size_y, half, total, *refs),
         out_shape=jax.ShapeDtypeStruct((pairs, RAD, 128), f32),
-        in_specs=[smem] * 4 + [vmem] + [hbm] * 5,
+        in_specs=[smem] * 4 + [hbm] * 6,
         out_specs=vmem,
         scratch_shapes=[
             pltpu.VMEM(shape, f32),
             pltpu.VMEM(shape, f32),
             pltpu.VMEM((pairs, RAD, 128), f32),
             pltpu.VMEM((pairs, 2, RAD, 128), f32),
-        ] + room(place, inner, spin, outer, when) + sems(1) + [pltpu.SemaphoreType.DMA((5,))],
+        ] + room(place, inner, spin, outer, when, table) + sems(1) + [pltpu.SemaphoreType.DMA((6,))],
         compiler_params=remote(1, 48 * mib),
         name="deliver",
     )(*bands, table, place, inner, spin, outer, when)

time: 80.2 us -> 78.9 us (0.984)
  Pallas kernels: 74.1 us -> 72.9 us
    pallas_call x1, Pallas kernels: 61 us -> 58.3 us  [spectrum(): pl.pallas_call(lambda *refs: transform_kernel(size_x, size_y, own, half,...]
    pallas_call x1, Pallas kernels: 13.1 us -> 14.6 us  [spectrum(): pl.pallas_call(lambda *refs: deliver_kernel(size_x, size_y, half, total,...]
where the time goes in v7:
time: 78.9 us; the launch traced here: 78.7 us
  Pallas kernels  72.9 us (92%)
  local copies, waits for them, and re-layouts  5.7 us (7%)
    pallas_call x1, Pallas kernels, spectrum(): pl.pallas_call(lambda *refs: transform_kernel(size_x, size_y, own, half,...  58.3 us
    pallas_call x1, Pallas kernels, spectrum(): pl.pallas_call(lambda *refs: deliver_kernel(size_x, size_y, half, total,...  14.6 us
    transpose x1, local copies, waits for them, and re-layouts, body(): turned = signal.reshape(chunk // RAD, RAD, cols).transpose(2, 0, 1)  2.59 us
    unnamed x20, local copies, waits for them, and re-layouts  1.86 us

profile of v7, /device:TPU:0, one launch (start us, length us, event | category | flops | bytes accessed | tf_op | source)
XLA Modules:
  0.0 78.7 jit_solution(3294644770778036724)
XLA Ops:
  0.0 2.6 %copy.18 = f32[128,8,256]{2,1,0:T(8,128)} copy(f32[128,8,256]{0,2,1:T(8,128)} %bitcast.13) | data formatting | bytes 2097152 | tf_op jit(solution)/shard_map/transpose | solution.py:417
  2.6 0.0 copy-start.1
  2.6 0.0 copy-start.2
  2.6 0.0 copy-start.3
  2.6 0.0 copy-start.5
  2.6 0.0 copy-start.9
  2.6 58.3 %transform.1 = f32[2048,128]{1,0:T(8,128)} custom-call(f32[32,4,8,256]{3,2,1,0:T(8,128)} %bitcast.11, bf16[4,2,128,256]{3,2,1,0:T(8,128)(2,1)} %constant.33.refs_1_, f32[4,2,64,256]{3,2,1,0:T(8,128)} %constant.23.clone.refs_2_, bf16[2,2,512,256]{3,2,1,0:T(8,128)(2,1)} %constant.24.clone.refs_3_, f32[2,256,256]{2,1,0:T(8,128)} %constant.25.clone.refs_4_, ...), custom_call_target="tpu_custom_call" | custom-call | tf_op jit(solution)/shard_map/transform/pallas_call | solution.py:359
  60.9 0.0 copy-start.6
  61.0 0.0 copy-start.7
  61.0 0.0 copy-start.8
  61.0 0.0 copy-done.1
  61.0 0.0 copy-done.2
  61.0 0.0 copy-done.3
  61.0 0.0 copy-done.4
  61.0 0.0 copy-done.5
  61.0 0.0 copy-done.9
  61.0 0.6 copy-done.6
  61.6 0.0 copy-done.7
  61.6 0.0 copy-done.8
  61.6 1.2 %copy-done = f32[2048,128]{1,0:T(8,128)S(1)} copy-done((f32[2048,128]{1,0:T(8,128)S(1)}, f32[2048,128]{1,0:T(8,128)}, u32[]{:S(2)}) %copy-start) | copy-done | bytes 1048600
  62.9 14.6 %deliver.1 = f32[2,256,128]{2,1,0:T(8,128)S(1)} custom-call(s32[64]{0:T(128)S(1)} %copy-done.6, s32[64]{0:T(128)S(1)} %copy-done.7, f32[64]{0:T(128)S(1)} %copy-done.8, s32[128]{0:T(128)S(1)} %copy-done.9, f32[256,8,128]{2,1,0:T(8,128)S(1)} %bitcast.10, s32[256,128]{1,0:T(8,128)S(1)} %copy-done.5, bf16[2,128,512]{2,1,0:T(8,128)(2,1)S(1)} %copy-done.3, ...), custom_call_target="tpu_custom_call" | custom-call | tf_op jit(solution)/shard_map/deliver/pallas_call | solution.py:391
  77.5 0.1 copy.19
  77.6 0.2 copy.20
  77.8 0.9 %reshape.19 = f32[4,16384]{1,0:T(4,128)} reshape(f32[2,2,256,64]{3,2,1,0:T(8,128)S(1)} %copy.20) | data formatting | bytes 524288 | tf_op jit(solution)/shard_map/reshape | solution.py:422
  (2 shorter events, 0.0 us)
Async XLA Ops:
  2.6 58.4 %copy-start.1 = (bf16[2,512,512]{2,1,0:T(8,128)(2,1)S(1)}, bf16[2,512,512]{2,1,0:T(8,128)(2,1)}, u32[]{:S(2)}) copy-start(bf16[2,512,512]{2,1,0:T(8,128)(2,1)} %constant.31.clone.refs_8_) | copy-start | bytes 3145732
  2.6 58.4 %copy-start.2 = (f32[2,256,128]{2,1,0:T(8,128)S(1)}, f32[2,256,128]{2,1,0:T(8,128)}, u32[]{:S(2)}) copy-start(f32[2,256,128]{2,1,0:T(8,128)} %constant.30.clone.refs_7_) | copy-start | bytes 786436
  2.6 58.4 %copy-start.3 = (bf16[2,128,512]{2,1,0:T(8,128)(2,1)S(1)}, bf16[2,128,512]{2,1,0:T(8,128)(2,1)}, u32[]{:S(2)}) copy-start(bf16[2,128,512]{2,1,0:T(8,128)(2,1)} %constant.29.clone.refs_6_) | copy-start | bytes 786436
  2.6 58.4 %copy-start.4 = (s32[256,128]{1,0:T(8,128)S(1)}, s32[256,128]{1,0:T(8,128)}, u32[]{:S(2)}) copy-start(s32[256,128]{1,0:T(8,128)} %constant.32.clone.refs_9_) | copy-start | bytes 393220
  2.6 58.4 %copy-start.5 = (s32[256,128]{1,0:T(8,128)S(1)}, s32[256,128]{1,0:T(8,128)}, u32[]{:S(2)}) copy-start(s32[256,128]{1,0:T(8,128)} %constant.28.clone.refs_5_) | copy-start | bytes 393220
  2.6 58.4 %copy-start.9 = (s32[128]{0:T(128)S(1)}, s32[128]{0:T(128)}, u32[]{:S(2)}) copy-start(s32[128]{0:T(128)} %refs_3_.2) | copy-start | bytes 1540
  60.9 0.7 copy-start.6
  61.0 0.7 copy-start.7
  61.0 0.7 copy-start.8
  61.6 1.2 %copy-start = (f32[2048,128]{1,0:T(8,128)S(1)}, f32[2048,128]{1,0:T(8,128)}, u32[]{:S(2)}) copy-start(f32[2048,128]{1,0:T(8,128)} %transform.1) | copy-start | bytes 3145732

commit v8 on v7

--- a/solution.py
+++ b/solution.py
@@ -187,7 +187,7 @@
     def put(result, h, i):
         for side in range(2):
             at = pl.ds(8 * side + h * half + i, cols, stride=16)
-            table_ref[at, :] = result[:, side * 128 : (side + 1) * 128]
+            table_ref.reshape(total // RAD // 16, 128)[at, :] = result[:, side * 128 : (side + 1) * 128]
 
     def general(i):
         result = product(mix, split(twist(values(i), i)))
@@ -215,19 +215,20 @@
 
     wait(turned_ref.at[pl.ds(0, others)], send_sem.at[0])
     wait(pass_ref.at[pl.ds(0, others * span)], send_sem.at[1])
+    return devices, me, send, wait
 
 
 def deliver_kernel(
-    size_x, size_y, half, total,
-    start_ref, width_ref, gains_ref, slot_ref, table_hbm, place_hbm, inner_hbm, twist_hbm, outer_hbm, when_hbm,
+    shared, half, total,
+    start_ref, width_ref, gains_ref, slot_ref, table_ref, place_hbm, inner_hbm, twist_hbm, outer_hbm, when_hbm,
     out_ref, leave_ref, land_ref, gain_ref, phase_ref, place_ref, inner_ref, twist_ref, outer_ref, when_ref,
-    table_ref, send_sem, recv_sem, load_sem,
+    send_sem, recv_sem, load_sem,
 ):
     loads = fetch(
-        load_sem, (table_hbm, table_ref), (place_hbm, place_ref), (when_hbm, when_ref), (inner_hbm, inner_ref), (twist_hbm, twist_ref),
+        load_sem, (place_hbm, place_ref), (when_hbm, when_ref), (inner_hbm, inner_ref), (twist_hbm, twist_ref),
         (outer_hbm, outer_ref),
     )
-    devices, me, send, wait = meet(size_x, size_y, send_sem, recv_sem)
+    devices, me, send, wait = shared
     pairs, height = leave_ref.shape[1:3]
     rows = total // RAD
     shape = (2 * half, 128)
@@ -264,14 +265,13 @@
 
         @pl.when(to != me)
         def _():
-            send(0, leave_ref.at[to], land_ref.at[me], to)
+            send(2, leave_ref.at[to], land_ref.at[me], to)
 
         return carry
 
-    loads[0].wait()
     lax.fori_loop(1, devices + 1, step, 0)
     land_ref[me] = leave_ref[me]
-    for copy in loads[1:]:
+    for copy in loads:
         copy.wait()
 
     is_low = lax.broadcasted_iota(jnp.int32, (1, 128), 1) < VL
@@ -290,7 +290,7 @@
         phase_ref[p, 0] = (phase_cos - phase_sin) * scale
         phase_ref[p, 1] = (phase_cos + phase_sin) * scale
 
-    wait(land_ref.at[pl.ds(0, devices - 1)], recv_sem.at[0])
+    wait(land_ref.at[pl.ds(0, devices - 1)], recv_sem.at[2])
     is_back = lax.broadcasted_iota(jnp.int32, (RAD, 1), 0) % height >= height // 2
     stacked = []
     for p in range(pairs):
@@ -306,7 +306,14 @@
     for p in range(pairs):
         lanes = slice(p * 128, (p + 1) * 128)
         out_ref[p] = result[:RAD, lanes] * phase_ref[p, 0] - result[RAD:, lanes] * phase_ref[p, 1]
-    wait(leave_ref.at[pl.ds(0, devices - 1)], send_sem.at[0])
+    wait(leave_ref.at[pl.ds(0, devices - 1)], send_sem.at[2])
+
+
+def spectrum_kernel(size_x, size_y, own, half, total, *refs):
+    bands, first, last, out_ref = refs[:4], refs[4:11], refs[11:16], refs[16]
+    scratch, rest, sems = refs[17:30], refs[30:39], refs[39:]
+    shared = transform_kernel(size_x, size_y, own, half, total, *first, *scratch, *sems[:3])
+    deliver_kernel(shared, half, total, *bands, scratch[0], *last, out_ref, *rest, *sems[:2], sems[3])
 
 
 def spectrum(turned, bands, base, total):
@@ -351,28 +358,8 @@
     hbm = pl.BlockSpec(memory_space=pl.ANY)
     first, twist, second = const_split(first).swapaxes(0, 1), const(twist), const_split(second)
     room = lambda *arrays: [pltpu.VMEM(array.shape, array.dtype) for array in arrays]
-    sems = lambda n: [pltpu.SemaphoreType.DMA((n,)), pltpu.SemaphoreType.DMA((n,))]
-    mib = 1024 * 1024
-    remote = lambda k, limit: pltpu.CompilerParams(vmem_limit_bytes=limit, collective_id=k, has_side_effects=True)
     alpha, mix = const(alpha), const_split(mix)
     swap = jnp.asarray(swap.astype(np.float32).astype(bf16))
-    table = pl.pallas_call(
-        lambda *refs: transform_kernel(size_x, size_y, own, half, total, *refs),
-        out_shape=jax.ShapeDtypeStruct((rows // 16, 128), f32),
-        in_specs=[hbm] * 7,
-        out_specs=vmem,
-        scratch_shapes=[
-            pltpu.VMEM((count * half * 2, 128), f32),
-            pltpu.VMEM(turned.shape, f32),
-            pltpu.VMEM((RAD, own * RAD), bf16),
-            pltpu.VMEM((RAD, own * RAD), bf16),
-            pltpu.VMEM((count * half * 2, 128), f32),
-            pltpu.VMEM((2, count, 128), f32),
-        ] + room(first, twist, second, alpha, mix, swap) + sems(2) + [pltpu.SemaphoreType.DMA((7,))],
-        compiler_params=remote(0, 60 * mib),
-        name="transform",
-    )(turned, first, twist, second, alpha, mix, swap)
-    table = table.reshape(rows // 128, 8, 128)
 
     all_residue = (base * np.array([1, -1])[None, :, None]) % RAD
     lane = np.arange(VL)
@@ -388,20 +375,33 @@
     cos_m, sin_m = np.cos(angle), np.sin(angle)
     outer = const_split(np.block([[cos_m, sin_m], [-sin_m, cos_m]]))
     when = jnp.asarray(np.tile(np.arange(BL).reshape(RAD, VL), (1, 2)).astype(np.int32))
+    dma = lambda n: pltpu.SemaphoreType.DMA((n,))
+    scratch = [
+        pltpu.VMEM((rows // 128, 8, 128), f32),
+        pltpu.VMEM((count * half * 2, 128), f32),
+        pltpu.VMEM(turned.shape, f32),
+        pltpu.VMEM((RAD, own * RAD), bf16),
+        pltpu.VMEM((RAD, own * RAD), bf16),
+        pltpu.VMEM((count * half * 2, 128), f32),
+        pltpu.VMEM((2, count, 128), f32),
+    ] + room(first, twist, second, alpha, mix, swap)
+    rest = [
+        pltpu.VMEM(shape, f32),
+        pltpu.VMEM(shape, f32),
+        pltpu.VMEM((pairs, RAD, 128), f32),
+        pltpu.VMEM((pairs, 2, RAD, 128), f32),
+    ] + room(place, inner, spin, outer, when)
     return pl.pallas_call(
-        lambda *refs: deliver_kernel(size_x, size_y, half, total, *refs),
+        lambda *refs: spectrum_kernel(size_x, size_y, own, half, total, *refs),
         out_shape=jax.ShapeDtypeStruct((pairs, RAD, 128), f32),
-        in_specs=[smem] * 4 + [hbm] * 6,
+        in_specs=[smem] * 4 + [hbm] * 12,
         out_specs=vmem,
-        scratch_shapes=[
-            pltpu.VMEM(shape, f32),
-            pltpu.VMEM(shape, f32),
-            pltpu.VMEM((pairs, RAD, 128), f32),
-            pltpu.VMEM((pairs, 2, RAD, 128), f32),
-        ] + room(place, inner, spin, outer, when, table) + sems(1) + [pltpu.SemaphoreType.DMA((6,))],
-        compiler_params=remote(1, 48 * mib),
-        name="deliver",
-    )(*bands, table, place, inner, spin, outer, when)
+        scratch_shapes=scratch + rest + [dma(3), dma(3), dma(6 + 1), dma(5)],
+        compiler_params=pltpu.CompilerParams(
+            vmem_limit_bytes=60 * 1024 * 1024, collective_id=0, has_side_effects=True
+        ),
+        name="spectrum",
+    )(*bands, turned, first, twist, second, alpha, mix, swap, place, inner, spin, outer, when)
 
 
 def body(signal, band_start, band_width, band_gain, slot_band):

time: 78.9 us -> 74.4 us (0.943)
  Pallas kernels: 72.9 us -> 69.3 us
  local copies, waits for them, and re-layouts: 5.7 us -> 4.82 us
    pallas_call x2 -> x1, Pallas kernels: 72.9 us -> 69.3 us  [spectrum(): pl.pallas_call(lambda *refs: spectrum_kernel(size_x, size_y, own, half, t...]
    unnamed x20 -> x0, local copies, waits for them, and re-layouts: 1.86 us -> none
    pallas_call x1, local copies, waits for them, and re-layouts: 0.13 us -> 1.08 us  [spectrum(): pl.pallas_call(lambda *refs: spectrum_kernel(size_x, size_y, own, half, t...]
where the time goes in v8:
time: 74.4 us; the launch traced here: 74.2 us
  Pallas kernels  69.3 us (93%)
  local copies, waits for them, and re-layouts  4.82 us (6%)
    pallas_call x1, Pallas kernels, spectrum(): pl.pallas_call(lambda *refs: spectrum_kernel(size_x, size_y, own, half, t...  69.3 us
    transpose x1, local copies, waits for them, and re-layouts, body(): turned = signal.reshape(chunk // RAD, RAD, cols).transpose(2, 0, 1)  2.62 us

profile of v8, /device:TPU:0, one launch (start us, length us, event | category | flops | bytes accessed | tf_op | source)
XLA Modules:
  0.0 74.2 jit_solution(121526407130022557)
XLA Ops:
  0.0 2.6 %copy.18 = f32[128,8,256]{2,1,0:T(8,128)} copy(f32[128,8,256]{0,2,1:T(8,128)} %bitcast.11) | data formatting | bytes 2097152 | tf_op jit(solution)/shard_map/transpose | solution.py:417
  2.6 69.3 %spectrum.1 = f32[2,256,128]{2,1,0:T(8,128)} custom-call(s32[64]{0:T(128)} %refs_0_.1, s32[64]{0:T(128)} %refs_1_.1, f32[64]{0:T(128)} %refs_2_.1, s32[128]{0:T(128)} %refs_3_.1, f32[32,4,8,256]{3,2,1,0:T(8,128)} %bitcast.9, bf16[4,2,128,256]{3,2,1,0:T(8,128)(2,1)} %constant.33.refs_5_, f32[4,2,64,256]{3,2,1,0:T(8,128)} %constant.23.clone.refs_6_, ...), custom_call_target="tpu_custom_call" | custom-call | tf_op jit(solution)/shard_map/spectrum/pallas_call | solution.py:394
  72.0 1.1 %copy.19 = f32[2,256,128]{1,2,0:T(8,128)S(1)} copy(f32[2,256,128]{2,1,0:T(8,128)} %spectrum.1) | data formatting | bytes 524288 | tf_op jit(solution)/shard_map/spectrum/pallas_call | solution.py:394
  73.1 0.2 copy.20
  73.3 0.9 %reshape.15 = f32[4,16384]{1,0:T(4,128)} reshape(f32[2,2,256,64]{3,2,1,0:T(8,128)S(1)} %copy.20) | data formatting | bytes 524288 | tf_op jit(solution)/shard_map/reshape | solution.py:422
